TPU v7x, 32 devices: a whole 2x2x4 slice. The times are simulated.
32 devices in a mesh: ctx: 4 (over z), exp: 8 (over y, x, core).
Axes of the slice: x: 2, y: 2, z: 4, core: 2. Of those that a mesh axis runs over, the one named last changes fastest.
Arguments:
- block_input: bfloat16 [2, 4096, 2048], P(None, ('ctx', 'exp')), may hold values from -16 to 16
- attend_gain: float32 [2048], replicated, may hold values from 0.5 to 1.5
- w_query: bfloat16 [2048, 2048], P(None, 'exp'), may hold values from -0.125 to 0.125
- w_key: bfloat16 [2048, 2048], P(None, 'exp'), may hold values from -0.125 to 0.125
- w_value: bfloat16 [2048, 2048], P(None, 'exp'), may hold values from -0.125 to 0.125
- w_out: bfloat16 [2048, 2048], P('exp'), may hold values from -1.5 to 1.5
- query_gain: float32 [2048], P('exp'), may hold values from 0.5 to 1.5
- key_gain: float32 [2048], P('exp'), may hold values from 0.5 to 1.5
- expert_gain: float32 [2048], replicated, may hold values from 0.5 to 1.5
- router: bfloat16 [2048, 16], replicated, may hold values from -1 to 1
- expert_weights: bfloat16 [2048, 16, 3, 1024], P(None, 'exp'), may hold values from -0.375 to 0.375
- routes: int32 [4096, 2, 8], P(('ctx', 'exp')), may hold values from 0 to 15, all different within a row; in each aligned block of 256 rows (0 to 255, 256 to 511, ..., all dimensions but the last counted through in order) at most 256 rows name the same one
- cotangent: bfloat16 [2, 4096, 2048], P(None, ('ctx', 'exp')), may hold values from -6 to 6
Outputs:
- block_output: bfloat16 [2, 4096, 2048], P(None, ('ctx', 'exp'))
- input_grad: float32 [2, 4096, 2048], P(None, ('ctx', 'exp'))
- attend_grad: float32 [2048], P('exp')
- query_grad: float32 [2048, 2048], P(None, 'exp')
- key_grad: float32 [2048, 2048], P(None, 'exp')
- value_grad: float32 [2048, 2048], P(None, 'exp')
- out_grad: float32 [2048, 2048], P('exp')
- qgain_grad: float32 [2048], P('exp')
- kgain_grad: float32 [2048], P('exp')
- egain_grad: float32 [2048], P('exp')
- router_grad: float32 [2048, 16], P('exp')
- expert_grad: float32 [2048, 16, 3, 1024], P('ctx', 'exp')
Inputs may be any that keep to these rules, and one draw needn't show every extreme that they name: `routes`: each token names 8 different experts; the tokens of one device (an aligned block of 256 rows, row first) name each expert at most 256 times.
All inputs are finite; a program needn't handle non-finite values.
Results may differ from a plain program's by a relative error of at most 0.02.
Values may be sent and summed in bfloat16 or wider, within the bound.
No kernel may reach another device: no remote copies, remote signals or barrier semaphores. Data moves between devices by JAX's collectives and lax.ppermute only.
A program may use at most 384 MiB of HBM per device.

v0:
```python
import math

import jax
import jax.numpy as jnp
from jax import lax
from jax.sharding import PartitionSpec as P

HD = 128
TOP = 8


norm_eps = 1e-05
rope_base = 10000.0
masked_score = -1e30


def rms_factor(values):
    return lax.rsqrt(jnp.mean(values * values, axis=-1, keepdims=True) + norm_eps)


def rotary_tables(positions, head_size):
    half_size = head_size // 2
    inverse_freq = rope_base ** (-(jnp.arange(half_size, dtype=jnp.float32) * 2.0) / head_size)
    angles = positions.astype(jnp.float32)[:, None] * inverse_freq[None, :]
    angles = jnp.concatenate([angles, angles], axis=1)
    return (jnp.cos(angles), jnp.sin(angles))


def rotate(values, cosine, sines):
    half_size = values.shape[-1] // 2
    turned = jnp.concatenate([-values[..., half_size:], values[..., :half_size]], axis=-1)
    return values * cosine[:, None, :] + turned * sines[:, None, :]


def unrotate(values, cosine, sines):
    half_size = values.shape[-1] // 2
    turned = jnp.concatenate([values[..., half_size:], -values[..., :half_size]], axis=-1)
    return values * cosine[:, None, :] + turned * sines[:, None, :]


def body(
    block_input,
    attend_gain,
    w_query,
    w_key,
    w_value,
    w_out,
    query_gain,
    key_gain,
    expert_gain,
    router,
    expert_weights,
    routes,
    cotangent,
):
    exp_count = lax.axis_size("exp")
    ctx_count = lax.axis_size("ctx")
    ctx_place = lax.axis_index("ctx")
    seq_count, shard_len, model_width = block_input.shape
    local_width = w_query.shape[1]
    local_heads = local_width // HD
    experts_all = router.shape[1]
    experts_here = expert_weights.shape[1]
    rows_dev = seq_count * shard_len
    capacity = 2 * rows_dev * TOP // experts_all
    score_scale = 1.0 / math.sqrt(HD)
    whole_input = lax.all_gather(block_input, "exp", axis=1, tiled=True)
    ctx_rows = whole_input.shape[1]
    half_rows = ctx_rows // 2
    input_float = whole_input.astype(jnp.float32)
    unit_rows = input_float * rms_factor(input_float)
    normed = (unit_rows * attend_gain).astype(jnp.bfloat16)
    queries = jnp.dot(normed, w_query, preferred_element_type=jnp.float32)
    keys_proj = jnp.dot(normed, w_key, preferred_element_type=jnp.float32)
    values_low = jnp.dot(normed, w_value, preferred_element_type=jnp.float32).astype(jnp.bfloat16)
    query_sq, key_sq = lax.psum(
        (jnp.sum(queries * queries, axis=-1), jnp.sum(keys_proj * keys_proj, axis=-1)), "exp"
    )
    query_factor = lax.rsqrt(query_sq[..., None] / model_width + norm_eps)
    key_factor = lax.rsqrt(key_sq[..., None] / model_width + norm_eps)
    query_unit = queries * query_factor
    key_unit = keys_proj * key_factor
    head_shape = (seq_count, ctx_rows, local_heads, HD)
    row_ids = jnp.arange(ctx_rows, dtype=jnp.int32)
    far_first = (2 * ctx_count - 1 - ctx_place) * half_rows
    query_pos = jnp.where(
        row_ids < half_rows, ctx_place * half_rows + row_ids, far_first + row_ids - half_rows
    )
    cosine, sines = rotary_tables(query_pos, HD)
    query_rot = rotate((query_unit * query_gain).reshape(head_shape), cosine, sines).astype(
        jnp.bfloat16
    )
    key_rot = rotate((key_unit * key_gain).reshape(head_shape), cosine, sines).astype(jnp.bfloat16)
    value_heads = values_low.reshape(head_shape)
    keys_all, values_all = (
        lax.all_gather(key_rot, "ctx", axis=1, tiled=True),
        lax.all_gather(value_heads, "ctx", axis=1, tiled=True),
    )
    seq_len = keys_all.shape[1]
    block_len = math.gcd(half_rows, 512)
    half_firsts = (ctx_place * half_rows, far_first)

    def row_start(first_pos):
        segment = first_pos // half_rows
        offset = first_pos % half_rows
        return jnp.where(
            segment < ctx_count,
            segment * 2 * half_rows + offset,
            (2 * ctx_count - 1 - segment) * 2 * half_rows + half_rows + offset,
        )

    def block_scores(query_block, query_first, key_block, key_first):
        scores = (
            jnp.einsum(
                "sqhd,skhd->shqk", query_block, key_block, preferred_element_type=jnp.float32
            )
            * score_scale
        )
        query_line = query_first + jnp.arange(query_block.shape[1], dtype=jnp.int32)
        allowed = (key_first + jnp.arange(key_block.shape[1], dtype=jnp.int32))[
            None, :
        ] <= query_line[:, None]
        return jnp.where(allowed, scores, masked_score)

    attended_halves = []
    log_halves = []
    for half_index in range(2):
        query_half = query_rot[:, half_index * half_rows : (half_index + 1) * half_rows]
        query_first = half_firsts[half_index]
        needed_blocks = (query_first + half_rows) // block_len

        def max_step(counter, carried):
            running_max, running_sum = carried
            key_first = counter * block_len
            key_block = lax.dynamic_slice_in_dim(keys_all, row_start(key_first), block_len, 1)
            scores = block_scores(query_half, query_first, key_block, key_first)
            new_max = jnp.maximum(running_max, jnp.max(scores, axis=-1))
            running_sum = running_sum * jnp.exp(running_max - new_max) + jnp.sum(
                jnp.exp(scores - new_max[..., None]), axis=-1
            )
            return (new_max, running_sum)

        stat_shape = (seq_count, local_heads, half_rows)
        running_max, running_sum = lax.fori_loop(
            0,
            needed_blocks,
            max_step,
            (jnp.full(stat_shape, masked_score, jnp.float32), jnp.zeros(stat_shape, jnp.float32)),
        )
        log_total = running_max + jnp.log(running_sum)

        def value_step(counter, carried):
            key_first = counter * block_len
            start_row = row_start(key_first)
            key_block = lax.dynamic_slice_in_dim(keys_all, start_row, block_len, 1)
            scores = block_scores(query_half, query_first, key_block, key_first)
            soft_probs = jnp.exp(scores - log_total[..., None]).astype(jnp.bfloat16)
            value_block = lax.dynamic_slice_in_dim(values_all, start_row, block_len, 1)
            return carried + jnp.einsum(
                "shqk,skhd->sqhd", soft_probs, value_block, preferred_element_type=jnp.float32
            )

        attended_halves.append(
            lax.fori_loop(
                0,
                needed_blocks,
                value_step,
                jnp.zeros((seq_count, half_rows, local_heads, HD), jnp.float32),
            )
        )
        log_halves.append(log_total)
    attended_float = jnp.concatenate(attended_halves, axis=1)
    attended = attended_float.reshape(seq_count, ctx_rows, local_width).astype(jnp.bfloat16)
    full_out = lax.all_gather(w_out, "exp", axis=0, tiled=True)
    own_attended = lax.all_to_all(attended, "exp", split_axis=1, concat_axis=2, tiled=True)
    branch_rows = jnp.dot(own_attended, full_out, preferred_element_type=jnp.float32)
    hidden = block_input.astype(jnp.float32) + branch_rows
    hidden_factor = rms_factor(hidden)
    unit_second = hidden * hidden_factor
    flat_mixed = (unit_second * expert_gain).astype(jnp.bfloat16).reshape(rows_dev, model_width)
    logits = jnp.dot(flat_mixed, router, preferred_element_type=jnp.float32)
    choice_prob = jax.nn.softmax(logits, axis=-1)
    expert_ids = jnp.arange(experts_all, dtype=jnp.int32)
    pos_routes = routes.reshape(rows_dev * TOP)
    pos_hot = (pos_routes[:, None] == expert_ids[None, :]).astype(jnp.int32)
    pos_slots = jnp.sum((jnp.cumsum(pos_hot, axis=0) - pos_hot) * pos_hot, axis=-1)
    flat_routes = jnp.transpose(routes, (1, 0, 2)).reshape(rows_dev, TOP)
    flat_slots = jnp.transpose(pos_slots.reshape(shard_len, seq_count, TOP), (1, 0, 2)).reshape(
        rows_dev, TOP
    )
    one_hot = (flat_routes[:, :, None] == expert_ids[None, None, :]).astype(jnp.float32)
    gate_vals = jnp.sum(one_hot * choice_prob[:, None, :], axis=-1)
    places = (
        flat_routes % experts_here * exp_count + flat_routes // experts_here
    ) * capacity + flat_slots
    flat_places = places.reshape(-1)
    slot_total = experts_here * exp_count * capacity
    send_shape = (experts_here, exp_count, capacity, model_width)
    row_copies = jnp.broadcast_to(flat_mixed[:, None, :], (rows_dev, TOP, model_width)).reshape(
        -1, model_width
    )
    send_rows = jnp.zeros((slot_total, model_width), jnp.bfloat16).at[flat_places].set(row_copies)
    grad_rows = cotangent.reshape(rows_dev, model_width).astype(jnp.float32)
    gated_grads = (
        (gate_vals[:, :, None] * grad_rows[:, None, :])
        .astype(jnp.bfloat16)
        .reshape(-1, model_width)
    )
    send_grads = jnp.zeros((slot_total, model_width), jnp.bfloat16).at[flat_places].set(gated_grads)
    got_rows, got_grads = (
        lax.all_to_all(
            send_rows.reshape(send_shape), "exp", split_axis=1, concat_axis=1, tiled=True
        ),
        lax.all_to_all(
            send_grads.reshape(send_shape), "exp", split_axis=1, concat_axis=1, tiled=True
        ),
    )
    rows_in = got_rows.reshape(experts_here, exp_count * capacity, model_width)
    grads_in = got_grads.reshape(experts_here, exp_count * capacity, model_width)
    w_gate = expert_weights[:, :, 0, :]
    w_up = expert_weights[:, :, 1, :]
    w_down = expert_weights[:, :, 2, :]
    pre_gate = jnp.einsum("erd,def->erf", rows_in, w_gate, preferred_element_type=jnp.float32)
    pre_up = jnp.einsum("erd,def->erf", rows_in, w_up, preferred_element_type=jnp.float32)
    activated = jax.nn.silu(pre_gate)
    middle = (activated * pre_up).astype(jnp.bfloat16)
    expert_out = jnp.einsum(
        "erf,def->erd", middle, w_down, preferred_element_type=jnp.float32
    ).astype(jnp.bfloat16)
    returned = lax.all_to_all(
        expert_out.reshape(send_shape), "exp", split_axis=1, concat_axis=1, tiled=True
    )
    picked = (
        returned.reshape(slot_total, model_width)[flat_places]
        .reshape(rows_dev, TOP, model_width)
        .astype(jnp.float32)
    )
    mixture = jnp.sum(gate_vals[:, :, None] * picked, axis=1)
    block_output = (
        (hidden.reshape(rows_dev, model_width) + mixture)
        .reshape(block_input.shape)
        .astype(jnp.bfloat16)
    )
    grad_middle = jnp.einsum("erd,def->erf", grads_in, w_down, preferred_element_type=jnp.float32)
    sigmoid_vals = jax.nn.sigmoid(pre_gate)
    grad_gate = (
        grad_middle * pre_up * sigmoid_vals * (1.0 + pre_gate * (1.0 - sigmoid_vals))
    ).astype(jnp.bfloat16)
    grad_up = (grad_middle * activated).astype(jnp.bfloat16)
    slot_rows = (
        jnp.einsum("erf,def->erd", grad_gate, w_gate, preferred_element_type=jnp.float32)
        + jnp.einsum("erf,def->erd", grad_up, w_up, preferred_element_type=jnp.float32)
    ).astype(jnp.bfloat16)
    returned_grads = lax.all_to_all(
        slot_rows.reshape(send_shape), "exp", split_axis=1, concat_axis=1, tiled=True
    )
    gate_term = jnp.einsum("erd,erf->def", rows_in, grad_gate, preferred_element_type=jnp.float32)
    up_term = jnp.einsum("erd,erf->def", rows_in, grad_up, preferred_element_type=jnp.float32)
    down_term = jnp.einsum("erd,erf->def", grads_in, middle, preferred_element_type=jnp.float32)
    expert_grad = lax.psum_scatter(
        jnp.stack([gate_term, up_term, down_term], axis=2), "ctx", scatter_dimension=0, tiled=True
    )
    gate_grad = jnp.sum(grad_rows[:, None, :] * picked, axis=-1)
    choice_grad = jnp.sum(one_hot * gate_grad[:, :, None], axis=1)
    logit_grad = (
        choice_prob * (choice_grad - jnp.sum(choice_prob * choice_grad, axis=-1, keepdims=True))
    ).astype(jnp.bfloat16)
    router_part = jnp.einsum(
        "td,te->de", flat_mixed, logit_grad, preferred_element_type=jnp.float32
    )
    slot_back = (
        returned_grads.reshape(slot_total, model_width)[flat_places]
        .reshape(rows_dev, TOP, model_width)
        .astype(jnp.float32)
    )
    mixed_grad = jnp.sum(slot_back, axis=1) + jnp.einsum(
        "te,de->td", logit_grad, router, preferred_element_type=jnp.float32
    )
    unit_flat = unit_second.reshape(rows_dev, model_width)
    egain_part = jnp.sum(mixed_grad * unit_flat, axis=0)
    usecond_grad = mixed_grad * expert_gain
    grad_hidden = (
        hidden_factor.reshape(rows_dev, 1)
        * (usecond_grad - unit_flat * jnp.mean(usecond_grad * unit_flat, axis=-1, keepdims=True))
        + grad_rows
    )
    grad_branch = lax.all_gather(
        grad_hidden.reshape(block_input.shape).astype(jnp.bfloat16), "exp", axis=1, tiled=True
    )
    outw_part = jnp.einsum("sqh,sqd->hd", attended, grad_branch, preferred_element_type=jnp.float32)
    grad_attended = jnp.einsum(
        "sqd,hd->sqh", grad_branch, w_out, preferred_element_type=jnp.float32
    ).astype(jnp.bfloat16)
    grad_heads = grad_attended.reshape(head_shape)
    delta_rows = jnp.transpose(
        jnp.sum(grad_heads.astype(jnp.float32) * attended_float, axis=-1), (0, 2, 1)
    )
    keyval_grads = jnp.zeros((seq_count, seq_len, 2 * local_width), jnp.float32)
    query_halves = []
    for half_index in range(2):
        row_slice = slice(half_index * half_rows, (half_index + 1) * half_rows)
        query_half = query_rot[:, row_slice]
        grad_half = grad_heads[:, row_slice]
        delta_half = delta_rows[:, :, row_slice]
        log_total = log_halves[half_index]
        query_first = half_firsts[half_index]
        needed_blocks = (query_first + half_rows) // block_len

        def one_block(counter, inner):
            query_acc, keyval_acc = inner
            key_first = counter * block_len
            start_row = row_start(key_first)
            key_block = lax.dynamic_slice_in_dim(keys_all, start_row, block_len, 1)
            value_block = lax.dynamic_slice_in_dim(values_all, start_row, block_len, 1)
            scores = block_scores(query_half, query_first, key_block, key_first)
            soft_probs = jnp.exp(scores - log_total[..., None])
            grad_probs = jnp.einsum(
                "sqhd,skhd->shqk", grad_half, value_block, preferred_element_type=jnp.float32
            )
            grad_scores = (soft_probs * (grad_probs - delta_half[..., None])).astype(jnp.bfloat16)
            query_acc = (
                query_acc
                + jnp.einsum(
                    "shqk,skhd->sqhd", grad_scores, key_block, preferred_element_type=jnp.float32
                )
                * score_scale
            )
            kblock_grad = (
                jnp.einsum(
                    "shqk,sqhd->skhd", grad_scores, query_half, preferred_element_type=jnp.float32
                )
                * score_scale
            )
            vblock_grad = jnp.einsum(
                "shqk,sqhd->skhd",
                soft_probs.astype(jnp.bfloat16),
                grad_half,
                preferred_element_type=jnp.float32,
            )
            combined = jnp.concatenate(
                [
                    kblock_grad.reshape(seq_count, block_len, local_width),
                    vblock_grad.reshape(seq_count, block_len, local_width),
                ],
                axis=-1,
            )
            keyval_acc = lax.dynamic_update_slice_in_dim(
                keyval_acc,
                lax.dynamic_slice_in_dim(keyval_acc, start_row, block_len, 1) + combined,
                start_row,
                1,
            )
            return (query_acc, keyval_acc)

        query_acc, keyval_grads = lax.fori_loop(
            0,
            needed_blocks,
            one_block,
            (jnp.zeros((seq_count, half_rows, local_heads, HD), jnp.float32), keyval_grads),
        )
        query_halves.append(query_acc)
    query_back = jnp.concatenate(query_halves, axis=1)
    keyval_local = lax.psum_scatter(keyval_grads, "ctx", scatter_dimension=1, tiled=True)
    key_back = keyval_local[..., :local_width].reshape(head_shape)
    grad_values = keyval_local[..., local_width:].astype(jnp.bfloat16)
    qnorm_grad = unrotate(query_back, cosine, sines).reshape(seq_count, ctx_rows, local_width)
    knorm_grad = unrotate(key_back, cosine, sines).reshape(seq_count, ctx_rows, local_width)
    qgain_part = jnp.sum(qnorm_grad * query_unit, axis=(0, 1))
    kgain_part = jnp.sum(knorm_grad * key_unit, axis=(0, 1))
    qunit_grad = qnorm_grad * query_gain
    kunit_grad = knorm_grad * key_gain
    query_dot, key_dot = lax.psum(
        (jnp.sum(qunit_grad * query_unit, axis=-1), jnp.sum(kunit_grad * key_unit, axis=-1)), "exp"
    )
    grad_queries = (
        query_factor * (qunit_grad - query_unit * query_dot[..., None] / model_width)
    ).astype(jnp.bfloat16)
    grad_keys = (key_factor * (kunit_grad - key_unit * key_dot[..., None] / model_width)).astype(
        jnp.bfloat16
    )
    query_part = jnp.einsum("sqd,sqh->dh", normed, grad_queries, preferred_element_type=jnp.float32)
    key_part = jnp.einsum("sqd,sqh->dh", normed, grad_keys, preferred_element_type=jnp.float32)
    value_part = jnp.einsum("sqd,sqh->dh", normed, grad_values, preferred_element_type=jnp.float32)
    grad_normed = jnp.einsum(
        "sqh,dh->sqd", grad_queries, w_query, preferred_element_type=jnp.float32
    )
    grad_normed = grad_normed + jnp.einsum(
        "sqh,dh->sqd", grad_keys, w_key, preferred_element_type=jnp.float32
    )
    grad_normed = grad_normed + jnp.einsum(
        "sqh,dh->sqd", grad_values, w_value, preferred_element_type=jnp.float32
    )
    attend_part = jnp.sum(grad_normed * unit_rows, axis=(0, 1))
    normed_back, attend_sum, egain_sum, router_sum = (
        lax.psum_scatter(grad_normed, "exp", scatter_dimension=1, tiled=True),
        lax.psum_scatter(attend_part, "exp", scatter_dimension=0, tiled=True),
        lax.psum_scatter(egain_part, "exp", scatter_dimension=0, tiled=True),
        lax.psum_scatter(router_part, "exp", scatter_dimension=0, tiled=True),
    )
    local_float = block_input.astype(jnp.float32)
    local_factor = rms_factor(local_float)
    local_unit = local_float * local_factor
    lunit_grad = normed_back * attend_gain
    input_grad = local_factor * (
        lunit_grad - local_unit * jnp.mean(lunit_grad * local_unit, axis=-1, keepdims=True)
    ) + grad_hidden.reshape(block_input.shape)
    summed = lax.psum(
        (
            query_part,
            key_part,
            value_part,
            outw_part,
            qgain_part,
            kgain_part,
            attend_sum,
            egain_sum,
            router_sum,
        ),
        "ctx",
    )
    return (
        block_output,
        input_grad,
        summed[6],
        summed[0],
        summed[1],
        summed[2],
        summed[3],
        summed[4],
        summed[5],
        summed[7],
        summed[8],
        expert_grad,
    )


def solution(mesh):
    placed = (
        P(None, ("ctx", "exp"), None),
        P(),
        P(None, "exp"),
        P(None, "exp"),
        P(None, "exp"),
        P("exp", None),
        P("exp"),
        P("exp"),
        P(),
        P(),
        P(None, "exp", None, None),
        P(("ctx", "exp"), None, None),
        P(None, ("ctx", "exp"), None),
    )
    return jax.shard_map(
        body,
        mesh=mesh,
        in_specs=placed,
        out_specs=(
            P(None, ("ctx", "exp"), None),
            P(None, ("ctx", "exp"), None),
            P("exp"),
            P(None, "exp"),
            P(None, "exp"),
            P(None, "exp"),
            P("exp", None),
            P("exp"),
            P("exp"),
            P("exp"),
            P("exp", None),
            P("ctx", "exp", None, None),
        ),
        check_vma=False,
    )
```

profile of v0, /device:TPU:0, one launch (start us, length us, event | category | flops | bytes accessed | tf_op | source)
XLA Modules:
  0.0 3198.1 jit_solution(4511849454785376254)
XLA Ops:
  10.8 56.2 %all-gather.6.cloned.1.call-done = bf16[2,1024,2048]{2,1,0:T(8,128)(2,1)} async-done(((bf16[2,128,2048]{2,1,0:T(8,128)(2,1)}), bf16[2,1024,2048]{2,1,0:T(8,128)(2,1)}) %all-gather.6.cloned.1.call-update) | async-done | bytes 8388624 | tf_op jit(solution)/shard_map/all_gather | solution.py:67
  80.3 23.5 all-reduce.4
  122.9 67.4 %all-gather.10.cloned.1.call-done = bf16[2,4096,2,128]{1,3,2,0:T(8,128)(2,1)} async-done(((bf16[2,1024,2,128]{1,3,2,0:T(8,128)(2,1)}), bf16[2,4096,2,128]{1,3,2,0:T(8,128)(2,1)}) %all-gather.10.cloned.1.call-update) | async-done | bytes 4194320 | tf_op jit(solution)/shard_map/all_gather | solution.py:96
  200.1 71.8 %all-gather.8.cloned.1.call-done = bf16[2,4096,2,128]{3,1,2,0:T(8,128)(2,1)} async-done(((bf16[2,1024,2,128]{3,1,2,0:T(8,128)(2,1)}), bf16[2,4096,2,128]{3,1,2,0:T(8,128)(2,1)}) %all-gather.8.cloned.1.call-update) | async-done | bytes 4194320 | tf_op jit(solution)/shard_map/all_gather | solution.py:97
  286.9 26.4 while.88
  313.5 26.6 while.89
  378.3 21.4 scatter_custom_fusion
  399.7 14.2 copy.341
  424.5 22.0 scatter_custom_fusion.1
  446.5 14.1 copy.349
  460.6 143.0 %all-to-all-done.1 = bf16[2,8,256,2048]{3,2,0,1:T(8,128)(2,1)} async-done(((bf16[2,8,256,2048]{3,2,0,1:T(8,128)(2,1)}), bf16[2,8,256,2048]{3,2,0,1:T(8,128)(2,1)}, u32[]{:S(2)}, u32[]{:S(2)}) %all-to-all-start.1) | async-done | bytes 16777248 | tf_op jit(solution)/shard_map/all_to_all | solution.py:211
  609.8 20.1 fusion.150
  638.1 24.7 fusion.96
  662.8 23.0 fusion.97
  685.9 107.9 %all-to-all-done.3 = bf16[2,8,256,2048]{3,2,0,1:T(8,128)(2,1)} async-done(((bf16[2,8,256,2048]{3,2,0,1:T(8,128)(2,1)}), bf16[2,8,256,2048]{3,2,0,1:T(8,128)(2,1)}, u32[]{:S(2)}, u32[]{:S(2)}) %all-to-all-start.3) | async-done | bytes 16777248 | tf_op jit(solution)/shard_map/all_to_all | solution.py:214
  793.8 14.1 copy.350
  808.0 35.8 %multiply_convert_fusion = (bf16[2,2048,1024]{2,1,0:T(8,128)(2,1)}, bf16[2,2048,1024]{2,1,0:T(8,128)(2,1)}, bf16[2,2048,1024]{2,1,0:T(8,128)(2,1)}) fusion(f32[2,2048,1024]{2,1,0:T(8,128)} %fusion.96, f32[2,2048,1024]{2,1,0:T(8,128)} %fusion.97, bf16[2,2048,2048]{2,1,0:T(8,128)(2,1)} %bitcast.402, bf16[2048,2,1,1024]{3,1,2,0:T(2,128)(2,1)} %get-tuple-element.1450), kind=kOutput, calls=%fused_computation.127 | convolution fusion | flops 17242783744 | bytes 83886080 | tf_op jit(solution)/shard_map/erd,def->erf/dot_general | solution.py:244
  843.7 24.8 convolution_convert_fusion
  868.6 14.1 copy.346
  888.7 26.7 fusion.95
  915.4 28.4 add_convert_fusion
  943.8 14.1 copy.351
  957.9 114.8 %all-to-all-done.2 = bf16[2,8,256,2048]{3,2,0,1:T(8,128)(2,1)} async-done(((bf16[2,8,256,2048]{3,2,0,1:T(8,128)(2,1)}), bf16[2,8,256,2048]{3,2,0,1:T(8,128)(2,1)}, u32[]{:S(2)}, u32[]{:S(2)}) %all-to-all-start.2) | async-done | bytes 16777248 | tf_op jit(solution)/shard_map/all_to_all | solution.py:230
  1078.5 14.6 copy.347
  1093.1 24.4 gather_fusion
  1126.9 135.4 %all-to-all-done.4 = bf16[2,8,256,2048]{3,2,0,1:T(8,128)(2,1)} async-done(((bf16[2,8,256,2048]{3,2,0,1:T(8,128)(2,1)}), bf16[2,8,256,2048]{3,2,0,1:T(8,128)(2,1)}, u32[]{:S(2)}, u32[]{:S(2)}) %all-to-all-start.4) | async-done | bytes 16777248 | tf_op jit(solution)/shard_map/all_to_all | solution.py:254
  1262.3 14.1 copy.352
  1276.4 24.4 gather_fusion.1
  1300.9 11.5 convert_reduce_fusion
  1319.1 50.6 %all-gather.14.cloned.1.call-done = bf16[2,1024,2048]{2,1,0:T(8,128)(2,1)} async-done(((bf16[2,128,2048]{2,1,0:T(8,128)(2,1)}), bf16[2,1024,2048]{2,1,0:T(8,128)(2,1)}) %all-gather.14.cloned.1.call-update) | async-done | bytes 8388624 | tf_op jit(solution)/shard_map/all_gather | solution.py:287
  1385.8 24.9 while.90
  1400.1 10.6 dynamic_update_slice.16
  1411.8 180.5 %while.91 = (s32[]{:T(128)}, f32[2,512,2,128]{1,3,2,0:T(8,128)}, f32[2,4096,512]{1,2,0:T(8,128)}, s32[]{:T(128)}, bf16[2,4096,2,128]{3,1,2,0:T(8,128)(2,1)}, /*i...) while((s32[]{:T(128)}, f32[2,512,2,128]{1,3,2,0:T(8,128)}, ...), condition=%wide.region_37.38_spmd, body=%wide.region_36.37_spmd.sunk | while | flops 1354761216 | bytes 42238560 | solution.py:355
  1424.3 10.6 dynamic_update_slice.17
  1492.3 10.5 dynamic_update_slice.17
  1581.8 10.5 dynamic_update_slice.17
  1598.9 280.3 %reduce-scatter.5.cloned.1.call-done = f32[2,1024,512]{1,2,0:T(8,128)} async-done(((f32[2,4096,512]{1,2,0:T(8,128)}), f32[2,1024,512]{1,2,0:T(8,128)}) %reduce-scatter.5.cloned.1.call-update) | async-done | bytes 4194320 | tf_op jit(solution)/shard_map/reduce_scatter | solution.py:363
  1890.6 24.4 all-reduce.3
  1930.0 15.7 fusion.79
  1946.0 25.0 convolution_bitcast_fusion
  1971.0 25.0 convolution_bitcast_fusion.1
  1996.0 25.1 convolution_bitcast_fusion.2
  2021.1 36.0 %pad_maximum_fusion = f32[2048,2,3,1024]{0,3,1,2:T(8,128)} fusion(f32[2048,2,1,1024]{0,3,1,2:T(8,128)} %convolution_bitcast_fusion, f32[2048,2,1,1024]{0,3,1,2:T(8,128)} %convolution_bitcast_fusion.1, f32[2048,2,1,1024]{0,3,1,2:T(8,128)} %convolution_bitcast_fusion.2), kind=kLoop, calls=%fused_computation.110 | loop fusion | flops 25165824 | bytes 100663296 | tf_op jit(solution)/shard_map/stack | solution.py:261
  2089.7 23.9 all-reduce.2
  2113.8 22.0 all-reduce.5
  2141.5 743.6 %reduce-scatter.11.cloned.1.call-done = f32[512,2,3,1024]{0,3,1,2:T(8,128)} async-done(((f32[2048,2,3,1024]{0,3,1,2:T(8,128)}), f32[512,2,3,1024]{0,3,1,2:T(8,128)}) %reduce-scatter.11.cloned.1.call-update) | async-done | bytes 12582928 | tf_op jit(solution)/shard_map/reduce_scatter | solution.py:260
  2885.1 19.5 copy.368
  2904.6 279.1 %all-reduce.9.cloned.1.call-done = (f32[2048,256]{1,0:T(8,128)}, f32[2048,256]{1,0:T(8,128)}, f32[2048,256]{1,0:T(8,128)}, f32[256,2048]{1,0:T(8,128)}) async-done(((f32[2048,256]{1,0:T(8,128)}, f32[2048,256]{1,0:T(8,128)}, f32[2048,256]{1,0:T(8,128)}, f32[256,2048]{1,0:T(8,128)}), (f32[2048,256]{1,0:T(8,128)}, f32[2048,256]{1,0:T(8,128)}, f32[2048,256]{1,0:T(8,128)}, ...) | async-done | bytes 8388624 | tf_op jit(solution)/shard_map/psum | solution.py:407
  (499 shorter events, 468.3 us)
Async XLA Ops:
  7.2 65.1 %copy-start = (bf16[2048,256]{1,0:T(8,128)(2,1)S(1)}, bf16[2048,256]{1,0:T(8,128)(2,1)}, u32[]{:S(2)}) copy-start(bf16[2048,256]{1,0:T(8,128)(2,1)} %param.27) | copy-start | bytes 3145732
  7.2 59.9 %all-gather.6.cloned.1.call-start = ((), (), s32[]{:S(2)}) async-start(), calls=%async_computation.9 | async-start | bytes 9437184 | tf_op jit(solution)/shard_map/all_gather | solution.py:67
  7.9 182.5 %all-gather.10.cloned.1.call-start = ((), (), s32[]{:S(2)}) async-start(), calls=%async_computation.11 | async-start | bytes 5242880 | tf_op jit(solution)/shard_map/all_gather | solution.py:96
  10.8 61.5 %copy-start.58 = (f32[2048]{0:T(1024)S(1)}, f32[2048]{0:T(1024)}, u32[]{:S(2)}) copy-start(f32[2048]{0:T(1024)} %param.26) | copy-start | bytes 24580
  72.8 36.9 %copy-start.56 = (f32[2,1024]{1,0:T(2,128)}, f32[2,1024]{1,0:T(2,128)S(1)}, u32[]{:S(2)}) copy-start(f32[2,1024]{1,0:T(2,128)S(1)} %add_rsqrt_fusion.2) | copy-start | bytes 24580
  77.2 26.7 copy-start.67
  80.3 25.7 copy-start.9
  109.4 162.4 %all-gather.8.cloned.1.call-start = ((), (), s32[]{:S(2)}) async-start(), calls=%async_computation.10 | async-start | bytes 5242880 | tf_op jit(solution)/shard_map/all_gather | solution.py:97
  119.3 250.1 %all-gather.12.cloned.1.call-start = ((), (), s32[]{:S(2)}) async-start(), calls=%async_computation.12 | async-start | bytes 9437184 | tf_op jit(solution)/shard_map/all_gather | solution.py:174
  121.1 75.6 %copy-start.1 = (bf16[2,512,2,128]{1,3,2,0:T(8,128)(2,1)}, bf16[2,512,2,128]{1,3,2,0:T(8,128)(2,1)S(1)}, u32[]{:S(2)}) copy-start(bf16[2,512,2,128]{1,3,2,0:T(8,128)(2,1)S(1)} %get-tuple-element.2126) | copy-start | bytes 1572868
  346.5 22.9 copy-start.15
  346.5 19.8 all-to-all-start
  357.2 67.3 %copy-start.61 = (s32[2048,1]{0,1:T(1,128)}, s32[2048,1]{0,1:T(1,128)S(1)}, u32[]{:S(2)}) copy-start(s32[2048,1]{0,1:T(1,128)S(1)} %compare_select_fusion) | copy-start | bytes 24580
  378.3 21.4 copy-start.12
  413.8 189.8 %all-to-all-start.1 = ((bf16[2,8,256,2048]{3,2,0,1:T(8,128)(2,1)}), bf16[2,8,256,2048]{3,2,0,1:T(8,128)(2,1)}, u32[]{:S(2)}, u32[]{:S(2)}) async-start(bf16[2,8,256,2048]{3,2,0,1:T(8,128)(2,1)} %copy.341), calls=%async_computation.1 | async-start | bytes 33554432 | tf_op jit(solution)/shard_map/all_to_all | solution.py:211
  421.2 25.3 copy-start.6
  424.4 22.2 copy-start.39
  603.7 190.1 %all-to-all-start.3 = ((bf16[2,8,256,2048]{3,2,0,1:T(8,128)(2,1)}), bf16[2,8,256,2048]{3,2,0,1:T(8,128)(2,1)}, u32[]{:S(2)}, u32[]{:S(2)}) async-start(bf16[2,8,256,2048]{3,2,0,1:T(8,128)(2,1)} %copy.349), calls=%async_computation.3 | async-start | bytes 33554432 | tf_op jit(solution)/shard_map/all_to_all | solution.py:214
  638.1 24.7 copy-start.14
  882.7 189.9 %all-to-all-start.2 = ((bf16[2,8,256,2048]{3,2,0,1:T(8,128)(2,1)}), bf16[2,8,256,2048]{3,2,0,1:T(8,128)(2,1)}, u32[]{:S(2)}, u32[]{:S(2)}) async-start(bf16[2,8,256,2048]{3,2,0,1:T(8,128)(2,1)} %copy.346), calls=%async_computation.2 | async-start | bytes 33554432 | tf_op jit(solution)/shard_map/all_to_all | solution.py:230
  957.9 120.6 %copy-start.62 = (s32[2048,1]{0,1:T(1,128)S(1)}, s32[2048,1]{0,1:T(1,128)}, u32[]{:S(2)}) copy-start(s32[2048,1]{0,1:T(1,128)} %copy-done.61) | copy-start | bytes 24580
  1072.6 189.7 %all-to-all-start.4 = ((bf16[2,8,256,2048]{3,2,0,1:T(8,128)(2,1)}), bf16[2,8,256,2048]{3,2,0,1:T(8,128)(2,1)}, u32[]{:S(2)}, u32[]{:S(2)}) async-start(bf16[2,8,256,2048]{3,2,0,1:T(8,128)(2,1)} %copy.351), calls=%async_computation.4 | async-start | bytes 33554432 | tf_op jit(solution)/shard_map/all_to_all | solution.py:254
  1078.4 291.3 %all-gather.14.cloned.1.call-start = ((), (), s32[]{:S(2)}) async-start(), calls=%async_computation.13 | async-start | bytes 9437184 | tf_op jit(solution)/shard_map/all_gather | solution.py:287
  1093.0 24.4 copy-start.7
  1093.1 24.4 copy-start.40
  1300.8 11.6 copy-start.53
  1300.9 11.6 copy-start.45
  1300.9 11.6 copy-start.64
  1300.9 11.6 copy-start.66
  1300.9 11.7 copy-start.8
  1300.9 11.7 copy-start.47
  1300.9 11.7 copy-start.55
  1316.4 53.4 %copy-start.28 = (f32[2,1024,2,128]{1,3,2,0:T(8,128)S(1)}, f32[2,1024,2,128]{1,3,2,0:T(8,128)}, u32[]{:S(2)}) copy-start(f32[2,1024,2,128]{1,3,2,0:T(8,128)} %constant_dynamic-update-slice_fusion) | copy-start | bytes 6291460
  1318.8 560.3 %reduce-scatter.5.cloned.1.call-start = ((), (), s32[]{:S(2)}) async-start(), calls=%async_computation.14 | async-start | bytes 20971520 | tf_op jit(solution)/shard_map/reduce_scatter | solution.py:363
  1385.8 26.0 copy-start.74
  1592.3 521.5 %reduce-scatter.9.cloned.1.call-start = ((), (), s32[]{:S(2)}) async-start(), calls=%async_computation.16 | async-start | bytes 147456 | tf_op jit(solution)/shard_map/reduce_scatter | solution.py:398
  1594.5 541.3 %reduce-scatter.7.cloned.1.call-start = ((), (), s32[]{:S(2)}) async-start(), calls=%async_computation.15 | async-start | bytes 18874368 | tf_op jit(solution)/shard_map/reduce_scatter | solution.py:395
  1597.4 284.7 %copy-start.51 = (f32[2,1024]{1,0:T(2,128)S(1)}, f32[2,1024]{1,0:T(2,128)}, u32[]{:S(2)}) copy-start(f32[2,1024]{1,0:T(2,128)} %copy-done.50) | copy-start | bytes 24580
  1921.8 8.2 copy-start.18
  1921.8 8.2 copy-start.57
  1945.7 939.4 %reduce-scatter.11.cloned.1.call-start = ((), (), s32[]{:S(2)}) async-start(), calls=%async_computation.17 | async-start | bytes 62914560 | tf_op jit(solution)/shard_map/reduce_scatter | solution.py:260
  2057.1 8.5 copy-start.33
  2057.2 8.5 copy-start.59
  2057.2 1126.5 %all-reduce.9.cloned.1.call-start = ((), (), s32[]{:S(2)}) async-start(), calls=%async_computation.18 | async-start | bytes 16777216 | tf_op jit(solution)/shard_map/psum | solution.py:407
  2058.3 15.4 slice-start
  2083.9 29.9 copy-start.76
  2083.9 29.9 copy-start.77
  2086.1 52.2 %copy-start.5 = (f32[256,2048]{1,0:T(8,128)S(1)}, f32[256,2048]{1,0:T(8,128)}, u32[]{:S(2)}) copy-start(f32[256,2048]{1,0:T(8,128)} %copy-done.4) | copy-start | bytes 6291460
  (63 other events, 166.8 us)
Sparse Core Ops, SparseCore 0:
  9.9 57.0 all-gather.5
  109.6 80.7 all-gather.9
  192.5 79.2 all-gather.7
  273.6 52.9 all-gather.11
  1318.9 50.7 all-gather.13
  1592.5 286.6 reduce-scatter.4
  1882.4 34.0 reduce-scatter.8
  1945.8 115.1 reduce-scatter.6
  2063.4 821.6 reduce-scatter.10
  2888.7 294.9 all-reduce.8
where the time goes:
time: 3210 us; the launch traced here: 3200 us
  waiting for transfers between devices  2060 us (64%)
  matrix products  458 us (14%)
  local copies, waits for them, and re-layouts  377 us (12%)
  other arithmetic  161 us (5%)
  blocking collectives  93.8 us (3%)
    reduce_scatter x1, waiting for transfers between devices, body(): lax.psum_scatter(jnp.stack([gate_term, up_term, down_term], axis=2), 'ctx...  744 us
    reduce_scatter x1, waiting for transfers between devices, body(): lax.psum_scatter(keyval_grads, 'ctx', scatter_dimension=1, tiled=True)  280 us
    psum x1, waiting for transfers between devices, body(): lax.psum((query_part, key_part, value_part, outw_part, qgain_part, kgain_...  279 us
    all_to_all x1, waiting for transfers between devices, body(): lax.all_to_all(send_rows.reshape(send_shape), 'exp', split_axis=1, concat...  143 us
    all_to_all x1, waiting for transfers between devices, body(): lax.all_to_all(slot_rows.reshape(send_shape), 'exp', split_axis=1, concat...  135 us
    all_to_all x1, waiting for transfers between devices, body(): lax.all_to_all(expert_out.reshape(send_shape), 'exp', split_axis=1, conca...  115 us
    all_to_all x1, waiting for transfers between devices, body(): lax.all_to_all(send_grads.reshape(send_shape), 'exp', split_axis=1, conca...  108 us
    dynamic_update_slice x9, local copies, waits for them, and re-layouts, one_block(): lax.dynamic_update_slice_in_dim(keyval_acc, lax.dynamic_slice_in_dim(keyv...  93.5 us
  transfers between devices with their start and end apart: 15, of which 12 were waited for; matrix products, arithmetic and copies ran while one was open for 17% of the time, Pallas kernels for 0%

commit v1 on v0

v1 whole, which is shorter than its diff:
```python
import functools
import math

import jax
import jax.numpy as jnp
from jax import lax
from jax.experimental import pallas as pl
from jax.experimental.pallas import tpu as pltpu
from jax.sharding import PartitionSpec as P

HD = 128
TOP = 8


norm_eps = 1e-05
rope_base = 10000.0
masked_score = -1e30
LOG2E = 1.4426950408889634
F32 = jnp.float32
BF16 = jnp.bfloat16


def rms_factor(values):
    return lax.rsqrt(jnp.mean(values * values, axis=-1, keepdims=True) + norm_eps)


def rotary_tables(positions, head_size):
    half_size = head_size // 2
    inverse_freq = rope_base ** (-(jnp.arange(half_size, dtype=F32) * 2.0) / head_size)
    angles = positions.astype(F32)[:, None] * inverse_freq[None, :]
    angles = jnp.concatenate([angles, angles], axis=1)
    return (jnp.cos(angles), jnp.sin(angles))


def turn(values):
    half_size = values.shape[-1] // 2
    return jnp.concatenate([-values[..., half_size:], values[..., :half_size]], axis=-1)


def turn_back(values):
    half_size = values.shape[-1] // 2
    return jnp.concatenate([values[..., half_size:], -values[..., :half_size]], axis=-1)


def dot32(a, b):
    return jnp.dot(a, b, preferred_element_type=F32)


def flip(values, axis, mask):
    return lax.ppermute(values, axis, [(i, i ^ mask) for i in range(lax.axis_size(axis))])


def pick(values, index, axis=0):
    return lax.dynamic_index_in_dim(values, index, axis, keepdims=False)


def butterfly_sum(values, axis):
    mask = 1
    while mask < lax.axis_size(axis):
        values = jax.tree.map(lambda v: v + flip(v, axis, mask), values)
        mask *= 2
    return values


def reduce_rows(partial, own=None):
    count = partial.shape[0]
    me = lax.axis_index("exp")
    core, chip = me % 2, me // 2
    pairs = partial.reshape((count // 2, 2) + partial.shape[1:])
    got = flip(pick(pairs, 1 - core, 1), "exp", 1)
    mine = pick(pairs, core, 1)
    both = (mine.astype(F32) + got.astype(F32)).astype(BF16)
    parts = [flip(pick(both, chip ^ m), "exp", 2 * m) for m in range(1, count // 2)]
    total = pick(mine, chip).astype(F32) + pick(got, chip).astype(F32)
    for part in parts:
        total = total + part.astype(F32)
    return total


def block_place(block, ctx_count, place):
    late = block >= ctx_count
    owner = jnp.where(late, 2 * ctx_count - 1 - block, block)
    return owner ^ place, jnp.where(late, 1, 0)


def causal_mask(rows):
    key_line = lax.broadcasted_iota(jnp.int32, (rows, rows), 0)
    query_line = lax.broadcasted_iota(jnp.int32, (rows, rows), 1)
    return key_line <= query_line


def attend_kernel(place_ref, qk_ref, v_ref, o_ref, ot_ref, lse_ref, qt_ref, vt_ref):
    ctx_count, rows = v_ref.shape[0], v_ref.shape[1] // 2
    blocks = 2 * ctx_count
    place = place_ref[0]
    scale = LOG2E / math.sqrt(HD)

    def lay(block, unused):
        slab, half = block_place(block, ctx_count, place)
        at = pl.ds(pl.multiple_of(half * rows, rows), rows)
        to = pl.ds(pl.multiple_of(block * rows, rows), rows)
        qt_ref[:, to] = qk_ref[slab, 0, at, :].T
        vt_ref[:, to] = v_ref[slab, at, :].T
        return unused

    lax.fori_loop(0, blocks, lay, 0)

    def query_block(block, unused):
        cols = pl.ds(pl.multiple_of(block * rows, rows), rows)
        query = qt_ref[:, cols]

        def part(key_block, carried, masked):
            high, total, acc = carried
            slab, half = block_place(key_block, ctx_count, place)
            at = pl.ds(pl.multiple_of(half * rows, rows), rows)
            scores = dot32(qk_ref[slab, 1, at, :], query) * scale
            if masked:
                scores = jnp.where(causal_mask(rows), scores, masked_score)
            new_high = jnp.maximum(high, jnp.max(scores, axis=0, keepdims=True))
            probs = jnp.exp2(scores - new_high)
            fade = jnp.exp2(high - new_high)
            total = total * fade + jnp.sum(probs, axis=0, keepdims=True)
            keys = pl.ds(pl.multiple_of(key_block * rows, rows), rows)
            acc = acc * fade + dot32(vt_ref[:, keys], probs.astype(BF16))
            return new_high, total, acc

        start = (
            jnp.full((1, rows), masked_score, F32),
            jnp.zeros((1, rows), F32),
            jnp.zeros((HD, rows), F32),
        )
        state = part(block, start, True)
        high, total, acc = lax.fori_loop(0, block, lambda j, c: part(j, c, False), state)
        out = acc / total
        ot_ref[:, cols] = out
        slab, half = block_place(block, ctx_count, place)
        o_ref[slab, pl.ds(pl.multiple_of(half * rows, rows), rows), :] = out.T.astype(BF16)
        lse_ref[block] = high + jnp.log2(total)
        return unused

    lax.fori_loop(0, blocks, query_block, 0)


def attend_back_kernel(
    place_ref, qk_ref, v_ref, do_ref, ot_ref, lse_ref, d_ref, qt_ref, kt_ref, dot_ref, dk_ref, dv_ref
):
    ctx_count, rows = v_ref.shape[0], v_ref.shape[1] // 2
    blocks = 2 * ctx_count
    place = place_ref[0]
    score_scale = 1.0 / math.sqrt(HD)
    scale = LOG2E * score_scale

    def lay(block, unused):
        slab, half = block_place(block, ctx_count, place)
        at = pl.ds(pl.multiple_of(half * rows, rows), rows)
        to = pl.ds(pl.multiple_of(block * rows, rows), rows)
        qt_ref[:, to] = qk_ref[slab, 0, at, :].T
        kt_ref[:, to] = qk_ref[slab, 1, at, :].T
        dot_ref[:, to] = do_ref[slab, at, :].T
        dk_ref[to, :] = jnp.zeros((rows, HD), F32)
        dv_ref[to, :] = jnp.zeros((rows, HD), F32)
        return unused

    lax.fori_loop(0, blocks, lay, 0)

    def query_block(block, unused):
        cols = pl.ds(pl.multiple_of(block * rows, rows), rows)
        slab_q, half_q = block_place(block, ctx_count, place)
        at_q = pl.ds(pl.multiple_of(half_q * rows, rows), rows)
        query_t, grad_t = qt_ref[:, cols], dot_ref[:, cols]
        delta = jnp.sum(grad_t.astype(F32) * ot_ref[:, cols], axis=0, keepdims=True)
        lse = lse_ref[block]

        def part(key_block, dq, masked):
            slab, half = block_place(key_block, ctx_count, place)
            at = pl.ds(pl.multiple_of(half * rows, rows), rows)
            keys = pl.ds(pl.multiple_of(key_block * rows, rows), rows)
            probs = jnp.exp2(dot32(qk_ref[slab, 1, at, :], query_t) * scale - lse)
            if masked:
                probs = jnp.where(causal_mask(rows), probs, 0.0)
            grad_probs = dot32(v_ref[slab, at, :], grad_t)
            grad_scores = (probs * (grad_probs - delta)).astype(BF16)
            dv_ref[keys, :] += dot32(probs.astype(BF16), do_ref[slab_q, at_q, :])
            dk_ref[keys, :] += dot32(grad_scores, qk_ref[slab_q, 0, at_q, :])
            return dq + dot32(kt_ref[:, keys], grad_scores)

        dq = part(block, jnp.zeros((HD, rows), F32), True)
        dq = lax.fori_loop(0, block, lambda j, c: part(j, c, False), dq)
        d_ref[slab_q, 0, at_q, :] = (dq * score_scale).T.astype(BF16)
        return unused

    lax.fori_loop(0, blocks, query_block, 0)

    def give(block, unused):
        slab, half = block_place(block, ctx_count, place)
        at = pl.ds(pl.multiple_of(half * rows, rows), rows)
        to = pl.ds(pl.multiple_of(block * rows, rows), rows)
        d_ref[slab, 1, at, :] = (dk_ref[to, :] * score_scale).astype(BF16)
        d_ref[slab, 2, at, :] = dv_ref[to, :].astype(BF16)
        return unused

    lax.fori_loop(0, blocks, give, 0)


VMEM = pl.BlockSpec(memory_space=pltpu.VMEM)
SMEM = pl.BlockSpec(memory_space=pltpu.SMEM)


def attend_call(place, qk, v):
    ctx_count, ctx_rows = v.shape[0], v.shape[1]
    length, rows = ctx_count * ctx_rows, ctx_rows // 2
    pairs = length * length // 2
    return pl.pallas_call(
        attend_kernel,
        out_shape=(
            jax.ShapeDtypeStruct(v.shape, BF16),
            jax.ShapeDtypeStruct((HD, length), F32),
            jax.ShapeDtypeStruct((2 * ctx_count, 1, rows), F32),
        ),
        in_specs=[SMEM, VMEM, VMEM],
        out_specs=(VMEM, VMEM, VMEM),
        scratch_shapes=[pltpu.VMEM((HD, length), BF16), pltpu.VMEM((HD, length), BF16)],
        compiler_params=pltpu.CompilerParams(vmem_limit_bytes=50 * 2**20),
        cost_estimate=pl.CostEstimate(
            flops=8 * pairs * HD, bytes_accessed=12 * length * HD, transcendentals=pairs
        ),
        name="attend",
    )(place, qk, v)


def attend_back_call(place, qk, v, grads, out_t, lse):
    ctx_count, ctx_rows = v.shape[0], v.shape[1]
    length = ctx_count * ctx_rows
    pairs = length * length // 2
    return pl.pallas_call(
        attend_back_kernel,
        out_shape=jax.ShapeDtypeStruct((ctx_count, 3, ctx_rows, HD), BF16),
        in_specs=[SMEM] + [VMEM] * 5,
        out_specs=VMEM,
        scratch_shapes=[pltpu.VMEM((HD, length), BF16)] * 3 + [pltpu.VMEM((length, HD), F32)] * 2,
        compiler_params=pltpu.CompilerParams(vmem_limit_bytes=50 * 2**20),
        cost_estimate=pl.CostEstimate(
            flops=20 * pairs * HD, bytes_accessed=18 * length * HD, transcendentals=pairs
        ),
        name="attend_back",
    )(place, qk, v, grads, out_t, lse)


def spread_pairs(values):
    count = values.shape[0]
    place = lax.axis_index("ctx")
    parts = [pick(values, place ^ m) for m in range(count)]
    return jnp.stack([parts[0]] + [flip(parts[m], "ctx", m) for m in range(1, count)])


def return_pairs(values):
    count = values.shape[0]
    place = lax.axis_index("ctx")
    parts = jnp.stack([values[0]] + [flip(values[m], "ctx", m) for m in range(1, count)])
    return jnp.stack([pick(parts, place ^ p) for p in range(count)])


def paired_forward(queries, keys_proj, values_low, query_gain, key_gain, cosine, sines, model_width):
    exp_count, seq_count, shard_len, local_width = queries.shape
    local_heads = local_width // HD
    ctx_rows = exp_count * shard_len

    def by_pair(values):
        values = values.reshape(exp_count, seq_count, shard_len, local_heads, HD)
        return jnp.transpose(values, (1, 3, 0, 2, 4)).reshape(-1, ctx_rows, HD)

    v_all = spread_pairs(by_pair(values_low))
    squares = jnp.stack(
        [jnp.sum(queries * queries, axis=-1), jnp.sum(keys_proj * keys_proj, axis=-1)]
    )
    squares = butterfly_sum(squares, "exp")
    factors = lax.rsqrt(squares[..., None] / model_width + norm_eps)
    query_unit = queries * factors[0]
    key_unit = keys_proj * factors[1]

    def rotated(values):
        pairs = by_pair(values)
        return (pairs * cosine + turn(pairs) * sines).astype(BF16)

    rotated_qk = jnp.stack([rotated(query_unit * query_gain), rotated(key_unit * key_gain)], axis=1)
    qk_all = spread_pairs(rotated_qk)
    place = lax.axis_index("ctx").astype(jnp.int32).reshape(1)
    out, out_t, lse = attend_call(place, qk_all, v_all)
    attended = return_pairs(out)
    return attended, (place, qk_all, v_all, out_t, lse, query_unit, key_unit, factors)


def paired_backward(kept, grads, query_gain, key_gain, cosine, sines, model_width):
    place, qk_all, v_all, out_t, lse, query_unit, key_unit, factors = kept
    exp_count, seq_count, shard_len, local_width = query_unit.shape
    local_heads = local_width // HD
    back = attend_back_call(place, qk_all, v_all, spread_pairs(grads), out_t, lse)
    back = return_pairs(back)

    def by_row(values):
        values = values.reshape(seq_count, local_heads, exp_count, shard_len, HD)
        return jnp.transpose(values, (2, 0, 3, 1, 4)).reshape(query_unit.shape)

    def unrotated(values):
        values = values.astype(F32)
        return by_row(values * cosine + turn_back(values) * sines)

    qnorm_grad, knorm_grad = unrotated(back[:, 0]), unrotated(back[:, 1])
    grad_values = by_row(back[:, 2])
    qgain_part = jnp.sum(qnorm_grad * query_unit, axis=(0, 1, 2))
    kgain_part = jnp.sum(knorm_grad * key_unit, axis=(0, 1, 2))
    qunit_grad = qnorm_grad * query_gain
    kunit_grad = knorm_grad * key_gain
    dots = jnp.stack(
        [jnp.sum(qunit_grad * query_unit, axis=-1), jnp.sum(kunit_grad * key_unit, axis=-1)]
    )
    dots = butterfly_sum(dots, "exp")[..., None] / model_width
    grad_queries = (factors[0] * (qunit_grad - query_unit * dots[0])).astype(BF16)
    grad_keys = (factors[1] * (kunit_grad - key_unit * dots[1])).astype(BF16)
    return jnp.concatenate([grad_queries, grad_keys, grad_values], axis=-1), qgain_part, kgain_part


def gathered_forward(queries, keys_proj, values_low, query_gain, key_gain, cosine, sines, model_width):
    exp_count, seq_count, shard_len, local_width = queries.shape
    ctx_count, ctx_place = lax.axis_size("ctx"), lax.axis_index("ctx")
    local_heads = local_width // HD
    ctx_rows = exp_count * shard_len
    half_rows = ctx_rows // 2
    squares = jnp.stack(
        [jnp.sum(queries * queries, axis=-1), jnp.sum(keys_proj * keys_proj, axis=-1)]
    )
    squares = lax.psum(squares, "exp")
    factors = lax.rsqrt(squares[..., None] / model_width + norm_eps)
    query_unit = queries * factors[0]
    key_unit = keys_proj * factors[1]

    def heads(values):
        values = values.reshape(exp_count, seq_count, shard_len, local_heads, HD)
        return jnp.transpose(values, (1, 0, 2, 3, 4)).reshape(seq_count, ctx_rows, local_heads, HD)

    def rotated(values):
        values = heads(values)
        return (values * cosine[:, None, :] + turn(values) * sines[:, None, :]).astype(BF16)

    query_rot = rotated(query_unit * query_gain)
    keys_all = lax.all_gather(rotated(key_unit * key_gain), "ctx", axis=1, tiled=True)
    values_all = lax.all_gather(heads(values_low), "ctx", axis=1, tiled=True)
    tools = block_tools(half_rows, ctx_count, ctx_place)
    block_len, half_firsts, row_start, block_scores = tools
    attended_halves = []
    log_halves = []
    for half_index in range(2):
        query_half = query_rot[:, half_index * half_rows : (half_index + 1) * half_rows]
        query_first = half_firsts[half_index]
        needed_blocks = (query_first + half_rows) // block_len

        def step(counter, carried):
            running_max, running_sum, acc = carried
            key_first = counter * block_len
            start_row = row_start(key_first)
            key_block = lax.dynamic_slice_in_dim(keys_all, start_row, block_len, 1)
            value_block = lax.dynamic_slice_in_dim(values_all, start_row, block_len, 1)
            scores = block_scores(query_half, query_first, key_block, key_first)
            new_max = jnp.maximum(running_max, jnp.max(scores, axis=-1))
            fade = jnp.exp(running_max - new_max)
            probs = jnp.exp(scores - new_max[..., None])
            running_sum = running_sum * fade + jnp.sum(probs, axis=-1)
            acc = acc * jnp.transpose(fade, (0, 2, 1))[..., None] + jnp.einsum(
                "shqk,skhd->sqhd", probs.astype(BF16), value_block, preferred_element_type=F32
            )
            return (new_max, running_sum, acc)

        stat_shape = (seq_count, local_heads, half_rows)
        running_max, running_sum, acc = lax.fori_loop(
            0,
            needed_blocks,
            step,
            (
                jnp.full(stat_shape, masked_score, F32),
                jnp.zeros(stat_shape, F32),
                jnp.zeros((seq_count, half_rows, local_heads, HD), F32),
            ),
        )
        attended_halves.append(acc / jnp.transpose(running_sum, (0, 2, 1))[..., None])
        log_halves.append(running_max + jnp.log(running_sum))
    attended_float = jnp.concatenate(attended_halves, axis=1)
    attended = jnp.transpose(attended_float.astype(BF16), (0, 2, 1, 3)).reshape(-1, ctx_rows, HD)
    kept = (
        query_rot, keys_all, values_all, attended_float, log_halves, query_unit, key_unit, factors
    )
    return attended, kept


def block_tools(half_rows, ctx_count, ctx_place):
    block_len = math.gcd(half_rows, 512)
    far_first = (2 * ctx_count - 1 - ctx_place) * half_rows
    half_firsts = (ctx_place * half_rows, far_first)

    def row_start(first_pos):
        segment = first_pos // half_rows
        offset = first_pos % half_rows
        return jnp.where(
            segment < ctx_count,
            segment * 2 * half_rows + offset,
            (2 * ctx_count - 1 - segment) * 2 * half_rows + half_rows + offset,
        )

    def block_scores(query_block, query_first, key_block, key_first):
        scores = jnp.einsum("sqhd,skhd->shqk", query_block, key_block, preferred_element_type=F32)
        scores = scores * (1.0 / math.sqrt(HD))
        query_line = query_first + jnp.arange(query_block.shape[1], dtype=jnp.int32)
        key_line = key_first + jnp.arange(key_block.shape[1], dtype=jnp.int32)
        return jnp.where(key_line[None, :] <= query_line[:, None], scores, masked_score)

    return block_len, half_firsts, row_start, block_scores


def gathered_backward(kept, grads, query_gain, key_gain, cosine, sines, model_width):
    query_rot, keys_all, values_all, attended_float, log_halves, query_unit, key_unit, factors = kept
    exp_count, seq_count, shard_len, local_width = query_unit.shape
    ctx_count, ctx_place = lax.axis_size("ctx"), lax.axis_index("ctx")
    local_heads = local_width // HD
    ctx_rows = exp_count * shard_len
    half_rows = ctx_rows // 2
    seq_len = keys_all.shape[1]
    score_scale = 1.0 / math.sqrt(HD)
    block_len, half_firsts, row_start, block_scores = block_tools(half_rows, ctx_count, ctx_place)
    grad_heads = jnp.transpose(
        grads.reshape(seq_count, local_heads, ctx_rows, HD), (0, 2, 1, 3)
    )
    delta_rows = jnp.transpose(jnp.sum(grad_heads.astype(F32) * attended_float, axis=-1), (0, 2, 1))
    keyval_grads = jnp.zeros((seq_count, seq_len, 2 * local_width), F32)
    query_halves = []
    for half_index in range(2):
        row_slice = slice(half_index * half_rows, (half_index + 1) * half_rows)
        query_half = query_rot[:, row_slice]
        grad_half = grad_heads[:, row_slice]
        delta_half = delta_rows[:, :, row_slice]
        log_total = log_halves[half_index]
        query_first = half_firsts[half_index]
        needed_blocks = (query_first + half_rows) // block_len

        def one_block(counter, inner):
            query_acc, keyval_acc = inner
            key_first = counter * block_len
            start_row = row_start(key_first)
            key_block = lax.dynamic_slice_in_dim(keys_all, start_row, block_len, 1)
            value_block = lax.dynamic_slice_in_dim(values_all, start_row, block_len, 1)
            scores = block_scores(query_half, query_first, key_block, key_first)
            soft_probs = jnp.exp(scores - log_total[..., None])
            grad_probs = jnp.einsum(
                "sqhd,skhd->shqk", grad_half, value_block, preferred_element_type=F32
            )
            grad_scores = (soft_probs * (grad_probs - delta_half[..., None])).astype(BF16)
            query_acc = query_acc + score_scale * jnp.einsum(
                "shqk,skhd->sqhd", grad_scores, key_block, preferred_element_type=F32
            )
            kblock_grad = score_scale * jnp.einsum(
                "shqk,sqhd->skhd", grad_scores, query_half, preferred_element_type=F32
            )
            vblock_grad = jnp.einsum(
                "shqk,sqhd->skhd", soft_probs.astype(BF16), grad_half, preferred_element_type=F32
            )
            flat = (seq_count, block_len, local_width)
            combined = jnp.concatenate([kblock_grad.reshape(flat), vblock_grad.reshape(flat)], -1)
            keyval_acc = lax.dynamic_update_slice_in_dim(
                keyval_acc,
                lax.dynamic_slice_in_dim(keyval_acc, start_row, block_len, 1) + combined,
                start_row,
                1,
            )
            return (query_acc, keyval_acc)

        query_acc, keyval_grads = lax.fori_loop(
            0,
            needed_blocks,
            one_block,
            (jnp.zeros((seq_count, half_rows, local_heads, HD), F32), keyval_grads),
        )
        query_halves.append(query_acc)
    query_back = jnp.concatenate(query_halves, axis=1)
    keyval_local = lax.psum_scatter(keyval_grads, "ctx", scatter_dimension=1, tiled=True)

    def by_row(values):
        values = values.reshape(seq_count, exp_count, shard_len, local_width)
        return jnp.transpose(values, (1, 0, 2, 3))

    def unrotated(values):
        values = values.reshape(seq_count, ctx_rows, local_heads, HD)
        return by_row(values * cosine[:, None, :] + turn_back(values) * sines[:, None, :])

    qnorm_grad = unrotated(query_back)
    knorm_grad = unrotated(keyval_local[..., :local_width])
    grad_values = by_row(keyval_local[..., local_width:].astype(BF16))
    qgain_part = jnp.sum(qnorm_grad * query_unit, axis=(0, 1, 2))
    kgain_part = jnp.sum(knorm_grad * key_unit, axis=(0, 1, 2))
    qunit_grad = qnorm_grad * query_gain
    kunit_grad = knorm_grad * key_gain
    dots = jnp.stack(
        [jnp.sum(qunit_grad * query_unit, axis=-1), jnp.sum(kunit_grad * key_unit, axis=-1)]
    )
    dots = lax.psum(dots, "exp")[..., None] / model_width
    grad_queries = (factors[0] * (qunit_grad - query_unit * dots[0])).astype(BF16)
    grad_keys = (factors[1] * (kunit_grad - key_unit * dots[1])).astype(BF16)
    return jnp.concatenate([grad_queries, grad_keys, grad_values], axis=-1), qgain_part, kgain_part


def body(
    block_input,
    attend_gain,
    w_query,
    w_key,
    w_value,
    w_out,
    query_gain,
    key_gain,
    expert_gain,
    router,
    expert_weights,
    routes,
    cotangent,
):
    exp_count, ctx_count = lax.axis_size("exp"), lax.axis_size("ctx")
    ctx_place, exp_place = lax.axis_index("ctx"), lax.axis_index("exp")
    seq_count, shard_len, model_width = block_input.shape
    local_width = w_query.shape[1]
    local_heads = local_width // HD
    experts_all = router.shape[1]
    experts_here = expert_weights.shape[1]
    hidden_units = expert_weights.shape[3]
    rows_dev = seq_count * shard_len
    rows_all = exp_count * rows_dev
    ctx_rows = exp_count * shard_len
    half_rows = ctx_rows // 2
    pair_count = seq_count * local_heads
    paired = pair_count == ctx_count and half_rows % 128 == 0

    def gather(values):
        return lax.all_gather(values, "exp", axis=0, tiled=False)

    local_float = block_input.astype(F32).reshape(rows_dev, model_width)
    local_factor = rms_factor(local_float)
    local_unit = local_float * local_factor
    normed = gather((local_unit * attend_gain).astype(BF16)).reshape(rows_all, model_width)
    all_routes = gather(jnp.transpose(routes, (1, 0, 2)).reshape(rows_dev, TOP))
    all_routes = all_routes.reshape(rows_all, TOP)
    grad_low = gather(cotangent.reshape(rows_dev, model_width)).reshape(rows_all, model_width)
    full_out = gather(w_out).reshape(exp_count * local_width, model_width)
    w_qkv = jnp.concatenate([w_query, w_key, w_value], axis=1)
    full_qkv = gather(w_qkv.T).reshape(exp_count * 3 * local_width, model_width)
    w_gate, w_up, w_down = (
        jnp.concatenate([expert_weights[:, e, k, :] for e in range(experts_here)], axis=1)
        for k in range(3)
    )

    projected = dot32(normed, w_qkv).reshape(exp_count, seq_count, shard_len, 3 * local_width)
    row_ids = jnp.arange(ctx_rows, dtype=jnp.int32)
    far_first = (2 * ctx_count - 1 - ctx_place) * half_rows
    query_pos = jnp.where(
        row_ids < half_rows, ctx_place * half_rows + row_ids, far_first + row_ids - half_rows
    )
    cosine, sines = rotary_tables(query_pos, HD)
    forward, backward = (
        (paired_forward, paired_backward) if paired else (gathered_forward, gathered_backward)
    )
    attended, kept = forward(
        projected[..., :local_width],
        projected[..., local_width : 2 * local_width],
        projected[..., 2 * local_width :].astype(BF16),
        query_gain,
        key_gain,
        cosine,
        sines,
        model_width,
    )

    def exchange(values):
        return lax.all_to_all(values, "exp", split_axis=0, concat_axis=0, tiled=True)

    sent = jnp.transpose(attended.reshape(pair_count, exp_count, shard_len, HD), (1, 0, 2, 3))
    own = exchange(sent).reshape(exp_count, seq_count, local_heads, shard_len, HD)
    own_attended = jnp.transpose(own, (1, 3, 0, 2, 4)).reshape(rows_dev, exp_count * local_width)
    hidden = local_float + dot32(own_attended, full_out)
    hidden_factor = rms_factor(hidden)
    unit_second = hidden * hidden_factor
    own_mixed = (unit_second * expert_gain).astype(BF16)

    expert_ids = jnp.arange(experts_all, dtype=jnp.int32)

    def chosen(table):
        return jnp.any(table[:, :, None] == expert_ids[None, None, :], axis=1)

    own_prob = jax.nn.softmax(dot32(own_mixed, router), axis=-1)
    own_routes = jnp.transpose(routes, (1, 0, 2)).reshape(rows_dev, TOP)
    own_chosen = chosen(own_routes)

    mixed = gather(own_mixed).reshape(rows_all, model_width)
    all_prob = jax.nn.softmax(dot32(mixed, router), axis=-1)
    all_gates = jnp.where(chosen(all_routes), all_prob, 0.0)
    gates = lax.dynamic_slice_in_dim(all_gates, exp_place * experts_here, experts_here, 1)
    gates = gates[:, :, None]

    wide = (rows_all, experts_here, hidden_units)
    grad_down = dot32(grad_low, w_down).reshape(wide)
    pre_gate = dot32(mixed, w_gate).reshape(wide)
    pre_up = dot32(mixed, w_up).reshape(wide)
    sigmoid_vals = jax.nn.sigmoid(pre_gate)
    activated = pre_gate * sigmoid_vals
    middle = activated * pre_up
    gate_grads = jnp.sum(middle * grad_down, axis=-1)
    grad_middle = gates * grad_down
    flat = (rows_all, experts_here * hidden_units)
    gated_middle = (gates * middle).astype(BF16).reshape(flat)
    grad_gate = grad_middle * pre_up * sigmoid_vals * (1.0 + pre_gate * (1.0 - sigmoid_vals))
    grad_gate = grad_gate.astype(BF16).reshape(flat)
    grad_up = (grad_middle * activated).astype(BF16).reshape(flat)

    def weight_term(rows, grads):
        term = jnp.einsum("rd,rf->df", rows, grads, preferred_element_type=F32).astype(BF16)
        return lax.psum_scatter(term, "ctx", scatter_dimension=0, tiled=True)

    down_term = weight_term(grad_low, gated_middle)
    gate_term = weight_term(mixed, grad_gate)
    up_term = weight_term(mixed, grad_up)
    expert_grad = jnp.stack(
        [
            t.astype(F32).reshape(t.shape[0], experts_here, hidden_units)
            for t in (gate_term, up_term, down_term)
        ],
        axis=2,
    )

    slot_rows = jnp.einsum("rf,df->rd", grad_gate, w_gate, preferred_element_type=F32)
    slot_rows = slot_rows + jnp.einsum("rf,df->rd", grad_up, w_up, preferred_element_type=F32)
    slot_sum = reduce_rows(slot_rows.astype(BF16).reshape(exp_count, rows_dev, model_width))
    expert_out = jnp.einsum("rf,df->rd", gated_middle, w_down, preferred_element_type=F32)
    mixture = reduce_rows(expert_out.astype(BF16).reshape(exp_count, rows_dev, model_width))
    block_output = (hidden + mixture).astype(BF16).reshape(block_input.shape)

    choice_grad = exchange(gate_grads.reshape(exp_count, rows_dev, experts_here))
    choice_grad = jnp.transpose(choice_grad, (1, 0, 2)).reshape(rows_dev, experts_all)
    choice_grad = jnp.where(own_chosen, choice_grad, 0.0)
    logit_grad = (
        own_prob * (choice_grad - jnp.sum(own_prob * choice_grad, axis=-1, keepdims=True))
    ).astype(BF16)
    router_part = jnp.einsum("td,te->de", own_mixed, logit_grad, preferred_element_type=F32)
    mixed_grad = slot_sum + jnp.einsum(
        "te,de->td", logit_grad, router, preferred_element_type=F32
    )
    egain_part = jnp.sum(mixed_grad * unit_second, axis=0)
    usecond_grad = mixed_grad * expert_gain
    grad_rows = cotangent.astype(F32).reshape(rows_dev, model_width)
    grad_hidden = (
        hidden_factor
        * (usecond_grad - unit_second * jnp.mean(usecond_grad * unit_second, axis=-1, keepdims=True))
        + grad_rows
    )
    own_branch = grad_hidden.astype(BF16)

    grad_attended = jnp.einsum(
        "rd,hd->rh", own_branch, full_out, preferred_element_type=F32
    ).astype(BF16)
    sent = grad_attended.reshape(seq_count, shard_len, exp_count, local_heads, HD)
    sent = jnp.transpose(sent, (2, 0, 3, 1, 4)).reshape(exp_count, pair_count, shard_len, HD)
    grads = jnp.transpose(exchange(sent), (1, 0, 2, 3)).reshape(pair_count, ctx_rows, HD)
    grad_qkv, qgain_part, kgain_part = backward(
        kept, grads, query_gain, key_gain, cosine, sines, model_width
    )
    own_qkv = exchange(grad_qkv.reshape(exp_count, rows_dev, 3 * local_width))
    own_qkv = jnp.transpose(own_qkv, (1, 0, 2)).reshape(rows_dev, exp_count * 3 * local_width)
    grad_normed = dot32(own_qkv, full_qkv)
    attend_part = jnp.sum(grad_normed * local_unit, axis=0)
    lunit_grad = grad_normed * attend_gain
    input_grad = grad_hidden + local_factor * (
        lunit_grad - local_unit * jnp.mean(lunit_grad * local_unit, axis=-1, keepdims=True)
    )

    branch_rows = gather(own_branch).reshape(exp_count, seq_count, shard_len, model_width)
    attended_rows = attended.reshape(seq_count, local_heads, exp_count, shard_len, HD)
    outw_part = jnp.einsum(
        "shetc,estd->hcd", attended_rows, branch_rows, preferred_element_type=F32
    ).reshape(local_width, model_width)
    out_grad = lax.psum(outw_part.astype(BF16), "ctx").astype(F32)
    qkv_part = jnp.einsum(
        "rd,rh->dh", normed, grad_qkv.reshape(rows_all, -1), preferred_element_type=F32
    )
    qkv_grad = lax.psum(qkv_part.astype(BF16), "ctx").astype(F32)
    attend_sum, egain_sum, router_sum = (
        lax.psum_scatter(part, "exp", scatter_dimension=0, tiled=True)
        for part in (attend_part, egain_part, router_part)
    )
    attend_sum, egain_sum, router_sum, qgain_grad, kgain_grad = lax.psum(
        (attend_sum, egain_sum, router_sum, qgain_part, kgain_part), "ctx"
    )
    return (
        block_output,
        input_grad.reshape(block_input.shape),
        attend_sum,
        qkv_grad[:, :local_width],
        qkv_grad[:, local_width : 2 * local_width],
        qkv_grad[:, 2 * local_width :],
        out_grad,
        qgain_grad,
        kgain_grad,
        egain_sum,
        router_sum,
        expert_grad,
    )


def solution(mesh):
    placed = (
        P(None, ("ctx", "exp"), None),
        P(),
        P(None, "exp"),
        P(None, "exp"),
        P(None, "exp"),
        P("exp", None),
        P("exp"),
        P("exp"),
        P(),
        P(),
        P(None, "exp", None, None),
        P(("ctx", "exp"), None, None),
        P(None, ("ctx", "exp"), None),
    )
    return jax.shard_map(
        body,
        mesh=mesh,
        in_specs=placed,
        out_specs=(
            P(None, ("ctx", "exp"), None),
            P(None, ("ctx", "exp"), None),
            P("exp"),
            P(None, "exp"),
            P(None, "exp"),
            P(None, "exp"),
            P("exp", None),
            P("exp"),
            P("exp"),
            P("exp"),
            P("exp", None),
            P("ctx", "exp", None, None),
        ),
        check_vma=False,
    )
```

time: 3210 us -> 1430 us (0.45)
  waiting for transfers between devices: 2060 us -> 545 us
  matrix products: 458 us -> 288 us
  local copies, waits for them, and re-layouts: 377 us -> 231 us
  other arithmetic: 161 us -> 92 us
  Pallas kernels: 0 us -> 62.9 us
    reduce_scatter x4, waiting for transfers between devices: 1020 us -> 107 us  [the longest x3 107 us: weight_term(): return lax.psum_scatter(term, 'ctx', scatter_dimension=0, tiled=True)]
    all_to_all x5 -> x2, waiting for transfers between devices: 510 us -> 41.6 us  [exchange(): lax.all_to_all(values, 'exp', split_axis=0, concat_axis=0, tiled=True)]
    ppermute x0 -> x29, waiting for transfers between devices: none -> 198 us  [flip(): lax.ppermute(values, axis, [(i, i ^ mask) for i in range(lax.axis_size(ax...]
    all_gather x5 -> x6, waiting for transfers between devices: 246 us -> 51.8 us  [gather(): return lax.all_gather(values, 'exp', axis=0, tiled=False)]
    dot_general x87 -> x19, matrix products: 458 us -> 288 us  [the longest x8 123 us: dot32(): return jnp.dot(a, b, preferred_element_type=F32)]
    psum x1, waiting for transfers between devices: 279 us -> 144 us  [body(): qkv_grad = lax.psum(qkv_part.astype(BF16), 'ctx').astype(F32)]
    dynamic_update_slice x9 -> x0, local copies, waits for them, and re-layouts: 93.5 us -> none  [one_block(): lax.dynamic_update_slice_in_dim(keyval_acc, lax.dynamic_slice_in_dim(keyv...]
    pallas_call x0 -> x2, Pallas kernels: none -> 62.9 us  [the longest x1 34.9 us: attend_back_call(): pl.pallas_call(attend_back_kernel, out_shape=jax.ShapeDtypeStruct((ctx_co...]
  transfers between devices with their start and end apart: 15 -> 42, of which waited for: 12 -> 16; matrix products, arithmetic and copies ran while one was open for 17% -> 41% of each run, Pallas kernels for 0% -> 4%
where the time goes in v1:
time: 1430 us; the launch traced here: 1420 us
  waiting for transfers between devices  545 us (38%)
  matrix products  288 us (20%)
  local copies, waits for them, and re-layouts  231 us (16%)
  blocking collectives  123 us (9%)
  other arithmetic  92 us (6%)
  Pallas kernels  62.9 us (4%)
  starting transfers between devices  61.3 us (4%)
  between operations  16 us (1%)
    ppermute x29, waiting for transfers between devices, flip(): lax.ppermute(values, axis, [(i, i ^ mask) for i in range(lax.axis_size(ax...  198 us
    psum x1, waiting for transfers between devices, body(): qkv_grad = lax.psum(qkv_part.astype(BF16), 'ctx').astype(F32)  144 us
    dot_general x8, matrix products, dot32(): return jnp.dot(a, b, preferred_element_type=F32)  123 us
    reduce_scatter x3, waiting for transfers between devices, weight_term(): return lax.psum_scatter(term, 'ctx', scatter_dimension=0, tiled=True)  107 us
    dot_general x3, matrix products, weight_term(): jnp.einsum('rd,rf->df', rows, grads, preferred_element_type=F32)  71.6 us
    ppermute x29, starting transfers between devices, flip(): lax.ppermute(values, axis, [(i, i ^ mask) for i in range(lax.axis_size(ax...  53 us
    all_gather x6, waiting for transfers between devices, gather(): return lax.all_gather(values, 'exp', axis=0, tiled=False)  51.8 us
    psum x1, blocking collectives, body(): lax.psum((attend_sum, egain_sum, router_sum, qgain_part, kgain_part), 'ctx')  49.9 us
  transfers between devices with their start and end apart: 42, of which 16 were waited for; matrix products, arithmetic and copies ran while one was open for 41% of the time, Pallas kernels for 4%

profile of v1, /device:TPU:0, one launch (start us, length us, event | category | flops | bytes accessed | tf_op | source)
XLA Modules:
  0.0 1419.6 jit_solution(5340956716364804534)
XLA Ops:
  18.3 51.8 %all-gather.11.cloned.1.call-done = bf16[8,256,2048]{2,1,0:T(8,128)(2,1)} async-done(((bf16[1,256,2048]{2,1,0:T(8,128)(2,1)}), bf16[8,256,2048]{2,1,0:T(8,128)(2,1)}) %all-gather.11.cloned.1.call-update) | async-done | bytes 8388624 | tf_op jit(solution)/shard_map/all_gather | solution.py:539
  70.0 9.0 fusion.16
  118.4 60.0 %collective-permute-done.7 = bf16[1024,128]{1,0:T(8,128)(2,1)S(1)} collective-permute-done((bf16[1024,128]{1,0:T(8,128)(2,1)S(1)}, bf16[1024,128]{1,0:T(8,128)(2,1)S(1)}, u32[]{:S(2)}, u32[]{:S(2)}) %collective-permute-start.7) | collective-permute-done | bytes 262176 | tf_op jit(solution)/shard_map/ppermute | solution.py:50
  181.1 28.0 %attend.1 = (bf16[4,1024,128]{2,1,0:T(8,128)(2,1)S(1)}, f32[128,4096]{1,0:T(8,128)}, f32[8,1,512]{2,1,0:T(1,128)S(1)}) custom-call(s32[1]{0:T(128)} %bitcast.1.place_ref, bf16[4,2,1024,128]{3,2,1,0:T(8,128)(2,1)} %pad_maximum_fusion.10.qk_ref, bf16[4,1024,128]{2,1,0:T(8,128)(2,1)S(1)} %pad_maximum_fusion.11.v_ref), custom_call_target="tpu_custom_call" | custom-call | flops 8589934592 | bytes 6291456 | tf_op jit(solution)/shard_map/attend/pallas_call | solution.py:213
  215.3 5.7 collective-permute-done.9
  221.0 12.8 collective-permute-done.10
  235.2 17.9 %all_to_all.20 = bf16[8,4,128,128]{3,2,1,0:T(8,128)(2,1)S(1)} all-to-all(bf16[8,4,128,128]{3,2,1,0:T(8,128)(2,1)S(1)} %bitcast.343), channel_id=1, replica_groups=mesh['ctx'=4,'exp'=8] {'exp'}, dimensions={0} | all-to-all | bytes 2097152 | tf_op jit(solution)/shard_map/all_to_all | solution.py:578
  255.8 6.2 multiply_reduce_fusion.9
  265.1 49.7 %fusion.75 = (bf16[2048,1,1,1024]{3,1,2,0:T(2,128)(2,1)}, bf16[2048,1,1,1024]{3,1,2,0:T(2,128)(2,1)}, bf16[2048,1,1,1024]{3,1,2,0:T(2,128)(2,1)}, bf16[2048,1,1,...) fusion(bf16[2048,2,3,1024]{3,1,2,0:T(2,128)(2,1)} %param.23), kind=kLoop, calls=%fused_computation.215 | loop fusion | bytes 50331648 | tf_op jit(solution)/shard_map/slice | solution.py:552
  314.8 12.8 copy_bitcast_fusion.2
  327.6 9.7 fusion.8
  337.3 12.3 copy.141
  349.6 12.6 copy_bitcast_fusion.4
  362.2 8.2 fusion.10
  370.4 12.4 copy.138
  382.8 8.8 all_gather.37
  391.7 12.8 copy_bitcast_fusion
  404.5 24.3 %fusion.7 = f32[2048,2048]{1,0:T(8,128)} fusion(bf16[2048,2048]{1,0:T(8,128)(2,1)} %bitcast.381, bf16[2048,1024]{1,0:T(8,128)(2,1)} %get-tuple-element.133, bf16[2048,1024]{1,0:T(8,128)(2,1)} %get-tuple-element.134), kind=kOutput, calls=%fused_computation.23 | convolution fusion | flops 17196646400 | bytes 33554432 | tf_op jit(solution)/shard_map/dot_general | solution.py:46
  428.8 5.8 fusion.82
  434.8 22.1 %fusion.3 = f32[2048,2,1024]{0,2,1:T(8,128)} fusion(bf16[2,1024,2048]{2,1,0:T(8,128)(2,1)} %bitcast.321, bf16[2048,2048]{1,0:T(8,128)(2,1)S(1)} %copy-done.12), kind=kOutput, calls=%fused_computation.14 | convolution fusion | flops 17179869184 | bytes 33554432 | tf_op jit(solution)/shard_map/dot_general | solution.py:46
  456.9 41.1 %multiply_convert_fusion = (bf16[2048,2,1024]{0,2,1:T(8,128)(2,1)}, f32[2048,2]{0,1:T(2,128)}, bf16[2048,2,1024]{0,2,1:T(8,128)(2,1)}, bf16[2048,2,1024]{0,2,1:T(8,128)(2,1)}) fusion(f32[2048,2048]{1,0:T(8,128)} %fusion.7, f32[2048,2]{0,1:T(2,128)S(1)} %dynamic-slice_select_fusion, f32[2048,2,1024]{0,2,1:T(8,128)} %fusion.3, f32[2048,2,1024]{0,2,1:T(8,128)} %bitcast.384, ...), kind=kOutput, calls=%fused_computation.2 | convolution fusion | flops 17263751168 | bytes 92307456 | tf_op jit(solution)/shard_map/dot_general | solution.py:46
  498.1 25.0 %fusion.9 = f32[2048,2048]{1,0:T(8,128)} fusion(bf16[2048,2048]{0,1:T(8,128)(2,1)} %bitcast.389, bf16[2048,1024]{1,0:T(8,128)(2,1)} %get-tuple-element.137, bf16[2048,1024]{1,0:T(8,128)(2,1)} %get-tuple-element.138), kind=kOutput, calls=%fused_computation.25 | convolution fusion | flops 17196646400 | bytes 33554432 | tf_op jit(solution)/shard_map/rf,df->rd/dot_general | solution.py:633
  523.1 24.8 %add_convert_fusion = bf16[2048,2048]{1,0:T(8,128)(2,1)} fusion(f32[2048,2048]{1,0:T(8,128)} %fusion.9, bf16[2048,2048]{0,1:T(8,128)(2,1)} %bitcast.387, bf16[2048,1024]{1,0:T(8,128)(2,1)S(1)} %copy-done.10, bf16[2048,1024]{1,0:T(8,128)(2,1)S(1)} %copy-done.11), kind=kOutput, calls=%fused_computation.1 | convolution fusion | flops 17205035008 | bytes 41943040 | tf_op jit(solution)/shard_map/rf,df->rd/dot_general | solution.py:634
  553.0 7.2 collective-permute-done.16
  574.7 41.6 %all-to-all-done.1 = f32[8,256,2]{1,2,0:T(2,128)S(1)} async-done(((f32[8,256,2]{1,2,0:T(2,128)}), f32[8,256,2]{1,2,0:T(2,128)S(1)}, u32[]{:S(2)}, u32[]{:S(2)}) %all-to-all-start.1) | async-done | bytes 16416 | tf_op jit(solution)/shard_map/all_to_all | solution.py:578
  625.5 23.6 %convert_bitcast_fusion = bf16[2048,2048]{0,1:T(8,128)(2,1)} fusion(bf16[2048,2048]{0,1:T(8,128)(2,1)} %bitcast.385, bf16[2048,2048]{1,0:T(8,128)(2,1)} %bitcast.382), kind=kOutput, calls=%fused_computation.18 | convolution fusion | flops 17184063488 | bytes 25165824 | tf_op jit(solution)/shard_map/rd,rf->df/dot_general | solution.py:619
  649.1 24.1 %convolution_convert_fusion.1 = bf16[2048,2048]{1,0:T(8,128)(2,1)} fusion(bf16[2048,2048]{1,0:T(8,128)(2,1)} %all-gather.17.cloned.1.call-done, bf16[2048,2048]{0,1:T(8,128)(2,1)} %bitcast.390), kind=kOutput, calls=%fused_computation.20 | convolution fusion | flops 17184063488 | bytes 25165824 | tf_op jit(solution)/shard_map/rd,rf->df/dot_general | solution.py:619
  673.3 24.0 %convolution_convert_fusion = bf16[2048,2048]{1,0:T(8,128)(2,1)} fusion(bf16[2048,2048]{1,0:T(8,128)(2,1)} %all-gather.17.cloned.1.call-done, bf16[2048,2048]{0,1:T(8,128)(2,1)} %bitcast.388), kind=kOutput, calls=%fused_computation.19 | convolution fusion | flops 17184063488 | bytes 25165824 | tf_op jit(solution)/shard_map/rd,rf->df/dot_general | solution.py:619
  698.5 5.7 convolution_convert_fusion.4
  705.3 18.8 %all_to_all.21 = bf16[8,4,128,128]{3,2,1,0:T(8,128)(2,1)S(1)} all-to-all(bf16[8,4,128,128]{3,2,1,0:T(8,128)(2,1)S(1)} %bitcast.341), channel_id=1, replica_groups=mesh['ctx'=4,'exp'=8] {'exp'}, dimensions={0} | all-to-all | bytes 2097152 | tf_op jit(solution)/shard_map/all_to_all | solution.py:578
  731.3 19.9 %convolution_convert_fusion.2 = bf16[2048,2048]{1,0:T(8,128)(2,1)S(1)} fusion(bf16[2048,2048]{0,1:T(8,128)(2,1)} %bitcast.386, bf16[2048,1024]{1,0:T(8,128)(2,1)S(1)} %copy-done.28, bf16[2048,1024]{1,0:T(8,128)(2,1)S(1)} %copy-done.29), kind=kOutput, calls=%fused_computation.21 | convolution fusion | flops 17200840704 | bytes 25165824 | tf_op jit(solution)/shard_map/rf,df->rd/dot_general | solution.py:636
  751.3 8.8 collective-permute-done.21
  764.2 34.9 %attend_back.1 = bf16[4,3,1024,128]{3,2,1,0:T(8,128)(2,1)} custom-call(s32[1]{0:T(128)} %bitcast.1.place_ref, bf16[4,2,1024,128]{3,2,1,0:T(8,128)(2,1)} %pad_maximum_fusion.10.qk_ref, bf16[4,1024,128]{2,1,0:T(8,128)(2,1)S(1)} %copy-done.3, bf16[4,1024,128]{2,1,0:T(8,128)(2,1)S(1)} %pad_maximum_fusion.14.do_ref, f32[128,4096]{1,0:T(8,128)} %get-tuple-element.16.ot_ref, ...), custom_call_target="tpu_custom_call" | custom-call | flops 21474836480 | bytes 9437184 | tf_op jit(solution)/shard_map/attend_back/pallas_call | solution.py:235
  801.2 16.4 %collective-permute-start.23 = (bf16[3,1024,128]{2,1,0:T(8,128)(2,1)S(1)}, bf16[3,1024,128]{2,1,0:T(8,128)(2,1)S(1)}, u32[]{:S(2)}, u32[]{:S(2)}) collective-permute-start(bf16[3,1024,128]{2,1,0:T(8,128)(2,1)S(1)} %get-tuple-element.79), channel_id=1, source_target_pairs={{0,8},{8,0},{16,24},{24,16},{1,9},{9,1},{17,25},{25,17},{2,10},{10... | collective-permute-start | bytes 2359304 | tf_op jit(solution)/shard_map/ppermute | solution.py:50
  825.3 60.7 %collective-permute-done.23 = bf16[3,1024,128]{2,1,0:T(8,128)(2,1)S(1)} collective-permute-done((bf16[3,1024,128]{2,1,0:T(8,128)(2,1)S(1)}, bf16[3,1024,128]{2,1,0:T(8,128)(2,1)S(1)}, u32[]{:S(2)}, u32[]{:S(2)}) %collective-permute-start.23) | collective-permute-done | bytes 786464 | tf_op jit(solution)/shard_map/ppermute | solution.py:50
  886.0 7.4 collective-permute-done.24
  893.5 28.8 %collective-permute-done.25 = bf16[3,1024,128]{2,1,0:T(8,128)(2,1)S(1)} collective-permute-done((bf16[3,1024,128]{2,1,0:T(8,128)(2,1)S(1)}, bf16[3,1024,128]{2,1,0:T(8,128)(2,1)S(1)}, u32[]{:S(2)}, u32[]{:S(2)}) %collective-permute-start.25) | collective-permute-done | bytes 786464 | tf_op jit(solution)/shard_map/ppermute | solution.py:50
  953.0 7.9 fusion.2
  982.2 10.7 convolution_convert_fusion.3
  992.9 33.0 %copy.159 = bf16[6144,2048]{1,0:T(8,128)(2,1)} copy(bf16[6144,2048]{0,1:T(8,128)(2,1)} %all-gather.19.cloned.1.call-done) | data formatting | bytes 50331648 | tf_op jit(solution)/shard_map/all_gather | solution.py:539
  1025.9 6.0 fusion.23
  1033.3 13.7 multiply_reduce_fusion.4
  1047.0 27.5 %all-reduce.2 = (f32[2048]{0:T(1024)S(1)}, f32[2048]{0:T(1024)S(1)}) all-reduce(f32[2048]{0:T(1024)S(1)} %get-tuple-element.28, f32[2048]{0:T(1024)S(1)} %copy-done.43), channel_id=6, replica_groups=mesh['ctx'=4,'exp'=8] {'exp'}, use_global_device_ids=true, to_apply=%region_17.18.clone | all-reduce | flops 4096 | bytes 32768
  1074.7 49.9 %all-reduce.3 = (f32[256]{0:T(256)}, f32[256]{0:T(256)}, f32[256]{0:T(256)}, f32[256]{0:T(256)}, f32[256,16]{0,1:T(8,128)}) all-reduce(f32[256]{0:T(256)S(1)} %dynamic-slice.5, f32[256]{0:T(256)S(1)} %get-tuple-element.23, f32[256]{0:T(256)S(1)} %get-tuple-element.18, ...), channel_id=1, replica_groups=mesh['ctx'=4,'exp'=8] {'ctx'}, use_global_device_ids=true, to_apply=%region_18.19 | all-reduce | flops 5120 | bytes 40960 | tf_op jit(solution)/shard_map/psum | solution.py:692
  1124.6 6.3 multiply_add_fusion
  1140.5 107.2 %reduce-scatter.9.cloned.1.call-done = bf16[512,2048]{1,0:T(8,128)(2,1)} async-done(((bf16[2048,2048]{1,0:T(8,128)(2,1)}), bf16[512,2048]{1,0:T(8,128)(2,1)}) %reduce-scatter.9.cloned.1.call-update) | async-done | bytes 2097168 | tf_op jit(solution)/shard_map/reduce_scatter | solution.py:620
  1252.1 9.9 maximum_convert_fusion
  1262.0 144.3 %all-reduce.7.cloned.1.call-done = (bf16[2048,768]{1,0:T(8,128)(2,1)}, bf16[256,2048]{1,0:T(8,128)(2,1)}) async-done(((bf16[2048,768]{1,0:T(8,128)(2,1)}, bf16[256,2048]{1,0:T(8,128)(2,1)}), (bf16[2048,768]{1,0:T(8,128)(2,1)}, bf16[256,2048]{1,0:T(8,128)(2,1)})) %all-reduce.7.cloned.1.call-update) | async-done | bytes 4194320 | tf_op jit(solution)/shard_map/psum | solution.py:687
  (302 shorter events, 191.6 us)
Async XLA Ops:
  7.2 421.6 %copy-start = (bf16[2048,16]{0,1:T(8,128)(2,1)S(1)}, bf16[2048,16]{0,1:T(8,128)(2,1)}, u32[]{:S(2)}) copy-start(bf16[2048,16]{0,1:T(8,128)(2,1)} %param.22) | copy-start | bytes 196612
  7.2 62.8 %all-gather.11.cloned.1.call-start = ((), (), s32[]{:S(2)}) async-start(), calls=%async_computation.8 | async-start | bytes 9437184 | tf_op jit(solution)/shard_map/all_gather | solution.py:539
  12.8 243.0 %all-gather.15.cloned.1.call-start = ((), (), s32[]{:S(2)}) async-start(), calls=%async_computation.14 | async-start | bytes 9437184 | tf_op jit(solution)/shard_map/all_gather | solution.py:539
  13.5 390.9 %all-gather.13.cloned.1.call-start = ((), (), s32[]{:S(2)}) async-start(), calls=%async_computation.9 | async-start | bytes 9437184 | tf_op jit(solution)/shard_map/all_gather | solution.py:539
  14.3 414.5 %all-gather.17.cloned.1.call-start = ((), (), s32[]{:S(2)}) async-start(), calls=%async_computation.15 | async-start | bytes 9437184 | tf_op jit(solution)/shard_map/all_gather | solution.py:539
  82.4 1.2 collective-permute-start
  83.7 6.2 collective-permute-start.1
  89.9 4.1 collective-permute-start.2
  91.4 25.1 %collective-permute-start.6 = (bf16[1024,128]{1,0:T(8,128)(2,1)}, bf16[1024,128]{1,0:T(8,128)(2,1)}, u32[]{:S(2)}, u32[]{:S(2)}) collective-permute-start(bf16[1024,128]{1,0:T(8,128)(2,1)} %get-tuple-element.113), channel_id=1, source_target_pairs={{0,8},{8,0},{16,24},{24,16},{1,9},{9,1},{17,25},{25,17},{2,10},{10... | collective-permute-start | bytes 786440 | tf_op jit(solution)/shard_map/ppermute | solution.py:50
  110.5 69.0 %collective-permute-start.3 = (bf16[2,1024,128]{2,1,0:T(8,128)(2,1)S(1)}, bf16[2,1024,128]{2,1,0:T(8,128)(2,1)S(1)}, u32[]{:S(2)}, u32[]{:S(2)}) collective-permute-start(bf16[2,1024,128]{2,1,0:T(8,128)(2,1)S(1)} %get-tuple-element.87), channel_id=1, source_target_pairs={{0,8},{8,0},{16,24},{24,16},{1,9},{9,1},{17,25},{25,17},{2,10},{10... | collective-permute-start | bytes 1572872 | tf_op jit(solution)/shard_map/ppermute | solution.py:50
  112.1 67.4 %collective-permute-start.4 = (bf16[2,1024,128]{2,1,0:T(8,128)(2,1)S(1)}, bf16[2,1024,128]{2,1,0:T(8,128)(2,1)S(1)}, u32[]{:S(2)}, u32[]{:S(2)}) collective-permute-start(bf16[2,1024,128]{2,1,0:T(8,128)(2,1)S(1)} %get-tuple-element.88), channel_id=1, source_target_pairs={{0,16},{8,24},{16,0},{24,8},{1,17},{9,25},{17,1},{25,9},{2,18},{10... | collective-permute-start | bytes 1572872 | tf_op jit(solution)/shard_map/ppermute | solution.py:50
  114.5 65.0 %collective-permute-start.5 = (bf16[2,1024,128]{2,1,0:T(8,128)(2,1)S(1)}, bf16[2,1024,128]{2,1,0:T(8,128)(2,1)S(1)}, u32[]{:S(2)}, u32[]{:S(2)}) collective-permute-start(bf16[2,1024,128]{2,1,0:T(8,128)(2,1)S(1)} %get-tuple-element.89), channel_id=1, source_target_pairs={{0,24},{8,16},{16,8},{24,0},{1,25},{9,17},{17,9},{25,1},{2,26},{10... | collective-permute-start | bytes 1572872 | tf_op jit(solution)/shard_map/ppermute | solution.py:50
  115.0 63.4 %collective-permute-start.7 = (bf16[1024,128]{1,0:T(8,128)(2,1)S(1)}, bf16[1024,128]{1,0:T(8,128)(2,1)S(1)}, u32[]{:S(2)}, u32[]{:S(2)}) collective-permute-start(bf16[1024,128]{1,0:T(8,128)(2,1)S(1)} %copy-done.33), channel_id=1, source_target_pairs={{0,16},{8,24},{16,0},{24,8},{1,17},{9,25},{17,1},{25,9},{2,18},{10... | collective-permute-start | bytes 786440 | tf_op jit(solution)/shard_map/ppermute | solution.py:50
  116.5 61.9 %collective-permute-start.8 = (bf16[1024,128]{1,0:T(8,128)(2,1)S(1)}, bf16[1024,128]{1,0:T(8,128)(2,1)S(1)}, u32[]{:S(2)}, u32[]{:S(2)}) collective-permute-start(bf16[1024,128]{1,0:T(8,128)(2,1)S(1)} %copy-done.32), channel_id=1, source_target_pairs={{0,24},{8,16},{16,8},{24,0},{1,25},{9,17},{17,9},{25,1},{2,26},{10... | collective-permute-start | bytes 786440 | tf_op jit(solution)/shard_map/ppermute | solution.py:50
  209.2 11.8 collective-permute-start.9
  212.8 20.9 %collective-permute-start.10 = (bf16[1024,128]{1,0:T(8,128)(2,1)S(1)}, bf16[1024,128]{1,0:T(8,128)(2,1)S(1)}, u32[]{:S(2)}, u32[]{:S(2)}) collective-permute-start(bf16[1024,128]{1,0:T(8,128)(2,1)S(1)} %get-tuple-element.108), channel_id=1, source_target_pairs={{0,16},{8,24},{16,0},{24,8},{1,17},{9,25},{17,1},{25,9},{2,18},{10... | collective-permute-start | bytes 786440 | tf_op jit(solution)/shard_map/ppermute | solution.py:50
  213.9 19.8 %collective-permute-start.11 = (bf16[1024,128]{1,0:T(8,128)(2,1)S(1)}, bf16[1024,128]{1,0:T(8,128)(2,1)S(1)}, u32[]{:S(2)}, u32[]{:S(2)}) collective-permute-start(bf16[1024,128]{1,0:T(8,128)(2,1)S(1)} %get-tuple-element.107), channel_id=1, source_target_pairs={{0,24},{8,16},{16,8},{24,0},{1,25},{9,17},{17,9},{25,1},{2,26},{10... | collective-permute-start | bytes 786440 | tf_op jit(solution)/shard_map/ppermute | solution.py:50
  264.5 728.4 %all-gather.19.cloned.1.call-start = ((), (), s32[]{:S(2)}) async-start(), calls=%async_computation.16 | async-start | bytes 28311552 | tf_op jit(solution)/shard_map/all_gather | solution.py:539
  552.7 7.5 collective-permute-start.16
  567.3 49.5 %collective-permute-start.17 = (bf16[256,2048]{1,0:T(8,128)(2,1)}, bf16[256,2048]{1,0:T(8,128)(2,1)}, u32[]{:S(2)}, u32[]{:S(2)}) collective-permute-start(bf16[256,2048]{1,0:T(8,128)(2,1)} %get-tuple-element.58), channel_id=1, source_target_pairs={{0,2},{1,3},{2,0},{3,1},{4,6},{5,7},{6,4},{7,5},{8,10},{9,11},{10,... | collective-permute-start | bytes 3145736 | tf_op jit(solution)/shard_map/ppermute | solution.py:50
  568.2 48.6 %collective-permute-start.18 = (bf16[256,2048]{1,0:T(8,128)(2,1)}, bf16[256,2048]{1,0:T(8,128)(2,1)}, u32[]{:S(2)}, u32[]{:S(2)}) collective-permute-start(bf16[256,2048]{1,0:T(8,128)(2,1)} %get-tuple-element.60), channel_id=1, source_target_pairs={{0,4},{1,5},{2,6},{3,7},{4,0},{5,1},{6,2},{7,3},{8,12},{9,13},{10,... | collective-permute-start | bytes 3145736 | tf_op jit(solution)/shard_map/ppermute | solution.py:50
  569.4 47.5 %collective-permute-start.19 = (bf16[256,2048]{1,0:T(8,128)(2,1)}, bf16[256,2048]{1,0:T(8,128)(2,1)}, u32[]{:S(2)}, u32[]{:S(2)}) collective-permute-start(bf16[256,2048]{1,0:T(8,128)(2,1)} %get-tuple-element.59), channel_id=1, source_target_pairs={{0,6},{1,7},{2,4},{3,5},{4,2},{5,3},{6,0},{7,1},{8,14},{9,15},{10,... | collective-permute-start | bytes 3145736 | tf_op jit(solution)/shard_map/ppermute | solution.py:50
  571.3 45.0 %all-to-all-start.1 = ((f32[8,256,2]{1,2,0:T(2,128)}), f32[8,256,2]{1,2,0:T(2,128)S(1)}, u32[]{:S(2)}, u32[]{:S(2)}) async-start(f32[8,256,2]{1,2,0:T(2,128)} %bitcast.90), calls=%async_computation.1 | async-start | bytes 32768 | tf_op jit(solution)/shard_map/all_to_all | solution.py:578
  574.6 451.3 %all-gather.21.cloned.1.call-start = ((), (), s32[]{:S(2)}) async-start(), calls=%async_computation.17 | async-start | bytes 9437184 | tf_op jit(solution)/shard_map/all_gather | solution.py:539
  624.5 450.2 %reduce-scatter.5.cloned.1.call-start = ((), (), s32[]{:S(2)}) async-start(), calls=%async_computation.10 | async-start | bytes 147456 | tf_op jit(solution)/shard_map/reduce_scatter | solution.py:689
  625.4 505.5 %reduce-scatter.11.cloned.1.call-start = ((), (), s32[]{:S(2)}) async-start(), calls=%async_computation.13 | async-start | bytes 10485760 | tf_op jit(solution)/shard_map/reduce_scatter | solution.py:620
  649.1 486.9 %reduce-scatter.7.cloned.1.call-start = ((), (), s32[]{:S(2)}) async-start(), calls=%async_computation.11 | async-start | bytes 10485760 | tf_op jit(solution)/shard_map/reduce_scatter | solution.py:620
  673.2 574.4 %reduce-scatter.9.cloned.1.call-start = ((), (), s32[]{:S(2)}) async-start(), calls=%async_computation.12 | async-start | bytes 10485760 | tf_op jit(solution)/shard_map/reduce_scatter | solution.py:620
  724.3 35.7 %collective-permute-start.21 = (bf16[1024,128]{1,0:T(8,128)(2,1)S(1)}, bf16[1024,128]{1,0:T(8,128)(2,1)S(1)}, u32[]{:S(2)}, u32[]{:S(2)}) collective-permute-start(bf16[1024,128]{1,0:T(8,128)(2,1)S(1)} %get-tuple-element.100), channel_id=1, source_target_pairs={{0,16},{8,24},{16,0},{24,8},{1,17},{9,25},{17,1},{25,9},{2,18},{10... | collective-permute-start | bytes 786440 | tf_op jit(solution)/shard_map/ppermute | solution.py:50
  729.9 30.1 %collective-permute-start.22 = (bf16[1024,128]{1,0:T(8,128)(2,1)S(1)}, bf16[1024,128]{1,0:T(8,128)(2,1)S(1)}, u32[]{:S(2)}, u32[]{:S(2)}) collective-permute-start(bf16[1024,128]{1,0:T(8,128)(2,1)S(1)} %get-tuple-element.99), channel_id=1, source_target_pairs={{0,24},{8,16},{16,8},{24,0},{1,25},{9,17},{17,9},{25,1},{2,26},{10... | collective-permute-start | bytes 786440 | tf_op jit(solution)/shard_map/ppermute | solution.py:50
  731.3 32.8 %collective-permute-start.20 = (bf16[1024,128]{1,0:T(8,128)(2,1)S(1)}, bf16[1024,128]{1,0:T(8,128)(2,1)S(1)}, u32[]{:S(2)}, u32[]{:S(2)}) collective-permute-start(bf16[1024,128]{1,0:T(8,128)(2,1)S(1)} %get-tuple-element.101), channel_id=1, source_target_pairs={{0,8},{8,0},{16,24},{24,16},{1,9},{9,1},{17,25},{25,17},{2,10},{10... | collective-permute-start | bytes 786440 | tf_op jit(solution)/shard_map/ppermute | solution.py:50
  751.3 69.0 %copy-start.13 = (bf16[2048,2048]{1,0:T(8,128)(2,1)}, bf16[2048,2048]{1,0:T(8,128)(2,1)S(1)}, u32[]{:S(2)}) copy-start(bf16[2048,2048]{1,0:T(8,128)(2,1)S(1)} %convolution_convert_fusion.2) | copy-start | bytes 25165828
  801.2 84.8 %collective-permute-start.23 = (bf16[3,1024,128]{2,1,0:T(8,128)(2,1)S(1)}, bf16[3,1024,128]{2,1,0:T(8,128)(2,1)S(1)}, u32[]{:S(2)}, u32[]{:S(2)}) collective-permute-start(bf16[3,1024,128]{2,1,0:T(8,128)(2,1)S(1)} %get-tuple-element.79), channel_id=1, source_target_pairs={{0,8},{8,0},{16,24},{24,16},{1,9},{9,1},{17,25},{25,17},{2,10},{10... | collective-permute-start | bytes 2359304 | tf_op jit(solution)/shard_map/ppermute | solution.py:50
  817.6 75.8 %collective-permute-start.24 = (bf16[3,1024,128]{2,1,0:T(8,128)(2,1)S(1)}, bf16[3,1024,128]{2,1,0:T(8,128)(2,1)S(1)}, u32[]{:S(2)}, u32[]{:S(2)}) collective-permute-start(bf16[3,1024,128]{2,1,0:T(8,128)(2,1)S(1)} %get-tuple-element.78), channel_id=1, source_target_pairs={{0,16},{8,24},{16,0},{24,8},{1,17},{9,25},{17,1},{25,9},{2,18},{10... | collective-permute-start | bytes 2359304 | tf_op jit(solution)/shard_map/ppermute | solution.py:50
  818.9 103.4 %collective-permute-start.25 = (bf16[3,1024,128]{2,1,0:T(8,128)(2,1)S(1)}, bf16[3,1024,128]{2,1,0:T(8,128)(2,1)S(1)}, u32[]{:S(2)}, u32[]{:S(2)}) collective-permute-start(bf16[3,1024,128]{2,1,0:T(8,128)(2,1)S(1)} %get-tuple-element.77), channel_id=1, source_target_pairs={{0,24},{8,16},{16,8},{24,0},{1,25},{9,17},{17,9},{25,1},{2,26},{10... | collective-permute-start | bytes 2359304 | tf_op jit(solution)/shard_map/ppermute | solution.py:50
  822.9 130.1 %collective-permute-start.12 = (bf16[4,256,2048]{2,1,0:T(8,128)(2,1)}, bf16[4,256,2048]{2,1,0:T(8,128)(2,1)}, u32[]{:S(2)}, u32[]{:S(2)}) collective-permute-start(bf16[4,256,2048]{2,1,0:T(8,128)(2,1)} %dynamic-slice_bitcast_fusion.1), channel_id=1, source_target_pairs={{0,1},{1,0},{2,3},{3,2},{4,5},{5,4},{6,7},{7,6},{8,9},{9,8},{10,11... | collective-permute-start | bytes 12582920 | tf_op jit(solution)/shard_map/ppermute | solution.py:50
  947.5 1.2 collective-permute-start.26
  948.8 4.0 collective-permute-start.27
  952.8 10.6 collective-permute-start.28
  970.2 61.8 %all-to-all-start.3 = ((bf16[8,256,768]{2,1,0:T(8,128)(2,1)}), bf16[8,256,768]{2,1,0:T(8,128)(2,1)}, u32[]{:S(2)}, u32[]{:S(2)}) async-start(bf16[8,256,768]{2,1,0:T(8,128)(2,1)} %pad_maximum_fusion.9), calls=%async_computation.3 | async-start | bytes 6291456 | tf_op jit(solution)/shard_map/all_to_all | solution.py:578
  974.6 431.7 %all-reduce.7.cloned.1.call-start = ((), (), s32[]{:S(2)}) async-start(), calls=%async_computation.18 | async-start | bytes 8388608 | tf_op jit(solution)/shard_map/psum | solution.py:687
  978.6 146.0 %collective-permute-start.13 = (bf16[256,2048]{1,0:T(8,128)(2,1)}, bf16[256,2048]{1,0:T(8,128)(2,1)}, u32[]{:S(2)}, u32[]{:S(2)}) collective-permute-start(bf16[256,2048]{1,0:T(8,128)(2,1)} %get-tuple-element.61), channel_id=1, source_target_pairs={{0,2},{1,3},{2,0},{3,1},{4,6},{5,7},{6,4},{7,5},{8,10},{9,11},{10,... | collective-permute-start | bytes 3145736 | tf_op jit(solution)/shard_map/ppermute | solution.py:50
  980.4 144.2 %collective-permute-start.14 = (bf16[256,2048]{1,0:T(8,128)(2,1)}, bf16[256,2048]{1,0:T(8,128)(2,1)}, u32[]{:S(2)}, u32[]{:S(2)}) collective-permute-start(bf16[256,2048]{1,0:T(8,128)(2,1)} %get-tuple-element.63), channel_id=1, source_target_pairs={{0,4},{1,5},{2,6},{3,7},{4,0},{5,1},{6,2},{7,3},{8,12},{9,13},{10,... | collective-permute-start | bytes 3145736 | tf_op jit(solution)/shard_map/ppermute | solution.py:50
  981.9 142.7 %collective-permute-start.15 = (bf16[256,2048]{1,0:T(8,128)(2,1)}, bf16[256,2048]{1,0:T(8,128)(2,1)}, u32[]{:S(2)}, u32[]{:S(2)}) collective-permute-start(bf16[256,2048]{1,0:T(8,128)(2,1)} %get-tuple-element.62), channel_id=1, source_target_pairs={{0,6},{1,7},{2,4},{3,5},{4,2},{5,3},{6,0},{7,1},{8,14},{9,15},{10,... | collective-permute-start | bytes 3145736 | tf_op jit(solution)/shard_map/ppermute | solution.py:50
  1033.2 91.4 %copy-start.7 = (f32[256,2048]{1,0:T(8,128)S(1)}, f32[256,2048]{1,0:T(8,128)}, u32[]{:S(2)}) copy-start(f32[256,2048]{1,0:T(8,128)} %copy-done.5) | copy-start | bytes 6291460
  1033.2 91.4 %copy-start.36 = (f32[2048]{0:T(1024)S(1)}, f32[2048]{0:T(1024)}, u32[]{:S(2)}) copy-start(f32[2048]{0:T(1024)} %param.21) | copy-start | bytes 24580
  1033.2 91.4 %copy-start.48 = (f32[256]{0:T(256)S(1)}, f32[256]{0:T(256)}, u32[]{:S(2)}) copy-start(f32[256]{0:T(256)} %copy-done.46) | copy-start | bytes 3076
  1033.3 91.4 %copy-start.52 = (f32[256]{0:T(256)S(1)}, f32[256]{0:T(256)}, u32[]{:S(2)}) copy-start(f32[256]{0:T(256)} %copy-done.51) | copy-start | bytes 3076
  (54 other events, 677.2 us)
Sparse Core Ops, SparseCore 0:
  12.9 57.0 all-gather.10
  71.9 54.7 all-gather.14
  128.6 54.3 all-gather.12
  264.7 54.4 all-gather.16
  320.9 125.0 all-gather.18
  624.6 55.7 all-gather.20
  683.4 33.4 reduce-scatter.4
  719.4 217.5 reduce-scatter.10
  939.4 160.0 reduce-scatter.6
  1101.8 145.7 reduce-scatter.8
  1250.2 156.0 all-reduce.6

commit v2 on v1

--- a/solution.py
+++ b/solution.py
@@ -17,6 +17,7 @@
 masked_score = -1e30
 LOG2E = 1.4426950408889634
 F32 = jnp.float32
+SMALL = pl.CostEstimate(flops=0, bytes_accessed=0, transcendentals=0)
 BF16 = jnp.bfloat16
 
 
@@ -54,6 +55,22 @@
     return lax.dynamic_index_in_dim(values, index, axis, keepdims=False)
 
 
+def hold_kernel(*refs):
+    del refs
+
+
+def hold(value, *after):
+    return pl.pallas_call(
+        hold_kernel,
+        out_shape=jax.ShapeDtypeStruct(value.shape, value.dtype),
+        in_specs=[pl.BlockSpec(memory_space=pl.ANY)] * (1 + len(after)),
+        out_specs=pl.BlockSpec(memory_space=pl.ANY),
+        input_output_aliases={0: 0},
+        cost_estimate=SMALL,
+        name="hold",
+    )(value, *after)
+
+
 def butterfly_sum(values, axis):
     mask = 1
     while mask < lax.axis_size(axis):
@@ -62,7 +79,7 @@
     return values
 
 
-def reduce_rows(partial, own=None):
+def reduce_rows(partial, *after):
     count = partial.shape[0]
     me = lax.axis_index("exp")
     core, chip = me % 2, me // 2
@@ -71,6 +88,7 @@
     mine = pick(pairs, core, 1)
     both = (mine.astype(F32) + got.astype(F32)).astype(BF16)
     parts = [flip(pick(both, chip ^ m), "exp", 2 * m) for m in range(1, count // 2)]
+    parts = [hold(part, *after) for part in parts]
     total = pick(mine, chip).astype(F32) + pick(got, chip).astype(F32)
     for part in parts:
         total = total + part.astype(F32)
@@ -142,7 +160,19 @@
 
 
 def attend_back_kernel(
-    place_ref, qk_ref, v_ref, do_ref, ot_ref, lse_ref, d_ref, qt_ref, kt_ref, dot_ref, dk_ref, dv_ref
+    place_ref,
+    qk_ref,
+    v_ref,
+    do_ref,
+    ot_ref,
+    lse_ref,
+    d_ref,
+    sums_ref,
+    qt_ref,
+    kt_ref,
+    dot_ref,
+    dk_ref,
+    dv_ref,
 ):
     ctx_count, rows = v_ref.shape[0], v_ref.shape[1] // 2
     blocks = 2 * ctx_count
@@ -186,7 +216,10 @@
 
         dq = part(block, jnp.zeros((HD, rows), F32), True)
         dq = lax.fori_loop(0, block, lambda j, c: part(j, c, False), dq)
-        d_ref[slab_q, 0, at_q, :] = (dq * score_scale).T.astype(BF16)
+        dq = dq * score_scale
+        d_ref[slab_q, 0, at_q, :] = dq.T.astype(BF16)
+        sums = jnp.sum(dq * query_t.astype(F32), axis=0, keepdims=True)
+        sums_ref[slab_q, pl.ds(half_q, 1), :] = sums
         return unused
 
     lax.fori_loop(0, blocks, query_block, 0)
@@ -195,7 +228,10 @@
         slab, half = block_place(block, ctx_count, place)
         at = pl.ds(pl.multiple_of(half * rows, rows), rows)
         to = pl.ds(pl.multiple_of(block * rows, rows), rows)
-        d_ref[slab, 1, at, :] = (dk_ref[to, :] * score_scale).astype(BF16)
+        dk = dk_ref[to, :] * score_scale
+        d_ref[slab, 1, at, :] = dk.astype(BF16)
+        sums = jnp.sum(dk.T * kt_ref[:, to].astype(F32), axis=0, keepdims=True)
+        sums_ref[slab, pl.ds(2 + half, 1), :] = sums
         d_ref[slab, 2, at, :] = dv_ref[to, :].astype(BF16)
         return unused
 
@@ -221,9 +257,7 @@
         out_specs=(VMEM, VMEM, VMEM),
         scratch_shapes=[pltpu.VMEM((HD, length), BF16), pltpu.VMEM((HD, length), BF16)],
         compiler_params=pltpu.CompilerParams(vmem_limit_bytes=50 * 2**20),
-        cost_estimate=pl.CostEstimate(
-            flops=8 * pairs * HD, bytes_accessed=12 * length * HD, transcendentals=pairs
-        ),
+        cost_estimate=SMALL,
         name="attend",
     )(place, qk, v)
 
@@ -234,14 +268,15 @@
     pairs = length * length // 2
     return pl.pallas_call(
         attend_back_kernel,
-        out_shape=jax.ShapeDtypeStruct((ctx_count, 3, ctx_rows, HD), BF16),
+        out_shape=(
+            jax.ShapeDtypeStruct((ctx_count, 3, ctx_rows, HD), BF16),
+            jax.ShapeDtypeStruct((ctx_count, 4, ctx_rows // 2), F32),
+        ),
         in_specs=[SMEM] + [VMEM] * 5,
-        out_specs=VMEM,
+        out_specs=(VMEM, VMEM),
         scratch_shapes=[pltpu.VMEM((HD, length), BF16)] * 3 + [pltpu.VMEM((length, HD), F32)] * 2,
         compiler_params=pltpu.CompilerParams(vmem_limit_bytes=50 * 2**20),
-        cost_estimate=pl.CostEstimate(
-            flops=20 * pairs * HD, bytes_accessed=18 * length * HD, transcendentals=pairs
-        ),
+        cost_estimate=SMALL,
         name="attend_back",
     )(place, qk, v, grads, out_t, lse)
 
@@ -260,67 +295,172 @@
     return jnp.stack([pick(parts, place ^ p) for p in range(count)])
 
 
-def paired_forward(queries, keys_proj, values_low, query_gain, key_gain, cosine, sines, model_width):
-    exp_count, seq_count, shard_len, local_width = queries.shape
+def rotate_kernel(proj_ref, stat_ref, gain_ref, cos_ref, sin_ref, out_ref):
+    heads, rows = out_ref.shape[1], proj_ref.shape[2]
+    for group in range(proj_ref.shape[0]):
+        line = slice(group * rows, (group + 1) * rows)
+        cosine, sines = cos_ref[line, :], sin_ref[line, :]
+        for which in range(2):
+            factor = stat_ref[group, 0, :, which : which + 1]
+            for head in range(heads):
+                at = slice((which * heads + head) * HD, (which * heads + head + 1) * HD)
+                unit = proj_ref[group, 0, :, at] * factor * gain_ref[:, at]
+                turned = pltpu.roll(unit, HD // 2, 1)
+                out_ref[0, head, which, line, :] = (unit * cosine + turned * sines).astype(BF16)
+
+
+def rotate_call(projected, stats, gains, cosine, turn_sines):
+    exp_count, seq_count, shard_len, width = projected.shape
+    local_heads = width // 3 // HD
+    group = math.gcd(exp_count, 4)
+    shape = (seq_count, local_heads, 2, exp_count * shard_len, HD)
+    line_spec = pl.BlockSpec((group * shard_len, HD), lambda s, e: (e, 0))
+    out = pl.pallas_call(
+        rotate_kernel,
+        grid=(seq_count, exp_count // group),
+        in_specs=[
+            pl.BlockSpec((group, 1, shard_len, width), lambda s, e: (e, s, 0, 0)),
+            pl.BlockSpec((group, 1, shard_len, stats.shape[-1]), lambda s, e: (e, s, 0, 0)),
+            pl.BlockSpec((1, gains.shape[1]), lambda s, e: (0, 0)),
+            line_spec,
+            line_spec,
+        ],
+        out_specs=pl.BlockSpec(
+            (1, local_heads, 2, group * shard_len, HD), lambda s, e: (s, 0, 0, e, 0)
+        ),
+        out_shape=jax.ShapeDtypeStruct(shape, BF16),
+        cost_estimate=SMALL,
+        name="rotate",
+    )(projected, stats, gains, cosine, turn_sines)
+    return out.reshape((-1,) + shape[2:])
+
+
+def norm_back_kernel(place_ref, proj_ref, stat_ref, gain_ref, cos_ref, sin_ref, *refs):
+    heads = len(refs) - 2
+    back_refs, out_ref, sum_ref = refs[:heads], refs[heads], refs[heads + 1]
+    rows = proj_ref.shape[2]
+
+    @pl.when((pl.program_id(0) == 0) & (pl.program_id(1) == 0))
+    def start():
+        sum_ref[...] = jnp.zeros_like(sum_ref)
+
+    for group in range(proj_ref.shape[0]):
+        line = slice(group * rows, (group + 1) * rows)
+        cosine, sines = cos_ref[line, :], sin_ref[line, :]
+        for which in range(2):
+            factor = stat_ref[group, 0, :, which : which + 1]
+            mean = stat_ref[group, 0, :, 2 + which : 3 + which]
+            for head in range(heads):
+                at = slice((which * heads + head) * HD, (which * heads + head + 1) * HD)
+                grad = back_refs[head][0, which, line, :].astype(F32)
+                grad = grad * cosine + pltpu.roll(grad, HD // 2, 1) * sines
+                unit = proj_ref[group, 0, :, at] * factor
+                sum_ref[:, at] += jnp.sum(grad * unit, axis=0, keepdims=True)
+                grad = factor * (grad * gain_ref[:, at] - unit * mean)
+                out_ref[group, 0, :, at] = grad.astype(BF16)
+        for head in range(heads):
+            at = slice((2 * heads + head) * HD, (2 * heads + head + 1) * HD)
+            out_ref[group, 0, :, at] = back_refs[head][0, 2, line, :]
+
+
+def norm_back_call(place, projected, stats, gains, cosine, back_sines, back):
+    exp_count, seq_count, shard_len, width = projected.shape
+    local_heads = width // 3 // HD
+    group = math.gcd(exp_count, 4)
+
+    def back_spec(head):
+        return pl.BlockSpec(
+            (1, 3, group * shard_len, HD),
+            lambda s, e, p: ((s * local_heads + head) ^ p[0], 0, e, 0),
+        )
+
+    wide_spec = pl.BlockSpec((group, 1, shard_len, width), lambda s, e, p: (e, s, 0, 0))
+    line_spec = pl.BlockSpec((group * shard_len, HD), lambda s, e, p: (e, 0))
+    gain_spec = pl.BlockSpec((1, gains.shape[1]), lambda s, e, p: (0, 0))
+    return pl.pallas_call(
+        norm_back_kernel,
+        grid_spec=pltpu.PrefetchScalarGridSpec(
+            num_scalar_prefetch=1,
+            grid=(seq_count, exp_count // group),
+            in_specs=[
+                wide_spec,
+                pl.BlockSpec(
+                    (group, 1, shard_len, stats.shape[-1]), lambda s, e, p: (e, s, 0, 0)
+                ),
+                gain_spec,
+                line_spec,
+                line_spec,
+            ]
+            + [back_spec(head) for head in range(local_heads)],
+            out_specs=(wide_spec, gain_spec),
+        ),
+        out_shape=(
+            jax.ShapeDtypeStruct(projected.shape, BF16),
+            jax.ShapeDtypeStruct(gains.shape, F32),
+        ),
+        cost_estimate=SMALL,
+        name="norm_back",
+    )(place, projected, stats, gains, cosine, back_sines, *([back] * local_heads))
+
+
+def half_signs(sines, first, second):
+    half_size = sines.shape[1] // 2
+    return jnp.concatenate([first * sines[:, :half_size], second * sines[:, half_size:]], axis=1)
+
+
+def paired_forward(projected, query_gain, key_gain, cosine, sines, model_width, early):
+    exp_count, seq_count, shard_len, width = projected.shape
+    local_width = width // 3
     local_heads = local_width // HD
     ctx_rows = exp_count * shard_len
-
-    def by_pair(values):
-        values = values.reshape(exp_count, seq_count, shard_len, local_heads, HD)
-        return jnp.transpose(values, (1, 3, 0, 2, 4)).reshape(-1, ctx_rows, HD)
-
-    v_all = spread_pairs(by_pair(values_low))
+    values = projected[..., 2 * local_width :].astype(BF16)
+    values = values.reshape(exp_count, seq_count, shard_len, local_heads, HD)
+    v_all = spread_pairs(jnp.transpose(values, (1, 3, 0, 2, 4)).reshape(-1, ctx_rows, HD))
     squares = jnp.stack(
-        [jnp.sum(queries * queries, axis=-1), jnp.sum(keys_proj * keys_proj, axis=-1)]
+        [
+            jnp.sum(jnp.square(projected[..., i * local_width : (i + 1) * local_width]), axis=-1)
+            for i in range(2)
+        ]
     )
     squares = butterfly_sum(squares, "exp")
-    factors = lax.rsqrt(squares[..., None] / model_width + norm_eps)
-    query_unit = queries * factors[0]
-    key_unit = keys_proj * factors[1]
-
-    def rotated(values):
-        pairs = by_pair(values)
-        return (pairs * cosine + turn(pairs) * sines).astype(BF16)
-
-    rotated_qk = jnp.stack([rotated(query_unit * query_gain), rotated(key_unit * key_gain)], axis=1)
-    qk_all = spread_pairs(rotated_qk)
+    factors = lax.rsqrt(squares / model_width + norm_eps)
+    gains = jnp.concatenate([query_gain, key_gain])[None]
+    stats = jnp.stack([factors[0], factors[1]], axis=-1)
+    rotated_qk = rotate_call(projected, stats, gains, cosine, half_signs(sines, -1.0, 1.0))
+    qk_all = hold(spread_pairs(rotated_qk), early)
     place = lax.axis_index("ctx").astype(jnp.int32).reshape(1)
     out, out_t, lse = attend_call(place, qk_all, v_all)
-    attended = return_pairs(out)
-    return attended, (place, qk_all, v_all, out_t, lse, query_unit, key_unit, factors)
-
-
-def paired_backward(kept, grads, query_gain, key_gain, cosine, sines, model_width):
-    place, qk_all, v_all, out_t, lse, query_unit, key_unit, factors = kept
-    exp_count, seq_count, shard_len, local_width = query_unit.shape
-    local_heads = local_width // HD
-    back = attend_back_call(place, qk_all, v_all, spread_pairs(grads), out_t, lse)
-    back = return_pairs(back)
-
-    def by_row(values):
-        values = values.reshape(seq_count, local_heads, exp_count, shard_len, HD)
-        return jnp.transpose(values, (2, 0, 3, 1, 4)).reshape(query_unit.shape)
-
-    def unrotated(values):
-        values = values.astype(F32)
-        return by_row(values * cosine + turn_back(values) * sines)
-
-    qnorm_grad, knorm_grad = unrotated(back[:, 0]), unrotated(back[:, 1])
-    grad_values = by_row(back[:, 2])
-    qgain_part = jnp.sum(qnorm_grad * query_unit, axis=(0, 1, 2))
-    kgain_part = jnp.sum(knorm_grad * key_unit, axis=(0, 1, 2))
-    qunit_grad = qnorm_grad * query_gain
-    kunit_grad = knorm_grad * key_gain
-    dots = jnp.stack(
-        [jnp.sum(qunit_grad * query_unit, axis=-1), jnp.sum(kunit_grad * key_unit, axis=-1)]
-    )
-    dots = butterfly_sum(dots, "exp")[..., None] / model_width
-    grad_queries = (factors[0] * (qunit_grad - query_unit * dots[0])).astype(BF16)
-    grad_keys = (factors[1] * (kunit_grad - key_unit * dots[1])).astype(BF16)
-    return jnp.concatenate([grad_queries, grad_keys, grad_values], axis=-1), qgain_part, kgain_part
-
-
-def gathered_forward(queries, keys_proj, values_low, query_gain, key_gain, cosine, sines, model_width):
+    natural = jnp.stack([pick(out, place[0] ^ p) for p in range(out.shape[0])])
+    natural = natural.reshape(-1, shard_len, HD)
+    own = lax.all_to_all(natural, ("ctx", "exp"), split_axis=0, concat_axis=0, tiled=True)
+    own = own.reshape(seq_count, local_heads, exp_count, shard_len, HD)
+    own = jnp.transpose(own, (0, 3, 2, 1, 4)).reshape(seq_count * shard_len, -1)
+    return (own, out), (place, qk_all, v_all, out_t, lse, projected, factors, gains)
+
+
+def paired_backward(kept, grads, query_gain, key_gain, cosine, sines, model_width, early, later):
+    place, qk_all, v_all, out_t, lse, projected, factors, gains = kept
+    exp_count, seq_count, shard_len, width = projected.shape
+    local_heads = width // 3 // HD
+    grads = hold(spread_pairs(grads), *early)
+    back, sums = attend_back_call(place, qk_all, v_all, grads, out_t, lse)
+    count = back.shape[0]
+    parts = jnp.stack([back[0]] + [flip(back[m], "ctx", m) for m in range(1, count)])
+    parts = hold(parts, *later)
+    sums = butterfly_sum(return_pairs(sums), "exp")
+    sums = sums.reshape(seq_count, local_heads, 2, exp_count, shard_len).sum(axis=1) / model_width
+    sums = jnp.transpose(sums, (1, 2, 0, 3))
+    stats = jnp.stack([factors[0], factors[1], sums[0], sums[1]], axis=-1)
+    grad_qkv, gain_parts = norm_back_call(
+        place, projected, stats, gains, cosine, half_signs(sines, 1.0, -1.0), parts
+    )
+    qgain_part, kgain_part = jnp.split(gain_parts[0], 2)
+    return grad_qkv, qgain_part, kgain_part, sums
+
+
+def gathered_forward(projected, query_gain, key_gain, cosine, sines, model_width, early):
+    queries, keys_proj, values_low = jnp.split(projected, 3, axis=-1)
+    values_low = values_low.astype(BF16)
     exp_count, seq_count, shard_len, local_width = queries.shape
     ctx_count, ctx_place = lax.axis_size("ctx"), lax.axis_index("ctx")
     local_heads = local_width // HD
@@ -388,7 +528,11 @@
     kept = (
         query_rot, keys_all, values_all, attended_float, log_halves, query_unit, key_unit, factors
     )
-    return attended, kept
+    sent = jnp.transpose(attended.reshape(-1, exp_count, shard_len, HD), (1, 0, 2, 3))
+    own = lax.all_to_all(sent, "exp", split_axis=0, concat_axis=0, tiled=True)
+    own = own.reshape(exp_count, seq_count, local_heads, shard_len, HD)
+    own = jnp.transpose(own, (1, 3, 0, 2, 4)).reshape(seq_count * shard_len, -1)
+    return (own, attended), kept
 
 
 def block_tools(half_rows, ctx_count, ctx_place):
@@ -415,7 +559,9 @@
     return block_len, half_firsts, row_start, block_scores
 
 
-def gathered_backward(kept, grads, query_gain, key_gain, cosine, sines, model_width):
+def gathered_backward(
+    kept, grads, query_gain, key_gain, cosine, sines, model_width, early, later
+):
     query_rot, keys_all, values_all, attended_float, log_halves, query_unit, key_unit, factors = kept
     exp_count, seq_count, shard_len, local_width = query_unit.shape
     ctx_count, ctx_place = lax.axis_size("ctx"), lax.axis_index("ctx")
@@ -502,7 +648,208 @@
     dots = lax.psum(dots, "exp")[..., None] / model_width
     grad_queries = (factors[0] * (qunit_grad - query_unit * dots[0])).astype(BF16)
     grad_keys = (factors[1] * (kunit_grad - key_unit * dots[1])).astype(BF16)
-    return jnp.concatenate([grad_queries, grad_keys, grad_values], axis=-1), qgain_part, kgain_part
+    grad_qkv = jnp.concatenate([grad_queries, grad_keys, grad_values], axis=-1)
+    return grad_qkv, qgain_part, kgain_part, dots
+
+
+NT = (((1,), (1,)), ((), ()))
+TN = (((0,), (0,)), ((), ()))
+EXPERT_PARAMS = pltpu.CompilerParams(vmem_limit_bytes=58 * 2**20)
+
+
+def down_kernel(half_ref, rows_ref, weight_ref, out_ref):
+    out_ref[0] = dot32(rows_ref[...], weight_ref[0, 0])
+
+
+def down_call(rows, weights, half, width):
+    count, model_width = rows.shape
+    experts = weights.shape[0]
+    tile, cols = math.gcd(count, 1024), math.gcd(width, 1024)
+    parts = width // cols
+    return pl.pallas_call(
+        down_kernel,
+        grid_spec=pltpu.PrefetchScalarGridSpec(
+            num_scalar_prefetch=1,
+            grid=(experts, parts, count // tile),
+            in_specs=[
+                pl.BlockSpec((tile, model_width), lambda e, f, r, h: (r, 0)),
+                pl.BlockSpec(
+                    (1, 1, model_width, cols), lambda e, f, r, h: (e, 2, 0, h[0] * parts + f)
+                ),
+            ],
+            out_specs=pl.BlockSpec((1, tile, cols), lambda e, f, r, h: (e, r, f)),
+        ),
+        out_shape=jax.ShapeDtypeStruct((experts, count, width), F32),
+        compiler_params=EXPERT_PARAMS,
+        cost_estimate=SMALL,
+        name="down",
+    )(half, rows, weights)
+
+
+def hidden_kernel(
+    half_ref, rows_ref, wg_ref, wu_ref, down_ref, gate_ref, gm_ref, gg_ref, gu_ref, *dots, chunk
+):
+    width = wg_ref.shape[-1]
+
+    def step(i, unused):
+        at = pl.ds(pl.multiple_of(i * chunk, chunk), chunk)
+        rows = rows_ref[at, :]
+        pre_gate = dot32(rows, wg_ref[0, 0])
+        pre_up = dot32(rows, wu_ref[0, 0])
+        down, gate = down_ref[0, at, :], gate_ref[0, at, :]
+        sigmoid_vals = 1.0 / (1.0 + jnp.exp(-pre_gate))
+        activated = pre_gate * sigmoid_vals
+        middle = activated * pre_up
+        for dot_ref in dots:
+            products = middle * down
+            acc = products[:, :128]
+            for c in range(1, width // 128):
+                acc = acc + products[:, c * 128 : (c + 1) * 128]
+            dot_ref[0, 0, at, :] = acc
+        gm_ref[0, at, :] = (gate * middle).astype(BF16)
+        grad = gate * down
+        gu_ref[0, at, :] = (grad * activated).astype(BF16)
+        slope = sigmoid_vals * (1.0 + pre_gate * (1.0 - sigmoid_vals))
+        gg_ref[0, at, :] = (grad * pre_up * slope).astype(BF16)
+        return unused
+
+    lax.fori_loop(0, rows_ref.shape[0] // chunk, step, 0)
+
+
+def hidden_call(rows, weights, down, gates, half, with_dots):
+    count, model_width = rows.shape
+    experts, width = weights.shape[0], down.shape[-1]
+    tile, cols = math.gcd(count, 1024), math.gcd(width, 512)
+    parts = width // cols
+    wide = pl.BlockSpec((1, tile, cols), lambda e, f, r, h: (e, r, f))
+    shape = jax.ShapeDtypeStruct((experts, count, width), BF16)
+    out_specs, out_shape = [wide] * 3, [shape] * 3
+    if with_dots:
+        out_specs.append(pl.BlockSpec((1, 1, tile, 128), lambda e, f, r, h: (e, f, r, 0)))
+        out_shape.append(jax.ShapeDtypeStruct((experts, parts, count, 128), F32))
+
+    def weight_spec(which):
+        return pl.BlockSpec(
+            (1, 1, model_width, cols), lambda e, f, r, h: (e, which, 0, h[0] * parts + f)
+        )
+
+    return pl.pallas_call(
+        functools.partial(hidden_kernel, chunk=math.gcd(tile, 256)),
+        grid_spec=pltpu.PrefetchScalarGridSpec(
+            num_scalar_prefetch=1,
+            grid=(experts, parts, count // tile),
+            in_specs=[
+                pl.BlockSpec((tile, model_width), lambda e, f, r, h: (r, 0)),
+                weight_spec(0),
+                weight_spec(1),
+                wide,
+                pl.BlockSpec((1, tile, 1), lambda e, f, r, h: (e, r, 0)),
+            ],
+            out_specs=out_specs,
+        ),
+        out_shape=out_shape,
+        compiler_params=EXPERT_PARAMS,
+        cost_estimate=SMALL,
+        name="hidden",
+    )(half, rows, weights, weights, down, gates)
+
+
+def back_kernel(*refs, count, chunk):
+    a_refs, b_refs, out_ref, acc_ref = refs[:count], refs[count : 2 * count], refs[-2], refs[-1]
+    turn_at = pl.program_id(2)
+
+    def step(i, unused):
+        at = pl.ds(pl.multiple_of(i * chunk, chunk), chunk)
+        total = None
+        for a, b in zip(a_refs, b_refs):
+            term = lax.dot_general(a[0, at, :], b[0, 0], NT, preferred_element_type=F32)
+            total = term if total is None else total + term
+
+        @pl.when(turn_at == 0)
+        def first():
+            acc_ref[at, :] = total
+
+        @pl.when(turn_at > 0)
+        def later():
+            acc_ref[at, :] += total
+
+        return unused
+
+    lax.fori_loop(0, out_ref.shape[0] // chunk, step, 0)
+
+    @pl.when(turn_at == pl.num_programs(2) - 1)
+    def last():
+        out_ref[...] = acc_ref[...].astype(out_ref.dtype)
+
+
+def back_call(parts, weights, which, kind=BF16, *after):
+    experts, count, width = parts[0].shape
+    model_width = weights.shape[2]
+    tile, cols = math.gcd(count, 512), math.gcd(model_width, 2048)
+
+    def weight_spec(k):
+        return pl.BlockSpec((1, 1, cols, width), lambda d, r, e: (e, k, d, 0))
+
+    return pl.pallas_call(
+        functools.partial(back_kernel, count=len(parts), chunk=math.gcd(tile, 256)),
+        grid=(model_width // cols, count // tile, experts),
+        in_specs=[pl.BlockSpec((1, tile, width), lambda d, r, e: (e, r, 0))] * len(parts)
+        + [weight_spec(k) for k in which]
+        + [pl.BlockSpec(memory_space=pl.ANY)] * len(after),
+        out_specs=pl.BlockSpec((tile, cols), lambda d, r, e: (r, d)),
+        out_shape=jax.ShapeDtypeStruct((count, model_width), kind),
+        scratch_shapes=[pltpu.VMEM((tile, cols), F32)],
+        compiler_params=EXPERT_PARAMS,
+        cost_estimate=SMALL,
+        name="back",
+    )(*parts, *([weights] * len(parts)), *after)
+
+
+def grad_kernel(half_ref, own_rows, own_grads, near_rows, near_grads, out_ref):
+    total = lax.dot_general(own_rows[...], own_grads[0], TN, preferred_element_type=F32)
+    total += lax.dot_general(near_rows[...], near_grads[0], TN, preferred_element_type=F32)
+    out_ref[...] = total.astype(BF16)
+
+
+def grad_call(own_rows, own_grads, near_rows, near_grads, half):
+    count, model_width = own_rows.shape
+    experts, _, width = near_grads.shape
+    cols = math.gcd(model_width, 512)
+    row_spec = pl.BlockSpec((count, cols), lambda e, d, h: (0, d))
+    return pl.pallas_call(
+        grad_kernel,
+        grid_spec=pltpu.PrefetchScalarGridSpec(
+            num_scalar_prefetch=1,
+            grid=(experts, model_width // cols),
+            in_specs=[
+                row_spec,
+                pl.BlockSpec((1, count, width), lambda e, d, h: (e, 0, h[0])),
+                row_spec,
+                pl.BlockSpec((1, count, width), lambda e, d, h: (e, 0, 0)),
+            ],
+            out_specs=pl.BlockSpec((cols, width), lambda e, d, h: (d, e)),
+        ),
+        out_shape=jax.ShapeDtypeStruct((model_width, experts * width), BF16),
+        compiler_params=EXPERT_PARAMS,
+        cost_estimate=SMALL,
+        name="grad",
+    )(half, own_rows, own_grads, near_rows, near_grads)
+
+
+def scatter_rows(term):
+    count = lax.axis_size("ctx")
+    groups = [[i for i in range(count) if i % 2 == parity] for parity in range(2)]
+    return lax.psum_scatter(
+        term, "ctx", scatter_dimension=0, axis_index_groups=groups, tiled=True
+    )
+
+
+def swap_rows(term):
+    size = term.shape[0] // 2
+    odd = lax.axis_index("ctx") % 2
+    sent = flip(lax.dynamic_slice_in_dim(term, (1 - odd) * size, size, 0), "ctx", 1)
+    kept = lax.dynamic_slice_in_dim(term, odd * size, size, 0)
+    return sent, kept
 
 
 def body(
@@ -538,20 +885,24 @@
     def gather(values):
         return lax.all_gather(values, "exp", axis=0, tiled=False)
 
+    half = (ctx_place % 2).astype(jnp.int32).reshape(1)
+    whole = jnp.zeros((1,), jnp.int32)
     local_float = block_input.astype(F32).reshape(rows_dev, model_width)
     local_factor = rms_factor(local_float)
     local_unit = local_float * local_factor
     normed = gather((local_unit * attend_gain).astype(BF16)).reshape(rows_all, model_width)
-    all_routes = gather(jnp.transpose(routes, (1, 0, 2)).reshape(rows_dev, TOP))
-    all_routes = all_routes.reshape(rows_all, TOP)
-    grad_low = gather(cotangent.reshape(rows_dev, model_width)).reshape(rows_all, model_width)
+    weights = jnp.transpose(expert_weights, (1, 2, 0, 3))
+    w_qkv = jnp.concatenate([w_query, w_key, w_value], axis=1)
+    own_routes = jnp.transpose(routes, (1, 0, 2)).reshape(rows_dev, TOP)
+    own_grads = cotangent.reshape(rows_dev, model_width)
+    grad_low = gather(own_grads).reshape(rows_all, model_width)
     full_out = gather(w_out).reshape(exp_count * local_width, model_width)
-    w_qkv = jnp.concatenate([w_query, w_key, w_value], axis=1)
-    full_qkv = gather(w_qkv.T).reshape(exp_count * 3 * local_width, model_width)
-    w_gate, w_up, w_down = (
-        jnp.concatenate([expert_weights[:, e, k, :] for e in range(experts_here)], axis=1)
-        for k in range(3)
-    )
+    near_low = gather(hold(flip(own_grads, "ctx", 1), weights)).reshape(rows_all, model_width)
+    all_routes = gather(own_routes).reshape(rows_all, TOP)
+    near_routes = flip(all_routes, "ctx", 1)
+    w_qkv = hold(w_qkv, weights, near_routes)
+    grad_down = down_call(grad_low, weights, whole, hidden_units)
+    near_down = down_call(near_low, weights, half, hidden_units // 2)
 
     projected = dot32(normed, w_qkv).reshape(exp_count, seq_count, shard_len, 3 * local_width)
     row_ids = jnp.arange(ctx_rows, dtype=jnp.int32)
@@ -563,23 +914,13 @@
     forward, backward = (
         (paired_forward, paired_backward) if paired else (gathered_forward, gathered_backward)
     )
-    attended, kept = forward(
-        projected[..., :local_width],
-        projected[..., local_width : 2 * local_width],
-        projected[..., 2 * local_width :].astype(BF16),
-        query_gain,
-        key_gain,
-        cosine,
-        sines,
-        model_width,
+    (own_attended, attended), kept = forward(
+        projected, query_gain, key_gain, cosine, sines, model_width, grad_down
     )
 
     def exchange(values):
         return lax.all_to_all(values, "exp", split_axis=0, concat_axis=0, tiled=True)
 
-    sent = jnp.transpose(attended.reshape(pair_count, exp_count, shard_len, HD), (1, 0, 2, 3))
-    own = exchange(sent).reshape(exp_count, seq_count, local_heads, shard_len, HD)
-    own_attended = jnp.transpose(own, (1, 3, 0, 2, 4)).reshape(rows_dev, exp_count * local_width)
     hidden = local_float + dot32(own_attended, full_out)
     hidden_factor = rms_factor(hidden)
     unit_second = hidden * hidden_factor
@@ -591,55 +932,42 @@
         return jnp.any(table[:, :, None] == expert_ids[None, None, :], axis=1)
 
     own_prob = jax.nn.softmax(dot32(own_mixed, router), axis=-1)
-    own_routes = jnp.transpose(routes, (1, 0, 2)).reshape(rows_dev, TOP)
-    own_chosen = chosen(own_routes)
-
-    mixed = gather(own_mixed).reshape(rows_all, model_width)
-    all_prob = jax.nn.softmax(dot32(mixed, router), axis=-1)
-    all_gates = jnp.where(chosen(all_routes), all_prob, 0.0)
-    gates = lax.dynamic_slice_in_dim(all_gates, exp_place * experts_here, experts_here, 1)
-    gates = gates[:, :, None]
-
-    wide = (rows_all, experts_here, hidden_units)
-    grad_down = dot32(grad_low, w_down).reshape(wide)
-    pre_gate = dot32(mixed, w_gate).reshape(wide)
-    pre_up = dot32(mixed, w_up).reshape(wide)
-    sigmoid_vals = jax.nn.sigmoid(pre_gate)
-    activated = pre_gate * sigmoid_vals
-    middle = activated * pre_up
-    gate_grads = jnp.sum(middle * grad_down, axis=-1)
-    grad_middle = gates * grad_down
-    flat = (rows_all, experts_here * hidden_units)
-    gated_middle = (gates * middle).astype(BF16).reshape(flat)
-    grad_gate = grad_middle * pre_up * sigmoid_vals * (1.0 + pre_gate * (1.0 - sigmoid_vals))
-    grad_gate = grad_gate.astype(BF16).reshape(flat)
-    grad_up = (grad_middle * activated).astype(BF16).reshape(flat)
-
-    def weight_term(rows, grads):
-        term = jnp.einsum("rd,rf->df", rows, grads, preferred_element_type=F32).astype(BF16)
-        return lax.psum_scatter(term, "ctx", scatter_dimension=0, tiled=True)
-
-    down_term = weight_term(grad_low, gated_middle)
-    gate_term = weight_term(mixed, grad_gate)
-    up_term = weight_term(mixed, grad_up)
-    expert_grad = jnp.stack(
-        [
-            t.astype(F32).reshape(t.shape[0], experts_here, hidden_units)
-            for t in (gate_term, up_term, down_term)
-        ],
-        axis=2,
-    )
-
-    slot_rows = jnp.einsum("rf,df->rd", grad_gate, w_gate, preferred_element_type=F32)
-    slot_rows = slot_rows + jnp.einsum("rf,df->rd", grad_up, w_up, preferred_element_type=F32)
-    slot_sum = reduce_rows(slot_rows.astype(BF16).reshape(exp_count, rows_dev, model_width))
-    expert_out = jnp.einsum("rf,df->rd", gated_middle, w_down, preferred_element_type=F32)
-    mixture = reduce_rows(expert_out.astype(BF16).reshape(exp_count, rows_dev, model_width))
-    block_output = (hidden + mixture).astype(BF16).reshape(block_input.shape)
-
-    choice_grad = exchange(gate_grads.reshape(exp_count, rows_dev, experts_here))
-    choice_grad = jnp.transpose(choice_grad, (1, 0, 2)).reshape(rows_dev, experts_all)
-    choice_grad = jnp.where(own_chosen, choice_grad, 0.0)
+
+    def local_gates(rows, table):
+        prob = jax.nn.softmax(dot32(rows, router), axis=-1)
+        gates = jnp.where(chosen(table), prob, 0.0)
+        gates = lax.dynamic_slice_in_dim(gates, exp_place * experts_here, experts_here, 1)
+        return jnp.transpose(gates)[:, :, None]
+
+    if paired:
+        attended = return_pairs(hold(attended, own_mixed))
+    mixed = hold(gather(own_mixed).reshape(rows_all, model_width), near_down, attended)
+    near_mixed = gather(hold(flip(own_mixed, "ctx", 1), near_down))
+    gates = local_gates(mixed, all_routes)
+
+    gated_middle, grad_gate, grad_up, dots = hidden_call(
+        mixed, weights, grad_down, gates, whole, True
+    )
+    gate_grads = jnp.sum(dots, axis=(1, 3))
+    choice_grad = exchange(
+        jnp.transpose(gate_grads.reshape(experts_here, exp_count, rows_dev), (1, 0, 2))
+    )
+    near_mixed = hold(near_mixed.reshape(rows_all, model_width), gated_middle)
+    near_gates = local_gates(near_mixed, near_routes)
+    near_middle, near_grad_gate, near_grad_up = hidden_call(
+        near_mixed, weights, near_down, near_gates, half, False
+    )
+
+    down_term = grad_call(grad_low, gated_middle, near_low, near_middle, half)
+    slot_rows = back_call([grad_gate, grad_up], weights, (0, 1), BF16, down_term, choice_grad)
+    gate_term = grad_call(mixed, grad_gate, near_mixed, near_grad_gate, half)
+    up_term = grad_call(mixed, grad_up, near_mixed, near_grad_up, half)
+    down_sum, gate_sum, up_sum = (scatter_rows(t) for t in (down_term, gate_term, up_term))
+    slot_sum = reduce_rows(
+        slot_rows.reshape(exp_count, rows_dev, model_width), gate_term, up_term
+    )
+    choice_grad = jnp.transpose(choice_grad, (2, 0, 1)).reshape(rows_dev, experts_all)
+    choice_grad = jnp.where(chosen(own_routes), choice_grad, 0.0)
     logit_grad = (
         own_prob * (choice_grad - jnp.sum(own_prob * choice_grad, axis=-1, keepdims=True))
     ).astype(BF16)
@@ -656,54 +984,77 @@
         + grad_rows
     )
     own_branch = grad_hidden.astype(BF16)
+    early_part = jnp.concatenate([router_part, egain_part[:, None]], axis=1)
+    early_part = exchange(early_part.reshape(exp_count, -1, experts_all + 1))
+    branch_rows = gather(hold(own_branch, up_sum)).reshape(exp_count, seq_count, shard_len, model_width)
 
     grad_attended = jnp.einsum(
         "rd,hd->rh", own_branch, full_out, preferred_element_type=F32
     ).astype(BF16)
+    expert_out = back_call([gated_middle], weights, (2,), BF16, grad_attended)
     sent = grad_attended.reshape(seq_count, shard_len, exp_count, local_heads, HD)
     sent = jnp.transpose(sent, (2, 0, 3, 1, 4)).reshape(exp_count, pair_count, shard_len, HD)
     grads = jnp.transpose(exchange(sent), (1, 0, 2, 3)).reshape(pair_count, ctx_rows, HD)
-    grad_qkv, qgain_part, kgain_part = backward(
-        kept, grads, query_gain, key_gain, cosine, sines, model_width
-    )
-    own_qkv = exchange(grad_qkv.reshape(exp_count, rows_dev, 3 * local_width))
-    own_qkv = jnp.transpose(own_qkv, (1, 0, 2)).reshape(rows_dev, exp_count * 3 * local_width)
-    grad_normed = dot32(own_qkv, full_qkv)
+    swapped = [swap_rows(term) for term in (gate_sum, hold(up_sum, grads), down_sum)]
+    grad_qkv, qgain_part, kgain_part, ended = backward(
+        kept, grads, query_gain, key_gain, cosine, sines, model_width, (expert_out, swapped[2][0]), (swapped[0][0], swapped[1][0])
+    )
+    attended_rows = attended.reshape(seq_count, local_heads, exp_count, shard_len, HD)
+    branch_rows = hold(branch_rows, ended)
+    outw_part = jnp.einsum(
+        "shetc,estd->hcd", attended_rows, branch_rows, preferred_element_type=F32
+    ).reshape(local_width, model_width)
+    qkv_part = jnp.einsum(
+        "rd,rh->dh", normed, grad_qkv.reshape(rows_all, -1), preferred_element_type=F32
+    )
+    qkv_part, outw_part = qkv_part.astype(BF16), outw_part.astype(BF16)
+    qkv_grad, out_grad = lax.psum((qkv_part, outw_part), "ctx")
+
+    w_qkv = jnp.concatenate([w_query, w_key, w_value], axis=1)
+    grad_rows_qkv = grad_qkv.reshape(1, rows_all, -1)
+    normed_back = back_call(
+        [grad_rows_qkv], w_qkv[None, None], (0,), BF16, qkv_part, outw_part
+    )
+    grad_normed = reduce_rows(normed_back.reshape(exp_count, rows_dev, model_width))
     attend_part = jnp.sum(grad_normed * local_unit, axis=0)
     lunit_grad = grad_normed * attend_gain
     input_grad = grad_hidden + local_factor * (
         lunit_grad - local_unit * jnp.mean(lunit_grad * local_unit, axis=-1, keepdims=True)
     )
-
-    branch_rows = gather(own_branch).reshape(exp_count, seq_count, shard_len, model_width)
-    attended_rows = attended.reshape(seq_count, local_heads, exp_count, shard_len, HD)
-    outw_part = jnp.einsum(
-        "shetc,estd->hcd", attended_rows, branch_rows, preferred_element_type=F32
-    ).reshape(local_width, model_width)
-    out_grad = lax.psum(outw_part.astype(BF16), "ctx").astype(F32)
-    qkv_part = jnp.einsum(
-        "rd,rh->dh", normed, grad_qkv.reshape(rows_all, -1), preferred_element_type=F32
-    )
-    qkv_grad = lax.psum(qkv_part.astype(BF16), "ctx").astype(F32)
-    attend_sum, egain_sum, router_sum = (
-        lax.psum_scatter(part, "exp", scatter_dimension=0, tiled=True)
-        for part in (attend_part, egain_part, router_part)
-    )
-    attend_sum, egain_sum, router_sum, qgain_grad, kgain_grad = lax.psum(
-        (attend_sum, egain_sum, router_sum, qgain_part, kgain_part), "ctx"
-    )
+    halves = []
+    even = ctx_place % 2 == 0
+    for sent_rows, kept_rows in swapped:
+        sent_rows = hold(sent_rows, grad_normed)
+        lower = jnp.where(even, kept_rows, sent_rows)
+        upper = jnp.where(even, sent_rows, kept_rows)
+        parts = [
+            v.astype(F32).reshape(-1, experts_here, hidden_units // 2) for v in (lower, upper)
+        ]
+        halves.append(jnp.concatenate(parts, axis=-1))
+    expert_grad = jnp.stack(halves, axis=2)
+    expert_out = hold(expert_out, normed_back)
+    mixture = reduce_rows(expert_out.reshape(exp_count, rows_dev, model_width), grad_normed)
+    block_output = (hidden + mixture).astype(BF16).reshape(block_input.shape)
+
+    attend_sum = jnp.sum(exchange(attend_part.reshape(exp_count, -1)), axis=0)
+    early_sum = jnp.sum(hold(early_part, grad_qkv), axis=0)
+    late = [v[:, None] for v in (attend_sum, qgain_part, kgain_part)]
+    sums = butterfly_sum(jnp.concatenate([early_sum] + late, axis=1), "ctx")
+    last = (sums, input_grad, block_output, expert_grad)
+    qkv_grad = hold(qkv_grad, *last).astype(F32)
+    out_grad = hold(out_grad, *last).astype(F32)
     return (
         block_output,
         input_grad.reshape(block_input.shape),
-        attend_sum,
+        sums[:, experts_all + 1],
         qkv_grad[:, :local_width],
         qkv_grad[:, local_width : 2 * local_width],
         qkv_grad[:, 2 * local_width :],
         out_grad,
-        qgain_grad,
-        kgain_grad,
-        egain_sum,
-        router_sum,
+        sums[:, experts_all + 2],
+        sums[:, experts_all + 3],
+        sums[:, experts_all],
+        sums[:, :experts_all],
         expert_grad,
     )
 

time: 1430 us -> 1110 us (0.78)
  Pallas kernels: 62.9 us -> 364 us
  matrix products: 288 us -> 53.3 us
  waiting for transfers between devices: 545 us -> 325 us
  blocking collectives: 123 us -> 38.4 us
  local copies, waits for them, and re-layouts: 231 us -> 153 us
    pallas_call x1 -> x41, Pallas kernels: 34.9 us -> 336 us  [the longest x3 88.9 us: back_call(): pl.pallas_call(functools.partial(back_kernel, count=len(parts), chunk=mat...]
    psum x1, waiting for transfers between devices: 144 us -> 0.01 us  [body(): qkv_grad, out_grad = lax.psum((qkv_part, outw_part), 'ctx')]
    dot_general x6 -> x0, matrix products: 141 us -> none  [the longest x3 71.6 us: weight_term(): jnp.einsum('rd,rf->df', rows, grads, preferred_element_type=F32)]
    reduce_scatter x4 -> x3, waiting for transfers between devices: 107 us -> 5.85 us  [scatter_rows(): lax.psum_scatter(term, 'ctx', scatter_dimension=0, axis_index_groups=grou...]
    dot_general x8 -> x5, matrix products: 123 us -> 28.1 us  [dot32(): return jnp.dot(a, b, preferred_element_type=F32)]
    ppermute x29 -> x44, waiting for transfers between devices: 198 us -> 274 us  [flip(): lax.ppermute(values, axis, [(i, i ^ mask) for i in range(lax.axis_size(ax...]
    unnamed x126 -> x138, local copies, waits for them, and re-layouts: 15.1 us -> 69 us
    psum x1 -> x0, blocking collectives: 49.9 us -> none  [body(): lax.psum((attend_sum, egain_sum, router_sum, qgain_part, kgain_part), 'ctx')]
  transfers between devices with their start and end apart: 42 -> 59, of which waited for: 16 -> 26; matrix products, arithmetic and copies ran while one was open for 41% -> 22% of each run, Pallas kernels for 4% -> 27%
where the time goes in v2:
time: 1110 us
  Pallas kernels  364 us (33%)
  waiting for transfers between devices  325 us (29%)
  local copies, waits for them, and re-layouts  153 us (14%)
  other arithmetic  92.9 us (8%)
  starting transfers between devices  67.7 us (6%)
  matrix products  53.3 us (5%)
  blocking collectives  38.4 us (3%)
  between operations  15.3 us (1%)
    ppermute x44, waiting for transfers between devices, flip(): lax.ppermute(values, axis, [(i, i ^ mask) for i in range(lax.axis_size(ax...  274 us
    pallas_call x3, Pallas kernels, back_call(): pl.pallas_call(functools.partial(back_kernel, count=len(parts), chunk=mat...  88.9 us
    pallas_call x2, Pallas kernels, hidden_call(): pl.pallas_call(functools.partial(hidden_kernel, chunk=math.gcd(tile, 256)...  80 us
    pallas_call x3, Pallas kernels, grad_call(): pl.pallas_call(grad_kernel, grid_spec=pltpu.PrefetchScalarGridSpec(num_sc...  75.7 us
    unnamed x138, local copies, waits for them, and re-layouts  69 us
    ppermute x44, starting transfers between devices, flip(): lax.ppermute(values, axis, [(i, i ^ mask) for i in range(lax.axis_size(ax...  53.4 us
    pallas_call x2, Pallas kernels, down_call(): pl.pallas_call(down_kernel, grid_spec=pltpu.PrefetchScalarGridSpec(num_sc...  40.2 us
    pallas_call x1, Pallas kernels, attend_back_call(): pl.pallas_call(attend_back_kernel, out_shape=(jax.ShapeDtypeStruct((ctx_c...  36.2 us
  transfers between devices with their start and end apart: 59, of which 26 were waited for; matrix products, arithmetic and copies ran while one was open for 22% of the time, Pallas kernels for 27%

profile of v2, /device:TPU:0, one launch (start us, length us, event | category | flops | bytes accessed | tf_op | source)
XLA Modules:
  0.0 1109.0 jit_solution(6503790937222299361)
XLA Ops:
  16.2 24.5 %copy.306 = bf16[2048,2,3,1024]{3,0,2,1:T(8,128)(2,1)} copy(bf16[2048,2,3,1024]{3,1,2,0:T(2,128)(2,1)} %param.23) | data formatting | bytes 50331648 | tf_op args[10]
  42.3 9.2 all_gather.41
  60.8 8.3 all-gather.13.cloned.1.call-done
  69.0 10.0 fusion.3.proj_ref
  97.1 7.2 rotate.1
  115.4 10.3 all-gather.15.cloned.1.call-done
  125.7 24.4 %down.2.refs_1_.down_ref = f32[2,2048,1024]{2,1,0:T(8,128)} custom-call(s32[1]{0:T(128)} %constant.254.clone.1.half_ref, bf16[2048,2048]{1,0:T(8,128)(2,1)} %bitcast.297, bf16[2,3,2048,1024]{3,2,1,0:T(8,128)(2,1)} %bitcast.279), custom_call_target="tpu_custom_call" | custom-call | tf_op jit(solution)/shard_map/down/pallas_call | solution.py:669
  150.1 17.1 %collective-permute-done.8 = bf16[1024,128]{1,0:T(8,128)(2,1)} collective-permute-done((bf16[1024,128]{1,0:T(8,128)(2,1)S(1)}, bf16[1024,128]{1,0:T(8,128)(2,1)}, u32[]{:S(2)}, u32[]{:S(2)}) %collective-permute-start.8) | collective-permute-done | bytes 262176 | tf_op jit(solution)/shard_map/ppermute | solution.py:51
  172.2 27.8 %attend.1 = (bf16[4,1024,128]{2,1,0:T(8,128)(2,1)S(1)}, f32[128,4096]{1,0:T(8,128)}, f32[8,1,512]{2,1,0:T(1,128)S(1)}) custom-call(s32[1]{0:T(128)} %bitcast.1.place_ref, bf16[4,2,1024,128]{3,2,1,0:T(8,128)(2,1)} %hold.29.qk_ref, bf16[4,1024,128]{2,1,0:T(8,128)(2,1)S(1)} %pad_maximum_fusion.2.v_ref), custom_call_target="tpu_custom_call" | custom-call | tf_op jit(solution)/shard_map/attend/pallas_call | solution.py:249
  200.3 29.2 %all_to_all.29 = bf16[32,128,128]{2,1,0:T(8,128)(2,1)S(1)} all-to-all(bf16[32,128,128]{2,1,0:T(8,128)(2,1)S(1)} %bitcast.324), channel_id=1, replica_groups=mesh['ctx'=4,'exp'=8] {'ctx','exp'}, dimensions={0} | all-to-all | bytes 2097152 | tf_op jit(solution)/shard_map/all_to_all | solution.py:435
  234.1 6.3 multiply_reduce_fusion.4
  247.7 15.8 %down.3.refs_1_.down_ref = f32[2,2048,512]{2,1,0:T(8,128)} custom-call(s32[1]{0:T(128)} %bitcast.37.half_ref, bf16[2048,2048]{1,0:T(8,128)(2,1)} %all-gather.21.cloned.1.call-done.rows_ref.near_rows, bf16[2,3,2048,1024]{3,2,1,0:T(8,128)(2,1)} %bitcast.280), custom_call_target="tpu_custom_call" | custom-call | tf_op jit(solution)/shard_map/down/pallas_call | solution.py:669
  274.7 6.5 collective-permute-done.13
  281.2 14.3 %collective-permute-done.12 = bf16[1024,128]{1,0:T(8,128)(2,1)S(1)} collective-permute-done((bf16[1024,128]{1,0:T(8,128)(2,1)S(1)}, bf16[1024,128]{1,0:T(8,128)(2,1)S(1)}, u32[]{:S(2)}, u32[]{:S(2)}) %collective-permute-start.12) | collective-permute-done | bytes 262176 | tf_op jit(solution)/shard_map/ppermute | solution.py:51
  296.9 7.0 all-gather.19.cloned.1.call-done.refs_0_
  303.9 5.7 fusion.43
  311.6 52.2 %hidden.2 = (bf16[2,2048,1024]{2,1,0:T(8,128)(2,1)}, bf16[2,2048,1024]{2,1,0:T(8,128)(2,1)}, bf16[2,2048,1024]{2,1,0:T(8,128)(2,1)}, f32[2,2,2048,128]{3,2,1,0:T(8,128)}) custom-call(s32[1]{0:T(128)} %constant.254.clone.1.half_ref, bf16[2048,2048]{1,0:T(8,128)(2,1)} %hold.32.rows_ref.own_rows, bf16[2,3,2048,1024]{3,2,1,0:T(8,128)(2,1)} %bitcast.281, ...), custom_call_target="tpu_custom_call" | custom-call | tf_op jit(solution)/shard_map/hidden/pallas_call | solution.py:736
  363.8 5.7 fusion.45
  371.6 27.7 %hidden.3 = (bf16[2,2048,512]{2,1,0:T(8,128)(2,1)}, bf16[2,2048,512]{2,1,0:T(8,128)(2,1)}, bf16[2,2048,512]{2,1,0:T(8,128)(2,1)}) custom-call(s32[1]{0:T(128)} %bitcast.37.half_ref, bf16[2048,2048]{1,0:T(8,128)(2,1)} %hold.34.rows_ref.near_rows, bf16[2,3,2048,1024]{3,2,1,0:T(8,128)(2,1)} %bitcast.283, bf16[2,3,2048,1024]{3,2,1,0:T(8,128)(2,1)} %bitcast.284, ...), custom_call_target="tpu_custom_call" | custom-call | tf_op jit(solution)/shard_map/hidden/pallas_call | solution.py:736
  399.3 24.9 %grad.5.refs_2_ = bf16[2048,1024]{1,0:T(8,128)(2,1)} custom-call(s32[1]{0:T(128)} %bitcast.37.half_ref, bf16[2048,2048]{1,0:T(8,128)(2,1)} %hold.32.rows_ref.own_rows, bf16[2,2048,1024]{2,1,0:T(8,128)(2,1)} %get-tuple-element.29.refs_1_.own_grads, bf16[2048,2048]{1,0:T(8,128)(2,1)} %hold.34.rows_ref.near_rows, bf16[2,2048,512]{2,1,0:T(8,128)(2,1)} %get-tuple-element.33.near_grads), custom_call_target="tpu_custom_call" | custom-call | tf_op jit(solution)/shard_map/grad/pallas_call | solution.py:819
  424.3 25.3 %grad.3.refs_4_ = bf16[2048,1024]{1,0:T(8,128)(2,1)} custom-call(s32[1]{0:T(128)} %bitcast.37.half_ref, bf16[2048,2048]{1,0:T(8,128)(2,1)} %bitcast.298, bf16[2,2048,1024]{2,1,0:T(8,128)(2,1)} %get-tuple-element.27.refs_1_.own_grads.refs_0_, bf16[2048,2048]{1,0:T(8,128)(2,1)} %all-gather.21.cloned.1.call-done.rows_ref.near_rows, ...), custom_call_target="tpu_custom_call" | custom-call | tf_op jit(solution)/shard_map/grad/pallas_call | solution.py:819
  456.5 25.5 %grad.4.refs_1_ = bf16[2048,1024]{1,0:T(8,128)(2,1)} custom-call(s32[1]{0:T(128)} %bitcast.37.half_ref, bf16[2048,2048]{1,0:T(8,128)(2,1)} %hold.32.rows_ref.own_rows, bf16[2,2048,1024]{2,1,0:T(8,128)(2,1)} %get-tuple-element.28.refs_0_.own_grads, bf16[2048,2048]{1,0:T(8,128)(2,1)} %hold.34.rows_ref.near_rows, bf16[2,2048,512]{2,1,0:T(8,128)(2,1)} %get-tuple-element.32.near_grads), custom_call_target="tpu_custom_call" | custom-call | tf_op jit(solution)/shard_map/grad/pallas_call | solution.py:819
  482.7 47.2 %back.3 = bf16[2048,2048]{1,0:T(8,128)(2,1)} custom-call(bf16[2,2048,1024]{2,1,0:T(8,128)(2,1)} %get-tuple-element.28.refs_0_.own_grads, bf16[2,2048,1024]{2,1,0:T(8,128)(2,1)} %get-tuple-element.29.refs_1_.own_grads, bf16[2,3,2048,1024]{3,2,1,0:T(8,128)(2,1)} %bitcast.285, bf16[2,3,2048,1024]{3,2,1,0:T(8,128)(2,1)} %bitcast.286, ...), custom_call_target="tpu_custom_call" | custom-call | tf_op jit(solution)/shard_map/back/pallas_call | solution.py:793
  534.8 7.3 collective-permute-done.15
  555.2 21.3 %collective-permute-done.18.refs_0_ = bf16[256,2048]{1,0:T(8,128)(2,1)S(1)} collective-permute-done((bf16[256,2048]{1,0:T(8,128)(2,1)}, bf16[256,2048]{1,0:T(8,128)(2,1)S(1)}, u32[]{:S(2)}, u32[]{:S(2)}) %collective-permute-start.18) | collective-permute-done | bytes 1048608 | tf_op jit(solution)/shard_map/ppermute | solution.py:51
  577.5 20.7 %collective-permute-done.17.refs_0_ = bf16[256,2048]{1,0:T(8,128)(2,1)S(1)} collective-permute-done((bf16[256,2048]{1,0:T(8,128)(2,1)}, bf16[256,2048]{1,0:T(8,128)(2,1)S(1)}, u32[]{:S(2)}, u32[]{:S(2)}) %collective-permute-start.17) | collective-permute-done | bytes 1048608 | tf_op jit(solution)/shard_map/ppermute | solution.py:51
  608.3 5.8 convolution_convert_fusion.1.refs_2_
  620.7 5.8 reduce-scatter.4.cloned.1.call-done
  628.8 7.2 all-to-all-done.2
  642.9 29.2 %back.4.refs_1_.refs_0_ = bf16[2048,2048]{1,0:T(8,128)(2,1)} custom-call(bf16[2,2048,1024]{2,1,0:T(8,128)(2,1)} %get-tuple-element.27.refs_1_.own_grads.refs_0_, bf16[2,3,2048,1024]{3,2,1,0:T(8,128)(2,1)} %bitcast.287, bf16[256,2048]{1,0:T(8,128)(2,1)} %copy-done.31), custom_call_target="tpu_custom_call" | custom-call | tf_op jit(solution)/shard_map/back/pallas_call | solution.py:793
  672.1 10.4 collective-permute-done.21
  682.5 24.6 %collective-permute-done.20 = bf16[1024,128]{1,0:T(8,128)(2,1)S(1)} collective-permute-done((bf16[1024,128]{1,0:T(8,128)(2,1)S(1)}, bf16[1024,128]{1,0:T(8,128)(2,1)S(1)}, u32[]{:S(2)}, u32[]{:S(2)}) %collective-permute-start.20) | collective-permute-done | bytes 262176 | tf_op jit(solution)/shard_map/ppermute | solution.py:51
  710.5 36.2 %attend_back.1 = (bf16[4,3,1024,128]{3,2,1,0:T(8,128)(2,1)}, f32[4,4,512]{2,1,0:T(4,128)S(1)}) custom-call(s32[1]{0:T(128)} %bitcast.1.place_ref, bf16[4,2,1024,128]{3,2,1,0:T(8,128)(2,1)} %hold.29.qk_ref, bf16[4,1024,128]{2,1,0:T(8,128)(2,1)S(1)} %pad_maximum_fusion.2.v_ref, bf16[4,1024,128]{2,1,0:T(8,128)(2,1)S(1)} %copy-done.3, ...), custom_call_target="tpu_custom_call" | custom-call | tf_op jit(solution)/shard_map/attend_back/pallas_call | solution.py:269
  775.7 24.0 %collective-permute-done.31 = bf16[3,1024,128]{2,1,0:T(8,128)(2,1)} collective-permute-done((bf16[3,1024,128]{2,1,0:T(8,128)(2,1)}, bf16[3,1024,128]{2,1,0:T(8,128)(2,1)}, u32[]{:S(2)}, u32[]{:S(2)}) %collective-permute-start.31) | collective-permute-done | bytes 786464 | tf_op jit(solution)/shard_map/ppermute | solution.py:51
  799.7 33.2 %collective-permute-done.30 = bf16[3,1024,128]{2,1,0:T(8,128)(2,1)} collective-permute-done((bf16[3,1024,128]{2,1,0:T(8,128)(2,1)}, bf16[3,1024,128]{2,1,0:T(8,128)(2,1)}, u32[]{:S(2)}, u32[]{:S(2)}) %collective-permute-start.30) | collective-permute-done | bytes 786464 | tf_op jit(solution)/shard_map/ppermute | solution.py:51
  836.2 18.1 %collective-permute-done.33.refs_2_.refs_0_ = bf16[512,1024]{1,0:T(8,128)(2,1)} collective-permute-done((bf16[512,1024]{1,0:T(8,128)(2,1)}, bf16[512,1024]{1,0:T(8,128)(2,1)}, u32[]{:S(2)}, u32[]{:S(2)}) %collective-permute-start.33) | collective-permute-done | bytes 1048608 | tf_op jit(solution)/shard_map/ppermute | solution.py:51
  854.3 7.6 norm_back.1
  861.9 11.4 %convolution_convert_fusion.refs_2_ = bf16[2048,768]{1,0:T(8,128)(2,1)} fusion(bf16[2048,2048]{1,0:T(8,128)(2,1)} %bitcast.362, bf16[2048,768]{1,0:T(8,128)(2,1)} %bitcast.301), kind=kOutput, calls=%fused_computation.11 | convolution fusion | flops 6444023808 | bytes 14680064 | tf_op jit(solution)/shard_map/rd,rh->dh/dot_general | solution.py:1007
  874.5 6.0 fusion.5.refs_3_
  880.5 12.5 %back.5.refs_1_ = bf16[2048,2048]{1,0:T(8,128)(2,1)} custom-call(bf16[1,2048,768]{2,1,0:T(8,128)(2,1)} %bitcast.302, bf16[1,1,2048,768]{3,2,1,0:T(8,128)(2,1)} %bitcast.300, bf16[2048,768]{1,0:T(8,128)(2,1)} %convolution_convert_fusion.refs_2_, bf16[256,2048]{1,0:T(8,128)(2,1)} %fusion.5.refs_3_), custom_call_target="tpu_custom_call" | custom-call | tf_op jit(solution)/shard_map/back/pallas_call | solution.py:793
  907.7 6.1 all-to-all-done.3
  937.2 12.2 %collective-permute-done.39.refs_0_ = bf16[256,2048]{1,0:T(8,128)(2,1)S(1)} collective-permute-done((bf16[256,2048]{1,0:T(8,128)(2,1)}, bf16[256,2048]{1,0:T(8,128)(2,1)S(1)}, u32[]{:S(2)}, u32[]{:S(2)}) %collective-permute-start.39) | collective-permute-done | bytes 1048608 | tf_op jit(solution)/shard_map/ppermute | solution.py:51
  951.0 40.8 %collective-permute-done.38.refs_0_ = bf16[256,2048]{1,0:T(8,128)(2,1)} collective-permute-done((bf16[256,2048]{1,0:T(8,128)(2,1)}, bf16[256,2048]{1,0:T(8,128)(2,1)}, u32[]{:S(2)}, u32[]{:S(2)}) %collective-permute-start.38) | collective-permute-done | bytes 1048608 | tf_op jit(solution)/shard_map/ppermute | solution.py:51
  1020.6 7.6 copy.279
  1028.1 17.7 %maximum_convert_fusion.refs_4_ = f32[512,2,3,1024]{3,2,1,0:T(4,128)} fusion(bf16[512,2,1,1024]{3,2,1,0:T(2,128)(2,1)S(1)} %copy-done.15, bf16[512,2,1,1024]{3,2,1,0:T(2,128)(2,1)S(1)} %copy-done.16, bf16[512,2,1,1024]{3,2,1,0:T(2,128)(2,1)} %copy.279), kind=kLoop, calls=%fused_computation.1 | loop fusion | flops 18874368 | bytes 18874368 | tf_op jit(solution)/shard_map/stack | solution.py:1034
  1049.6 15.4 %collective-permute-done.42 = f32[256,20]{1,0:T(8,128)} collective-permute-done((f32[256,20]{1,0:T(8,128)}, f32[256,20]{1,0:T(8,128)}, u32[]{:S(2)}, u32[]{:S(2)}) %collective-permute-start.42) | collective-permute-done | bytes 20512 | tf_op jit(solution)/shard_map/ppermute | solution.py:51
  1066.3 6.4 multiply_add_fusion
  1076.3 16.7 %copy.283 = f32[512,2,3,1024]{3,1,2,0:T(2,128)} copy(f32[512,2,3,1024]{3,2,1,0:T(4,128)S(1)} %copy-done.4) | data formatting | bytes 25165824
  (395 shorter events, 257.4 us)
Async XLA Ops:
  7.2 61.8 %all-gather.13.cloned.1.call-start = ((), (), s32[]{:S(2)}) async-start(), calls=%async_computation.8 | async-start | bytes 9437184 | tf_op jit(solution)/shard_map/all_gather | solution.py:886
  11.5 114.2 %all-gather.15.cloned.1.call-start = ((), (), s32[]{:S(2)}) async-start(), calls=%async_computation.9 | async-start | bytes 9437184 | tf_op jit(solution)/shard_map/all_gather | solution.py:886
  12.3 221.8 %all-gather.17.cloned.1.call-start = ((), (), s32[]{:S(2)}) async-start(), calls=%async_computation.13 | async-start | bytes 9437184 | tf_op jit(solution)/shard_map/all_gather | solution.py:886
  13.0 234.7 %all-gather.21.cloned.1.call-start = ((), (), s32[]{:S(2)}) async-start(), calls=%async_computation.15 | async-start | bytes 9437184 | tf_op jit(solution)/shard_map/all_gather | solution.py:886
  13.1 27.6 %collective-permute-start.10 = (bf16[256,2048]{1,0:T(8,128)(2,1)S(1)}, bf16[256,2048]{1,0:T(8,128)(2,1)S(1)}, u32[]{:S(2)}, u32[]{:S(2)}) collective-permute-start(bf16[256,2048]{1,0:T(8,128)(2,1)S(1)} %bitcast.307), channel_id=1, source_target_pairs={{0,8},{8,0},{16,24},{24,16},{1,9},{9,1},{17,25},{25,17},{2,10},{10... | collective-permute-start | bytes 3145736 | tf_op jit(solution)/shard_map/ppermute | solution.py:51
  41.6 262.2 %all-gather.19.cloned.1.call-start = ((), (), s32[]{:S(2)}) async-start(), calls=%async_computation.14 | async-start | bytes 9437184 | tf_op jit(solution)/shard_map/all_gather | solution.py:886
  91.0 22.4 %collective-permute-start.9 = (bf16[1024,128]{1,0:T(8,128)(2,1)S(1)}, bf16[1024,128]{1,0:T(8,128)(2,1)S(1)}, u32[]{:S(2)}, u32[]{:S(2)}) collective-permute-start(bf16[1024,128]{1,0:T(8,128)(2,1)S(1)} %get-tuple-element.199), channel_id=1, source_target_pairs={{0,24},{8,16},{16,8},{24,0},{1,25},{9,17},{17,9},{25,1},{2,26},{10... | collective-permute-start | bytes 786440 | tf_op jit(solution)/shard_map/ppermute | solution.py:51
  107.2 61.9 %collective-permute-start.6 = (bf16[2,1024,128]{2,1,0:T(8,128)(2,1)}, bf16[2,1024,128]{2,1,0:T(8,128)(2,1)}, u32[]{:S(2)}, u32[]{:S(2)}) collective-permute-start(bf16[2,1024,128]{2,1,0:T(8,128)(2,1)} %get-tuple-element.179), channel_id=1, source_target_pairs={{0,24},{8,16},{16,8},{24,0},{1,25},{9,17},{17,9},{25,1},{2,26},{10... | collective-permute-start | bytes 1572872 | tf_op jit(solution)/shard_map/ppermute | solution.py:51
  110.4 58.7 %collective-permute-start.5 = (bf16[2,1024,128]{2,1,0:T(8,128)(2,1)}, bf16[2,1024,128]{2,1,0:T(8,128)(2,1)}, u32[]{:S(2)}, u32[]{:S(2)}) collective-permute-start(bf16[2,1024,128]{2,1,0:T(8,128)(2,1)} %get-tuple-element.180), channel_id=1, source_target_pairs={{0,16},{8,24},{16,0},{24,8},{1,17},{9,25},{17,1},{25,9},{2,18},{10... | collective-permute-start | bytes 1572872 | tf_op jit(solution)/shard_map/ppermute | solution.py:51
  110.4 58.7 %collective-permute-start.4 = (bf16[2,1024,128]{2,1,0:T(8,128)(2,1)}, bf16[2,1024,128]{2,1,0:T(8,128)(2,1)}, u32[]{:S(2)}, u32[]{:S(2)}) collective-permute-start(bf16[2,1024,128]{2,1,0:T(8,128)(2,1)} %get-tuple-element.181), channel_id=1, source_target_pairs={{0,8},{8,0},{16,24},{24,16},{1,9},{9,1},{17,25},{25,17},{2,10},{10... | collective-permute-start | bytes 1572872 | tf_op jit(solution)/shard_map/ppermute | solution.py:51
  111.6 55.6 %collective-permute-start.8 = (bf16[1024,128]{1,0:T(8,128)(2,1)S(1)}, bf16[1024,128]{1,0:T(8,128)(2,1)}, u32[]{:S(2)}, u32[]{:S(2)}) collective-permute-start(bf16[1024,128]{1,0:T(8,128)(2,1)S(1)} %get-tuple-element.200), channel_id=1, source_target_pairs={{0,16},{8,24},{16,0},{24,8},{1,17},{9,25},{17,1},{25,9},{2,18},{10... | collective-permute-start | bytes 786440 | tf_op jit(solution)/shard_map/ppermute | solution.py:51
  113.4 53.8 %collective-permute-start.7 = (bf16[1024,128]{1,0:T(8,128)(2,1)S(1)}, bf16[1024,128]{1,0:T(8,128)(2,1)S(1)}, u32[]{:S(2)}, u32[]{:S(2)}) collective-permute-start(bf16[1024,128]{1,0:T(8,128)(2,1)S(1)} %get-tuple-element.201), channel_id=1, source_target_pairs={{0,8},{8,0},{16,24},{24,16},{1,9},{9,1},{17,25},{25,17},{2,10},{10... | collective-permute-start | bytes 786440 | tf_op jit(solution)/shard_map/ppermute | solution.py:51
  243.0 120.9 %all-gather.23.cloned.1.call-start = ((), (), s32[]{:S(2)}) async-start(), calls=%async_computation.16 | async-start | bytes 9437184 | tf_op jit(solution)/shard_map/all_gather | solution.py:886
  243.0 24.7 %collective-permute-start.14 = (bf16[256,2048]{1,0:T(8,128)(2,1)}, bf16[256,2048]{1,0:T(8,128)(2,1)S(1)}, u32[]{:S(2)}, u32[]{:S(2)}) collective-permute-start(bf16[256,2048]{1,0:T(8,128)(2,1)} %multiply_convert_fusion.refs_1_), channel_id=1, source_target_pairs={{0,8},{8,0},{16,24},{24,16},{1,9},{9,1},{17,25},{25,17},{2,10},{10... | collective-permute-start | bytes 3145736 | tf_op jit(solution)/shard_map/ppermute | solution.py:51
  268.7 345.5 %reduce-scatter.8.cloned.1.call-start = ((), (), s32[]{:S(2)}) async-start(), calls=%async_computation.12 | async-start | bytes 6291456 | tf_op jit(solution)/shard_map/reduce_scatter | solution.py:842
  270.0 11.2 %collective-permute-start.13 = (bf16[1024,128]{1,0:T(8,128)(2,1)S(1)}, bf16[1024,128]{1,0:T(8,128)(2,1)S(1)}, u32[]{:S(2)}, u32[]{:S(2)}) collective-permute-start(bf16[1024,128]{1,0:T(8,128)(2,1)S(1)} %get-tuple-element.191), channel_id=1, source_target_pairs={{0,24},{8,16},{16,8},{24,0},{1,25},{9,17},{17,9},{25,1},{2,26},{10... | collective-permute-start | bytes 786440 | tf_op jit(solution)/shard_map/ppermute | solution.py:51
  272.0 23.6 %collective-permute-start.12 = (bf16[1024,128]{1,0:T(8,128)(2,1)S(1)}, bf16[1024,128]{1,0:T(8,128)(2,1)S(1)}, u32[]{:S(2)}, u32[]{:S(2)}) collective-permute-start(bf16[1024,128]{1,0:T(8,128)(2,1)S(1)} %get-tuple-element.192), channel_id=1, source_target_pairs={{0,16},{8,24},{16,0},{24,8},{1,17},{9,25},{17,1},{25,9},{2,18},{10... | collective-permute-start | bytes 786440 | tf_op jit(solution)/shard_map/ppermute | solution.py:51
  273.2 22.4 %collective-permute-start.11 = (bf16[1024,128]{1,0:T(8,128)(2,1)S(1)}, bf16[1024,128]{1,0:T(8,128)(2,1)S(1)}, u32[]{:S(2)}, u32[]{:S(2)}) collective-permute-start(bf16[1024,128]{1,0:T(8,128)(2,1)S(1)} %get-tuple-element.193), channel_id=1, source_target_pairs={{0,8},{8,0},{16,24},{24,16},{1,9},{9,1},{17,25},{25,17},{2,10},{10... | collective-permute-start | bytes 786440 | tf_op jit(solution)/shard_map/ppermute | solution.py:51
  424.2 202.3 %reduce-scatter.4.cloned.1.call-start = ((), (), s32[]{:S(2)}) async-start(), calls=%async_computation.10 | async-start | bytes 6291456 | tf_op jit(solution)/shard_map/reduce_scatter | solution.py:842
  453.0 29.0 %all-to-all-start.1 = ((f32[8,2,256]{2,1,0:T(2,128)}), f32[8,2,256]{2,1,0:T(2,128)S(1)}, u32[]{:S(2)}, u32[]{:S(2)}) async-start(f32[8,2,256]{2,1,0:T(2,128)} %bitcast.50), calls=%async_computation.1 | async-start | bytes 32768 | tf_op jit(solution)/shard_map/all_to_all | solution.py:922
  456.4 296.4 %reduce-scatter.6.cloned.1.call-start = ((), (), s32[]{:S(2)}) async-start(), calls=%async_computation.11 | async-start | bytes 6291456 | tf_op jit(solution)/shard_map/reduce_scatter | solution.py:842
  549.4 27.2 %collective-permute-start.18 = (bf16[256,2048]{1,0:T(8,128)(2,1)}, bf16[256,2048]{1,0:T(8,128)(2,1)S(1)}, u32[]{:S(2)}, u32[]{:S(2)}) collective-permute-start(bf16[256,2048]{1,0:T(8,128)(2,1)} %get-tuple-element.161), channel_id=1, source_target_pairs={{0,6},{1,7},{2,4},{3,5},{4,2},{5,3},{6,0},{7,1},{8,14},{9,15},{10,... | collective-permute-start | bytes 3145736 | tf_op jit(solution)/shard_map/ppermute | solution.py:51
  552.0 46.1 %collective-permute-start.17 = (bf16[256,2048]{1,0:T(8,128)(2,1)}, bf16[256,2048]{1,0:T(8,128)(2,1)S(1)}, u32[]{:S(2)}, u32[]{:S(2)}) collective-permute-start(bf16[256,2048]{1,0:T(8,128)(2,1)} %get-tuple-element.162), channel_id=1, source_target_pairs={{0,4},{1,5},{2,6},{3,7},{4,0},{5,1},{6,2},{7,3},{8,12},{9,13},{10,... | collective-permute-start | bytes 3145736 | tf_op jit(solution)/shard_map/ppermute | solution.py:51
  552.6 46.6 %collective-permute-start.16 = (bf16[256,2048]{1,0:T(8,128)(2,1)}, bf16[256,2048]{1,0:T(8,128)(2,1)}, u32[]{:S(2)}, u32[]{:S(2)}) collective-permute-start(bf16[256,2048]{1,0:T(8,128)(2,1)} %get-tuple-element.160), channel_id=1, source_target_pairs={{0,2},{1,3},{2,0},{3,1},{4,6},{5,7},{6,4},{7,5},{8,10},{9,11},{10,... | collective-permute-start | bytes 3145736 | tf_op jit(solution)/shard_map/ppermute | solution.py:51
  614.1 259.2 %all-gather.25.cloned.1.call-start = ((), (), s32[]{:S(2)}) async-start(), calls=%async_computation.17 | async-start | bytes 9437184 | tf_op jit(solution)/shard_map/all_gather | solution.py:886
  617.1 18.9 %all-to-all-start.2 = ((bf16[8,4,128,128]{3,2,1,0:T(8,128)(2,1)}), bf16[8,4,128,128]{3,2,1,0:T(8,128)(2,1)S(1)}, u32[]{:S(2)}, u32[]{:S(2)}) async-start(bf16[8,4,128,128]{3,2,1,0:T(8,128)(2,1)} %bitcast.62), calls=%async_computation.2 | async-start | bytes 2097152 | tf_op jit(solution)/shard_map/all_to_all | solution.py:922
  628.8 79.5 %collective-permute-start.22 = (bf16[512,1024]{1,0:T(8,128)(2,1)}, bf16[512,1024]{1,0:T(8,128)(2,1)S(1)}, u32[]{:S(2)}, u32[]{:S(2)}) collective-permute-start(bf16[512,1024]{1,0:T(8,128)(2,1)} %constant_dynamic-slice_fusion.6), channel_id=1, source_target_pairs={{0,8},{8,0},{16,24},{24,16},{1,9},{9,1},{17,25},{25,17},{2,10},{10... | collective-permute-start | bytes 3145736 | tf_op jit(solution)/shard_map/ppermute | solution.py:51
  638.4 44.1 %collective-permute-start.21 = (bf16[1024,128]{1,0:T(8,128)(2,1)S(1)}, bf16[1024,128]{1,0:T(8,128)(2,1)S(1)}, u32[]{:S(2)}, u32[]{:S(2)}) collective-permute-start(bf16[1024,128]{1,0:T(8,128)(2,1)S(1)} %get-tuple-element.183), channel_id=1, source_target_pairs={{0,24},{8,16},{16,8},{24,0},{1,25},{9,17},{17,9},{25,1},{2,26},{10... | collective-permute-start | bytes 786440 | tf_op jit(solution)/shard_map/ppermute | solution.py:51
  641.7 65.5 %collective-permute-start.20 = (bf16[1024,128]{1,0:T(8,128)(2,1)S(1)}, bf16[1024,128]{1,0:T(8,128)(2,1)S(1)}, u32[]{:S(2)}, u32[]{:S(2)}) collective-permute-start(bf16[1024,128]{1,0:T(8,128)(2,1)S(1)} %get-tuple-element.184), channel_id=1, source_target_pairs={{0,16},{8,24},{16,0},{24,8},{1,17},{9,25},{17,1},{25,9},{2,18},{10... | collective-permute-start | bytes 786440 | tf_op jit(solution)/shard_map/ppermute | solution.py:51
  641.7 65.5 %collective-permute-start.19 = (bf16[1024,128]{1,0:T(8,128)(2,1)S(1)}, bf16[1024,128]{1,0:T(8,128)(2,1)S(1)}, u32[]{:S(2)}, u32[]{:S(2)}) collective-permute-start(bf16[1024,128]{1,0:T(8,128)(2,1)S(1)} %get-tuple-element.185), channel_id=1, source_target_pairs={{0,8},{8,0},{16,24},{24,16},{1,9},{9,1},{17,25},{25,17},{2,10},{10... | collective-permute-start | bytes 786440 | tf_op jit(solution)/shard_map/ppermute | solution.py:51
  755.2 81.1 %collective-permute-start.32 = (bf16[512,1024]{1,0:T(8,128)(2,1)}, bf16[512,1024]{1,0:T(8,128)(2,1)}, u32[]{:S(2)}, u32[]{:S(2)}) collective-permute-start(bf16[512,1024]{1,0:T(8,128)(2,1)} %constant_dynamic-slice_fusion.1), channel_id=1, source_target_pairs={{0,8},{8,0},{16,24},{24,16},{1,9},{9,1},{17,25},{25,17},{2,10},{10... | collective-permute-start | bytes 3145736 | tf_op jit(solution)/shard_map/ppermute | solution.py:51
  757.2 10.0 collective-permute-start.27
  762.8 37.0 %collective-permute-start.31 = (bf16[3,1024,128]{2,1,0:T(8,128)(2,1)}, bf16[3,1024,128]{2,1,0:T(8,128)(2,1)}, u32[]{:S(2)}, u32[]{:S(2)}) collective-permute-start(bf16[3,1024,128]{2,1,0:T(8,128)(2,1)} %get-tuple-element.173), channel_id=1, source_target_pairs={{0,24},{8,16},{16,8},{24,0},{1,25},{9,17},{17,9},{25,1},{2,26},{10... | collective-permute-start | bytes 2359304 | tf_op jit(solution)/shard_map/ppermute | solution.py:51
  764.3 68.7 %collective-permute-start.30 = (bf16[3,1024,128]{2,1,0:T(8,128)(2,1)}, bf16[3,1024,128]{2,1,0:T(8,128)(2,1)}, u32[]{:S(2)}, u32[]{:S(2)}) collective-permute-start(bf16[3,1024,128]{2,1,0:T(8,128)(2,1)} %get-tuple-element.174), channel_id=1, source_target_pairs={{0,16},{8,24},{16,0},{24,8},{1,17},{9,25},{17,1},{25,9},{2,18},{10... | collective-permute-start | bytes 2359304 | tf_op jit(solution)/shard_map/ppermute | solution.py:51
  764.5 68.5 %collective-permute-start.29 = (bf16[3,1024,128]{2,1,0:T(8,128)(2,1)}, bf16[3,1024,128]{2,1,0:T(8,128)(2,1)}, u32[]{:S(2)}, u32[]{:S(2)}) collective-permute-start(bf16[3,1024,128]{2,1,0:T(8,128)(2,1)} %get-tuple-element.175), channel_id=1, source_target_pairs={{0,8},{8,0},{16,24},{24,16},{1,9},{9,1},{17,25},{25,17},{2,10},{10... | collective-permute-start | bytes 2359304 | tf_op jit(solution)/shard_map/ppermute | solution.py:51
  771.9 82.4 %collective-permute-start.33 = (bf16[512,1024]{1,0:T(8,128)(2,1)}, bf16[512,1024]{1,0:T(8,128)(2,1)}, u32[]{:S(2)}, u32[]{:S(2)}) collective-permute-start(bf16[512,1024]{1,0:T(8,128)(2,1)} %constant_dynamic-slice_fusion), channel_id=1, source_target_pairs={{0,8},{8,0},{16,24},{24,16},{1,9},{9,1},{17,25},{25,17},{2,10},{10... | collective-permute-start | bytes 3145736 | tf_op jit(solution)/shard_map/ppermute | solution.py:51
  897.8 17.3 %collective-permute-start.36 = (bf16[4,256,2048]{2,1,0:T(8,128)(2,1)}, bf16[4,256,2048]{2,1,0:T(8,128)(2,1)}, u32[]{:S(2)}, u32[]{:S(2)}) collective-permute-start(bf16[4,256,2048]{2,1,0:T(8,128)(2,1)} %dynamic-slice_bitcast_fusion), channel_id=1, source_target_pairs={{0,1},{1,0},{2,3},{3,2},{4,5},{5,4},{6,7},{7,6},{8,9},{9,8},{10,11... | collective-permute-start | bytes 12582920 | tf_op jit(solution)/shard_map/ppermute | solution.py:51
  902.7 25.4 %collective-permute-start.34 = (bf16[4,256,2048]{2,1,0:T(8,128)(2,1)}, bf16[4,256,2048]{2,1,0:T(8,128)(2,1)}, u32[]{:S(2)}, u32[]{:S(2)}) collective-permute-start(bf16[4,256,2048]{2,1,0:T(8,128)(2,1)} %dynamic-slice_bitcast_fusion.1), channel_id=1, source_target_pairs={{0,1},{1,0},{2,3},{3,2},{4,5},{5,4},{6,7},{7,6},{8,9},{9,8},{10,11... | collective-permute-start | bytes 12582920 | tf_op jit(solution)/shard_map/ppermute | solution.py:51
  907.6 186.3 %all-reduce.3.cloned.1.call-start = ((), (), s32[]{:S(2)}) async-start(), calls=%async_computation.18 | async-start | bytes 8388608 | tf_op jit(solution)/shard_map/psum | solution.py:1011
  922.3 27.2 %collective-permute-start.39 = (bf16[256,2048]{1,0:T(8,128)(2,1)}, bf16[256,2048]{1,0:T(8,128)(2,1)S(1)}, u32[]{:S(2)}, u32[]{:S(2)}) collective-permute-start(bf16[256,2048]{1,0:T(8,128)(2,1)} %get-tuple-element.158), channel_id=1, source_target_pairs={{0,6},{1,7},{2,4},{3,5},{4,2},{5,3},{6,0},{7,1},{8,14},{9,15},{10,... | collective-permute-start | bytes 3145736 | tf_op jit(solution)/shard_map/ppermute | solution.py:51
  922.8 69.0 %collective-permute-start.38 = (bf16[256,2048]{1,0:T(8,128)(2,1)}, bf16[256,2048]{1,0:T(8,128)(2,1)}, u32[]{:S(2)}, u32[]{:S(2)}) collective-permute-start(bf16[256,2048]{1,0:T(8,128)(2,1)} %get-tuple-element.159), channel_id=1, source_target_pairs={{0,4},{1,5},{2,6},{3,7},{4,0},{5,1},{6,2},{7,3},{8,12},{9,13},{10,... | collective-permute-start | bytes 3145736 | tf_op jit(solution)/shard_map/ppermute | solution.py:51
  924.3 67.5 %collective-permute-start.37 = (bf16[256,2048]{1,0:T(8,128)(2,1)}, bf16[256,2048]{1,0:T(8,128)(2,1)}, u32[]{:S(2)}, u32[]{:S(2)}) collective-permute-start(bf16[256,2048]{1,0:T(8,128)(2,1)} %get-tuple-element.157), channel_id=1, source_target_pairs={{0,2},{1,3},{2,0},{3,1},{4,6},{5,7},{6,4},{7,5},{8,10},{9,11},{10,... | collective-permute-start | bytes 3145736 | tf_op jit(solution)/shard_map/ppermute | solution.py:51
  935.3 114.2 %collective-permute-start.41 = (bf16[256,2048]{1,0:T(8,128)(2,1)}, bf16[256,2048]{1,0:T(8,128)(2,1)}, u32[]{:S(2)}, u32[]{:S(2)}) collective-permute-start(bf16[256,2048]{1,0:T(8,128)(2,1)} %get-tuple-element.155), channel_id=1, source_target_pairs={{0,6},{1,7},{2,4},{3,5},{4,2},{5,3},{6,0},{7,1},{8,14},{9,15},{10,... | collective-permute-start | bytes 3145736 | tf_op jit(solution)/shard_map/ppermute | solution.py:51
  935.8 113.8 %collective-permute-start.40 = (bf16[256,2048]{1,0:T(8,128)(2,1)}, bf16[256,2048]{1,0:T(8,128)(2,1)}, u32[]{:S(2)}, u32[]{:S(2)}) collective-permute-start(bf16[256,2048]{1,0:T(8,128)(2,1)} %get-tuple-element.156), channel_id=1, source_target_pairs={{0,4},{1,5},{2,6},{3,7},{4,0},{5,1},{6,2},{7,3},{8,12},{9,13},{10,... | collective-permute-start | bytes 3145736 | tf_op jit(solution)/shard_map/ppermute | solution.py:51
  950.5 99.1 %collective-permute-start.35 = (bf16[256,2048]{1,0:T(8,128)(2,1)}, bf16[256,2048]{1,0:T(8,128)(2,1)}, u32[]{:S(2)}, u32[]{:S(2)}) collective-permute-start(bf16[256,2048]{1,0:T(8,128)(2,1)} %get-tuple-element.154), channel_id=1, source_target_pairs={{0,2},{1,3},{2,0},{3,1},{4,6},{5,7},{6,4},{7,5},{8,10},{9,11},{10,... | collective-permute-start | bytes 3145736 | tf_op jit(solution)/shard_map/ppermute | solution.py:51
  997.3 48.5 %all-to-all-start.4 = ((f32[8,1,256]{2,1,0:T(1,128)}), f32[8,1,256]{2,1,0:T(1,128)S(1)}, u32[]{:S(2)}, u32[]{:S(2)}) async-start(f32[8,1,256]{2,1,0:T(1,128)} %bitcast.114), calls=%async_computation.7 | async-start | bytes 16384 | tf_op jit(solution)/shard_map/all_to_all | solution.py:922
  1047.8 17.2 %collective-permute-start.42 = (f32[256,20]{1,0:T(8,128)}, f32[256,20]{1,0:T(8,128)}, u32[]{:S(2)}, u32[]{:S(2)}) collective-permute-start(f32[256,20]{1,0:T(8,128)} %pad_maximum_fusion.11), channel_id=1, source_target_pairs={{0,8},{8,0},{16,24},{24,16},{1,9},{9,1},{17,25},{25,17},{2,10},{10... | collective-permute-start | bytes 61448 | tf_op jit(solution)/shard_map/ppermute | solution.py:51
  1066.2 26.8 %collective-permute-start.43 = (f32[256,20]{1,0:T(8,128)S(1)}, f32[256,20]{1,0:T(8,128)S(1)}, u32[]{:S(2)}, u32[]{:S(2)}) collective-permute-start(f32[256,20]{1,0:T(8,128)S(1)} %fusion.67), channel_id=1, source_target_pairs={{0,16},{8,24},{16,0},{24,8},{1,17},{9,25},{17,1},{25,9},{2,18},{10... | collective-permute-start | bytes 61448 | tf_op jit(solution)/shard_map/ppermute | solution.py:51
  (76 other events, 965.7 us)
Sparse Core Ops, SparseCore 0:
  11.6 57.3 all-gather.12
  70.9 54.7 all-gather.14
  127.6 54.3 all-gather.16
  184.3 63.3 all-gather.20
  250.0 53.8 all-gather.18
  305.6 54.3 all-gather.22
  424.4 100.5 reduce-scatter.7
  527.3 99.1 reduce-scatter.3
  628.8 122.1 reduce-scatter.5
  752.9 53.8 all-gather.24
  928.2 158.7 all-reduce.2

commit v3 on v2

--- a/solution.py
+++ b/solution.py
@@ -79,7 +79,7 @@
     return values
 
 
-def reduce_rows(partial, *after):
+def reduce_start(partial):
     count = partial.shape[0]
     me = lax.axis_index("exp")
     core, chip = me % 2, me // 2
@@ -87,12 +87,28 @@
     got = flip(pick(pairs, 1 - core, 1), "exp", 1)
     mine = pick(pairs, core, 1)
     both = (mine.astype(F32) + got.astype(F32)).astype(BF16)
-    parts = [flip(pick(both, chip ^ m), "exp", 2 * m) for m in range(1, count // 2)]
-    parts = [hold(part, *after) for part in parts]
-    total = pick(mine, chip).astype(F32) + pick(got, chip).astype(F32)
+    return both, (pick(mine, chip), pick(got, chip))
+
+
+def reduce_send(both):
+    chip = lax.axis_index("exp") // 2
+    return [flip(pick(both, chip ^ m), "exp", 2 * m) for m in range(1, both.shape[0])]
+
+
+def reduce_total(parts, own, *after):
+    parts = [hold(part, *after) for part in parts] if after else parts
+    total = own[0].astype(F32) + own[1].astype(F32)
     for part in parts:
         total = total + part.astype(F32)
     return total
+
+
+def reduce_finish(both, own, *after):
+    return reduce_total(reduce_send(both), own, *after)
+
+
+def reduce_rows(partial, *after):
+    return reduce_finish(*reduce_start(partial), *after)
 
 
 def block_place(block, ctx_count, place):
@@ -276,16 +292,21 @@
         out_specs=(VMEM, VMEM),
         scratch_shapes=[pltpu.VMEM((HD, length), BF16)] * 3 + [pltpu.VMEM((length, HD), F32)] * 2,
         compiler_params=pltpu.CompilerParams(vmem_limit_bytes=50 * 2**20),
-        cost_estimate=SMALL,
+        cost_estimate=pl.CostEstimate(
+            flops=160 * length * length // 2 * HD, bytes_accessed=0, transcendentals=0
+        ),
         name="attend_back",
     )(place, qk, v, grads, out_t, lse)
 
 
-def spread_pairs(values):
+def spread_pairs(values, *after):
     count = values.shape[0]
     place = lax.axis_index("ctx")
     parts = [pick(values, place ^ m) for m in range(count)]
-    return jnp.stack([parts[0]] + [flip(parts[m], "ctx", m) for m in range(1, count)])
+    parts[1:] = [flip(parts[m], "ctx", m) for m in range(1, count)]
+    if after:
+        parts[1:] = [hold(part, *after) for part in parts[1:]]
+    return jnp.stack(parts)
 
 
 def return_pairs(values):
@@ -442,12 +463,13 @@
     place, qk_all, v_all, out_t, lse, projected, factors, gains = kept
     exp_count, seq_count, shard_len, width = projected.shape
     local_heads = width // 3 // HD
-    grads = hold(spread_pairs(grads), *early)
+    grads = spread_pairs(grads, *early)
     back, sums = attend_back_call(place, qk_all, v_all, grads, out_t, lse)
     count = back.shape[0]
-    parts = jnp.stack([back[0]] + [flip(back[m], "ctx", m) for m in range(1, count)])
-    parts = hold(parts, *later)
-    sums = butterfly_sum(return_pairs(sums), "exp")
+    parts = [flip(back[m], "ctx", m) for m in range(1, count)]
+    sums = butterfly_sum(return_pairs(hold(sums, later[1])), "exp")
+    during = later[0](sums)
+    parts = jnp.stack([back[0]] + [hold(part, during) for part in parts])
     sums = sums.reshape(seq_count, local_heads, 2, exp_count, shard_len).sum(axis=1) / model_width
     sums = jnp.transpose(sums, (1, 2, 0, 3))
     stats = jnp.stack([factors[0], factors[1], sums[0], sums[1]], axis=-1)
@@ -455,7 +477,7 @@
         place, projected, stats, gains, cosine, half_signs(sines, 1.0, -1.0), parts
     )
     qgain_part, kgain_part = jnp.split(gain_parts[0], 2)
-    return grad_qkv, qgain_part, kgain_part, sums
+    return grad_qkv, qgain_part, kgain_part, parts
 
 
 def gathered_forward(projected, query_gain, key_gain, cosine, sines, model_width, early):
@@ -648,6 +670,7 @@
     dots = lax.psum(dots, "exp")[..., None] / model_width
     grad_queries = (factors[0] * (qunit_grad - query_unit * dots[0])).astype(BF16)
     grad_keys = (factors[1] * (kunit_grad - key_unit * dots[1])).astype(BF16)
+    later[0](grad_heads)
     grad_qkv = jnp.concatenate([grad_queries, grad_keys, grad_values], axis=-1)
     return grad_qkv, qgain_part, kgain_part, dots
 
@@ -782,7 +805,7 @@
         out_ref[...] = acc_ref[...].astype(out_ref.dtype)
 
 
-def back_call(parts, weights, which, kind=BF16, *after):
+def back_call(parts, weights, which, kind=BF16, *after, cost=SMALL):
     experts, count, width = parts[0].shape
     model_width = weights.shape[2]
     tile, cols = math.gcd(count, 512), math.gcd(model_width, 2048)
@@ -800,22 +823,33 @@
         out_shape=jax.ShapeDtypeStruct((count, model_width), kind),
         scratch_shapes=[pltpu.VMEM((tile, cols), F32)],
         compiler_params=EXPERT_PARAMS,
-        cost_estimate=SMALL,
+        cost_estimate=cost,
         name="back",
     )(*parts, *([weights] * len(parts)), *after)
 
 
-def grad_kernel(half_ref, own_rows, own_grads, near_rows, near_grads, out_ref):
+def grad_kernel(half_ref, own_rows, own_grads, near_rows, near_grads, *refs):
     total = lax.dot_general(own_rows[...], own_grads[0], TN, preferred_element_type=F32)
     total += lax.dot_general(near_rows[...], near_grads[0], TN, preferred_element_type=F32)
-    out_ref[...] = total.astype(BF16)
-
-
-def grad_call(own_rows, own_grads, near_rows, near_grads, half):
+    refs[-1][...] = total.astype(BF16)
+
+
+def grad_call(own_rows, own_grads, near_rows, near_grads, half, *after):
     count, model_width = own_rows.shape
     experts, _, width = near_grads.shape
-    cols = math.gcd(model_width, 512)
+    shards = lax.axis_size("ctx")
+    cols = math.gcd(model_width // shards, 512)
+    tiles = model_width // shards // cols
     row_spec = pl.BlockSpec((count, cols), lambda e, d, h: (0, d))
+
+    def scatter_order(tile, half):
+        shard = tile // tiles
+        apart = jnp.where(half == 0, shard, shards - 1 - shard)
+        near = apart < shards // 2
+        step = jnp.where(half == 0, shard, shard - shards // 2)
+        step = jnp.where(near, step, jnp.where(half == 0, shards - 1 - shard, shards // 2 - 1 - shard))
+        return (2 * step + jnp.where(near, 0, 1)) * tiles + tile % tiles
+
     return pl.pallas_call(
         grad_kernel,
         grid_spec=pltpu.PrefetchScalarGridSpec(
@@ -826,19 +860,22 @@
                 pl.BlockSpec((1, count, width), lambda e, d, h: (e, 0, h[0])),
                 row_spec,
                 pl.BlockSpec((1, count, width), lambda e, d, h: (e, 0, 0)),
-            ],
-            out_specs=pl.BlockSpec((cols, width), lambda e, d, h: (d, e)),
+            ]
+            + [pl.BlockSpec(memory_space=pl.ANY)] * len(after),
+            out_specs=pl.BlockSpec(
+                (cols, width), lambda e, d, h: (scatter_order(d, h[0]), e)
+            ),
         ),
         out_shape=jax.ShapeDtypeStruct((model_width, experts * width), BF16),
         compiler_params=EXPERT_PARAMS,
         cost_estimate=SMALL,
         name="grad",
-    )(half, own_rows, own_grads, near_rows, near_grads)
+    )(half, own_rows, own_grads, near_rows, near_grads, *after)
 
 
 def scatter_rows(term):
     count = lax.axis_size("ctx")
-    groups = [[i for i in range(count) if i % 2 == parity] for parity in range(2)]
+    groups = [list(range(count // 2)), list(range(count // 2, count))]
     return lax.psum_scatter(
         term, "ctx", scatter_dimension=0, axis_index_groups=groups, tiled=True
     )
@@ -846,10 +883,7 @@
 
 def swap_rows(term):
     size = term.shape[0] // 2
-    odd = lax.axis_index("ctx") % 2
-    sent = flip(lax.dynamic_slice_in_dim(term, (1 - odd) * size, size, 0), "ctx", 1)
-    kept = lax.dynamic_slice_in_dim(term, odd * size, size, 0)
-    return sent, kept
+    return flip(term[size:], "ctx", lax.axis_size("ctx") - 1), term[:size]
 
 
 def body(
@@ -885,7 +919,8 @@
     def gather(values):
         return lax.all_gather(values, "exp", axis=0, tiled=False)
 
-    half = (ctx_place % 2).astype(jnp.int32).reshape(1)
+    mirror = ctx_count - 1
+    half = (ctx_place * 2 // ctx_count).astype(jnp.int32).reshape(1)
     whole = jnp.zeros((1,), jnp.int32)
     local_float = block_input.astype(F32).reshape(rows_dev, model_width)
     local_factor = rms_factor(local_float)
@@ -897,9 +932,9 @@
     own_grads = cotangent.reshape(rows_dev, model_width)
     grad_low = gather(own_grads).reshape(rows_all, model_width)
     full_out = gather(w_out).reshape(exp_count * local_width, model_width)
-    near_low = gather(hold(flip(own_grads, "ctx", 1), weights)).reshape(rows_all, model_width)
+    near_low = gather(hold(flip(own_grads, "ctx", mirror), weights)).reshape(rows_all, model_width)
     all_routes = gather(own_routes).reshape(rows_all, TOP)
-    near_routes = flip(all_routes, "ctx", 1)
+    near_routes = flip(all_routes, "ctx", mirror)
     w_qkv = hold(w_qkv, weights, near_routes)
     grad_down = down_call(grad_low, weights, whole, hidden_units)
     near_down = down_call(near_low, weights, half, hidden_units // 2)
@@ -939,10 +974,8 @@
         gates = lax.dynamic_slice_in_dim(gates, exp_place * experts_here, experts_here, 1)
         return jnp.transpose(gates)[:, :, None]
 
-    if paired:
-        attended = return_pairs(hold(attended, own_mixed))
-    mixed = hold(gather(own_mixed).reshape(rows_all, model_width), near_down, attended)
-    near_mixed = gather(hold(flip(own_mixed, "ctx", 1), near_down))
+    mixed = hold(gather(own_mixed).reshape(rows_all, model_width), near_down)
+    near_mixed = gather(hold(flip(own_mixed, "ctx", mirror), near_down))
     gates = local_gates(mixed, all_routes)
 
     gated_middle, grad_gate, grad_up, dots = hidden_call(
@@ -952,20 +985,24 @@
     choice_grad = exchange(
         jnp.transpose(gate_grads.reshape(experts_here, exp_count, rows_dev), (1, 0, 2))
     )
-    near_mixed = hold(near_mixed.reshape(rows_all, model_width), gated_middle)
+    slot_rows = back_call([grad_gate, grad_up], weights, (0, 1), BF16)
+    if paired:
+        attended = return_pairs(hold(attended, gated_middle))
+    slot_both, slot_own = reduce_start(slot_rows.reshape(exp_count, rows_dev, model_width))
+    slot_parts = reduce_send(slot_both)
+    near_mixed = hold(
+        near_mixed.reshape(rows_all, model_width), slot_both, choice_grad
+    )
     near_gates = local_gates(near_mixed, near_routes)
     near_middle, near_grad_gate, near_grad_up = hidden_call(
         near_mixed, weights, near_down, near_gates, half, False
     )
 
-    down_term = grad_call(grad_low, gated_middle, near_low, near_middle, half)
-    slot_rows = back_call([grad_gate, grad_up], weights, (0, 1), BF16, down_term, choice_grad)
-    gate_term = grad_call(mixed, grad_gate, near_mixed, near_grad_gate, half)
-    up_term = grad_call(mixed, grad_up, near_mixed, near_grad_up, half)
-    down_sum, gate_sum, up_sum = (scatter_rows(t) for t in (down_term, gate_term, up_term))
-    slot_sum = reduce_rows(
-        slot_rows.reshape(exp_count, rows_dev, model_width), gate_term, up_term
-    )
+    down_term = grad_call(
+        grad_low, gated_middle, near_low, near_middle, half, attended, *slot_parts
+    )
+    slot_sum = reduce_total(slot_parts, slot_own)
+
     choice_grad = jnp.transpose(choice_grad, (2, 0, 1)).reshape(rows_dev, experts_all)
     choice_grad = jnp.where(chosen(own_routes), choice_grad, 0.0)
     logit_grad = (
@@ -986,76 +1023,104 @@
     own_branch = grad_hidden.astype(BF16)
     early_part = jnp.concatenate([router_part, egain_part[:, None]], axis=1)
     early_part = exchange(early_part.reshape(exp_count, -1, experts_all + 1))
-    branch_rows = gather(hold(own_branch, up_sum)).reshape(exp_count, seq_count, shard_len, model_width)
 
     grad_attended = jnp.einsum(
         "rd,hd->rh", own_branch, full_out, preferred_element_type=F32
     ).astype(BF16)
-    expert_out = back_call([gated_middle], weights, (2,), BF16, grad_attended)
     sent = grad_attended.reshape(seq_count, shard_len, exp_count, local_heads, HD)
     sent = jnp.transpose(sent, (2, 0, 3, 1, 4)).reshape(exp_count, pair_count, shard_len, HD)
     grads = jnp.transpose(exchange(sent), (1, 0, 2, 3)).reshape(pair_count, ctx_rows, HD)
-    swapped = [swap_rows(term) for term in (gate_sum, hold(up_sum, grads), down_sum)]
+    gate_term = grad_call(mixed, grad_gate, near_mixed, near_grad_gate, half, grads)
+    down_sum, gate_sum = scatter_rows(down_term), scatter_rows(gate_term)
+    def place_rows(whole_grad, halves, which, *after):
+        sent_rows, kept_rows = halves
+        sent_rows = hold(sent_rows, *after)
+        lower = jnp.where(half[0] == 0, kept_rows, sent_rows)
+        upper = jnp.where(half[0] == 0, sent_rows, kept_rows)
+        parts = [
+            v.astype(F32).reshape(-1, experts_here, hidden_units // 2) for v in (lower, upper)
+        ]
+        part = jnp.concatenate(parts, axis=-1)[:, None]
+        return lax.dynamic_update_slice_in_dim(whole_grad, part, which, 1)
+
+    down_swapped = swap_rows(hold(down_sum, grads))
+    branch_rows = gather(hold(own_branch, gate_term))
+    late_terms = []
+
+    def meanwhile(sums):
+        up_term = grad_call(
+            mixed, grad_up, near_mixed, near_grad_up, half, sums
+        )
+        up_sum = scatter_rows(up_term)
+        cost = pl.CostEstimate(
+            flops=16 * rows_all * model_width * experts_here * hidden_units,
+            bytes_accessed=0,
+            transcendentals=0,
+        )
+        expert_out = back_call([gated_middle], weights, (2,), BF16, up_term, cost=cost)
+        late_terms.append((up_sum, expert_out))
+        return expert_out
+
     grad_qkv, qgain_part, kgain_part, ended = backward(
-        kept, grads, query_gain, key_gain, cosine, sines, model_width, (expert_out, swapped[2][0]), (swapped[0][0], swapped[1][0])
+        kept, grads, query_gain, key_gain, cosine, sines, model_width, (gate_term, early_part), (meanwhile, down_swapped[0])
     )
     attended_rows = attended.reshape(seq_count, local_heads, exp_count, shard_len, HD)
+    up_sum, expert_out = late_terms[0]
+    early_sum = jnp.sum(early_part, axis=0)
+    gain_parts = [v[:, None] for v in (qgain_part, kgain_part)]
+    sums = butterfly_sum(jnp.concatenate([early_sum] + gain_parts, axis=1), "ctx")
+    gate_swapped = swap_rows(hold(gate_sum, sums))
+    grad_qkv = hold(grad_qkv, gate_swapped[0], up_sum)
     branch_rows = hold(branch_rows, ended)
+    branch_rows = branch_rows.reshape(exp_count, seq_count, shard_len, model_width)
     outw_part = jnp.einsum(
-        "shetc,estd->hcd", attended_rows, branch_rows, preferred_element_type=F32
-    ).reshape(local_width, model_width)
+        "shetc,estd->dhc", attended_rows, branch_rows, preferred_element_type=F32
+    ).reshape(model_width, local_width)
     qkv_part = jnp.einsum(
         "rd,rh->dh", normed, grad_qkv.reshape(rows_all, -1), preferred_element_type=F32
     )
-    qkv_part, outw_part = qkv_part.astype(BF16), outw_part.astype(BF16)
-    qkv_grad, out_grad = lax.psum((qkv_part, outw_part), "ctx")
+    proj_part = jnp.concatenate([qkv_part.astype(BF16), outw_part.astype(BF16)], axis=1)
+    proj_sum = lax.psum_scatter(proj_part, "ctx", scatter_dimension=0, tiled=True)
 
     w_qkv = jnp.concatenate([w_query, w_key, w_value], axis=1)
     grad_rows_qkv = grad_qkv.reshape(1, rows_all, -1)
     normed_back = back_call(
-        [grad_rows_qkv], w_qkv[None, None], (0,), BF16, qkv_part, outw_part
-    )
-    grad_normed = reduce_rows(normed_back.reshape(exp_count, rows_dev, model_width))
+        [grad_rows_qkv], w_qkv[None, None], (0,), BF16, proj_part
+    )
+    normed_both, normed_own = reduce_start(normed_back.reshape(exp_count, rows_dev, model_width))
+    normed_parts = reduce_send(normed_both)
+    up_swapped = swap_rows(hold(up_sum, proj_part))
+    grad_normed = reduce_total(normed_parts, normed_own, up_swapped[0])
     attend_part = jnp.sum(grad_normed * local_unit, axis=0)
+    attend_sum = jnp.sum(exchange(attend_part.reshape(exp_count, -1)), axis=0)
+    attend_grad = butterfly_sum(attend_sum, "ctx")
+    proj_sum = hold(proj_sum, attend_grad)
+    proj_grad = lax.all_gather(proj_sum, "ctx", axis=0, tiled=True)
     lunit_grad = grad_normed * attend_gain
     input_grad = grad_hidden + local_factor * (
         lunit_grad - local_unit * jnp.mean(lunit_grad * local_unit, axis=-1, keepdims=True)
     )
-    halves = []
-    even = ctx_place % 2 == 0
-    for sent_rows, kept_rows in swapped:
-        sent_rows = hold(sent_rows, grad_normed)
-        lower = jnp.where(even, kept_rows, sent_rows)
-        upper = jnp.where(even, sent_rows, kept_rows)
-        parts = [
-            v.astype(F32).reshape(-1, experts_here, hidden_units // 2) for v in (lower, upper)
-        ]
-        halves.append(jnp.concatenate(parts, axis=-1))
-    expert_grad = jnp.stack(halves, axis=2)
-    expert_out = hold(expert_out, normed_back)
-    mixture = reduce_rows(expert_out.reshape(exp_count, rows_dev, model_width), grad_normed)
+    expert_grad = jnp.zeros((model_width // ctx_count, 3, experts_here, hidden_units), F32)
+    expert_grad = place_rows(expert_grad, down_swapped, 2, normed_both)
+    expert_grad = place_rows(expert_grad, gate_swapped, 0, normed_both)
+    expert_grad = place_rows(expert_grad, up_swapped, 1, grad_normed)
+    produced = hold(expert_out, normed_both).reshape(exp_count, rows_dev, model_width)
+    mixture = reduce_finish(*reduce_start(produced), grad_normed)
     block_output = (hidden + mixture).astype(BF16).reshape(block_input.shape)
 
-    attend_sum = jnp.sum(exchange(attend_part.reshape(exp_count, -1)), axis=0)
-    early_sum = jnp.sum(hold(early_part, grad_qkv), axis=0)
-    late = [v[:, None] for v in (attend_sum, qgain_part, kgain_part)]
-    sums = butterfly_sum(jnp.concatenate([early_sum] + late, axis=1), "ctx")
-    last = (sums, input_grad, block_output, expert_grad)
-    qkv_grad = hold(qkv_grad, *last).astype(F32)
-    out_grad = hold(out_grad, *last).astype(F32)
+    proj_grad = hold(proj_grad, input_grad, block_output, expert_grad).astype(F32)
+    grads_of = [proj_grad[:, i * local_width : (i + 1) * local_width] for i in range(4)]
     return (
         block_output,
         input_grad.reshape(block_input.shape),
+        attend_grad,
+        *grads_of[:3],
+        grads_of[3].T,
         sums[:, experts_all + 1],
-        qkv_grad[:, :local_width],
-        qkv_grad[:, local_width : 2 * local_width],
-        qkv_grad[:, 2 * local_width :],
-        out_grad,
         sums[:, experts_all + 2],
-        sums[:, experts_all + 3],
         sums[:, experts_all],
         sums[:, :experts_all],
-        expert_grad,
+        jnp.transpose(expert_grad, (0, 2, 1, 3)),
     )
 
 

time: 1110 us -> 1100 us (level)
  waiting for transfers between devices: 325 us -> 250 us
  starting transfers between devices: 67.7 us -> 135 us
  blocking collectives: 38.4 us -> 72.5 us
  local copies, waits for them, and re-layouts: 153 us -> 126 us
    ppermute x44 -> x46, waiting for transfers between devices: 274 us -> 196 us  [flip(): lax.ppermute(values, axis, [(i, i ^ mask) for i in range(lax.axis_size(ax...]
    ppermute x44 -> x46, starting transfers between devices: 53.4 us -> 130 us  [flip(): lax.ppermute(values, axis, [(i, i ^ mask) for i in range(lax.axis_size(ax...]
    all_to_all x0 -> x3, blocking collectives: none -> 34.5 us  [exchange(): lax.all_to_all(values, 'exp', split_axis=0, concat_axis=0, tiled=True)]
    another operation x8 -> x4, other arithmetic: 28.5 us -> 8.23 us  [the longest x3 5.13 us: spread_pairs(): return jnp.stack(parts)]
    another operation x3 -> x0, local copies, waits for them, and re-layouts: 18.1 us -> none  [body(): expert_grad = jnp.stack(halves, axis=2)]
    unnamed x138 -> x165, local copies, waits for them, and re-layouts: 69 us -> 53.8 us
    all_to_all x4 -> x1, waiting for transfers between devices: 13.3 us -> 0.01 us  [exchange(): lax.all_to_all(values, 'exp', split_axis=0, concat_axis=0, tiled=True)]
    dynamic_update_slice x0 -> x3, other arithmetic: none -> 13.2 us  [place_rows(): return lax.dynamic_update_slice_in_dim(whole_grad, part, which, 1)]
  transfers between devices with their start and end apart: 59 -> 59, of which waited for: 26 -> 27; matrix products, arithmetic and copies ran while one was open for 22% -> 19% of each run, Pallas kernels for 27% -> 31%
where the time goes in v3:
time: 1100 us
  Pallas kernels  363 us (33%)
  waiting for transfers between devices  250 us (23%)
  starting transfers between devices  135 us (12%)
  local copies, waits for them, and re-layouts  126 us (11%)
  other arithmetic  81.9 us (7%)
  blocking collectives  72.5 us (7%)
  matrix products  56.8 us (5%)
  between operations  15.6 us (1%)
    ppermute x46, waiting for transfers between devices, flip(): lax.ppermute(values, axis, [(i, i ^ mask) for i in range(lax.axis_size(ax...  196 us
    ppermute x46, starting transfers between devices, flip(): lax.ppermute(values, axis, [(i, i ^ mask) for i in range(lax.axis_size(ax...  130 us
    pallas_call x3, Pallas kernels, back_call(): pl.pallas_call(functools.partial(back_kernel, count=len(parts), chunk=mat...  89.2 us
    pallas_call x2, Pallas kernels, hidden_call(): pl.pallas_call(functools.partial(hidden_kernel, chunk=math.gcd(tile, 256)...  79.8 us
    pallas_call x3, Pallas kernels, grad_call(): pl.pallas_call(grad_kernel, grid_spec=pltpu.PrefetchScalarGridSpec(num_sc...  75.1 us
    unnamed x165, local copies, waits for them, and re-layouts  53.8 us
    pallas_call x2, Pallas kernels, down_call(): pl.pallas_call(down_kernel, grid_spec=pltpu.PrefetchScalarGridSpec(num_sc...  40.2 us
    all_gather x7, waiting for transfers between devices, gather(): return lax.all_gather(values, 'exp', axis=0, tiled=False)  37.9 us
  transfers between devices with their start and end apart: 59, of which 27 were waited for; matrix products, arithmetic and copies ran while one was open for 19% of the time, Pallas kernels for 31%

profile of v3, /device:TPU:0, one launch (start us, length us, event | category | flops | bytes accessed | tf_op | source)
XLA Modules:
  0.0 1100.0 jit_solution(15451534257757651650)
XLA Ops:
  18.2 24.6 %copy.212 = bf16[2048,2,3,1024]{3,0,2,1:T(8,128)(2,1)} copy(bf16[2048,2,3,1024]{3,1,2,0:T(2,128)(2,1)} %param.23) | data formatting | bytes 50331648 | tf_op args[10]
  44.5 9.3 all_gather.44
  69.0 10.0 fusion.3.proj_ref
  93.1 6.9 rotate.1
  105.5 14.9 %collective-permute-start.5 = (bf16[2,1024,128]{2,1,0:T(8,128)(2,1)S(1)}, bf16[2,1024,128]{2,1,0:T(8,128)(2,1)}, u32[]{:S(2)}, u32[]{:S(2)}) collective-permute-start(bf16[2,1024,128]{2,1,0:T(8,128)(2,1)S(1)} %get-tuple-element.153), channel_id=1, source_target_pairs={{0,16},{8,24},{16,0},{24,8},{1,17},{9,25},{17,1},{25,9},{2,18},{10... | collective-permute-start | bytes 1572872 | tf_op jit(solution)/shard_map/ppermute | solution.py:51
  122.7 13.1 %collective-permute-start.7 = (bf16[1024,128]{1,0:T(8,128)(2,1)S(1)}, bf16[1024,128]{1,0:T(8,128)(2,1)}, u32[]{:S(2)}, u32[]{:S(2)}) collective-permute-start(bf16[1024,128]{1,0:T(8,128)(2,1)S(1)} %copy-done.50), channel_id=1, source_target_pairs={{0,8},{8,0},{16,24},{24,16},{1,9},{9,1},{17,25},{25,17},{2,10},{10... | collective-permute-start | bytes 786440 | tf_op jit(solution)/shard_map/ppermute | solution.py:51
  135.8 24.2 %down.2.refs_1_.down_ref = f32[2,2048,1024]{2,1,0:T(8,128)} custom-call(s32[1]{0:T(128)} %constant.258.clone.1.half_ref, bf16[2048,2048]{1,0:T(8,128)(2,1)} %bitcast.281, bf16[2,3,2048,1024]{3,2,1,0:T(8,128)(2,1)} %bitcast.263), custom_call_target="tpu_custom_call" | custom-call | tf_op jit(solution)/shard_map/down/pallas_call | solution.py:692
  160.0 8.8 collective-permute-done.8
  173.6 27.8 %attend.1 = (bf16[4,1024,128]{2,1,0:T(8,128)(2,1)S(1)}, f32[128,4096]{1,0:T(8,128)}, f32[8,1,512]{2,1,0:T(1,128)S(1)}) custom-call(s32[1]{0:T(128)} %bitcast.1.place_ref, bf16[4,2,1024,128]{3,2,1,0:T(8,128)(2,1)} %hold.33.qk_ref, bf16[4,1024,128]{2,1,0:T(8,128)(2,1)S(1)} %pad_maximum_fusion.3.v_ref), custom_call_target="tpu_custom_call" | custom-call | tf_op jit(solution)/shard_map/attend/pallas_call | solution.py:265
  201.7 28.7 %all_to_all.29 = bf16[32,128,128]{2,1,0:T(8,128)(2,1)S(1)} all-to-all(bf16[32,128,128]{2,1,0:T(8,128)(2,1)S(1)} %bitcast.302), channel_id=1, replica_groups=mesh['ctx'=4,'exp'=8] {'ctx','exp'}, dimensions={0} | all-to-all | bytes 2097152 | tf_op jit(solution)/shard_map/all_to_all | solution.py:456
  233.1 6.8 multiply_reduce_fusion.4
  244.6 16.0 %down.3.refs_1_.down_ref = f32[2,2048,512]{2,1,0:T(8,128)} custom-call(s32[1]{0:T(128)} %bitcast.37.half_ref, bf16[2048,2048]{1,0:T(8,128)(2,1)} %all-gather.24.cloned.1.call-done.rows_ref.near_rows, bf16[2,3,2048,1024]{3,2,1,0:T(8,128)(2,1)} %bitcast.264), custom_call_target="tpu_custom_call" | custom-call | tf_op jit(solution)/shard_map/down/pallas_call | solution.py:692
  260.6 7.6 collective-permute-done.11.refs_0_
  268.4 31.8 %all-gather.22.cloned.1.call-done.refs_0_ = bf16[2048,2048]{1,0:T(8,128)(2,1)} async-done(((bf16[256,2048]{1,0:T(8,128)(2,1)}), bf16[2048,2048]{1,0:T(8,128)(2,1)}) %all-gather.22.cloned.1.call-update) | async-done | bytes 8388624 | tf_op jit(solution)/shard_map/all_gather | solution.py:920
  300.2 5.7 fusion.44
  307.9 52.1 %hidden.2 = (bf16[2,2048,1024]{2,1,0:T(8,128)(2,1)}, bf16[2,2048,1024]{2,1,0:T(8,128)(2,1)}, bf16[2,2048,1024]{2,1,0:T(8,128)(2,1)}, f32[2,2,2048,128]{3,2,1,0:T(8,128)}) custom-call(s32[1]{0:T(128)} %constant.258.clone.1.half_ref, bf16[2048,2048]{1,0:T(8,128)(2,1)} %hold.35.rows_ref.own_rows, bf16[2,3,2048,1024]{3,2,1,0:T(8,128)(2,1)} %bitcast.265, ...), custom_call_target="tpu_custom_call" | custom-call | tf_op jit(solution)/shard_map/hidden/pallas_call | solution.py:759
  360.0 46.9 %back.3 = bf16[2048,2048]{1,0:T(8,128)(2,1)} custom-call(bf16[2,2048,1024]{2,1,0:T(8,128)(2,1)} %get-tuple-element.29.refs_0_.own_grads, bf16[2,2048,1024]{2,1,0:T(8,128)(2,1)} %get-tuple-element.28.refs_1_.own_grads, bf16[2,3,2048,1024]{3,2,1,0:T(8,128)(2,1)} %bitcast.267, bf16[2,3,2048,1024]{3,2,1,0:T(8,128)(2,1)} %bitcast.268), custom_call_target="tpu_custom_call" | custom-call | tf_op jit(solution)/shard_map/back/pallas_call | solution.py:816
  426.4 14.3 %collective-permute-done.20 = bf16[1024,128]{1,0:T(8,128)(2,1)} collective-permute-done((bf16[1024,128]{1,0:T(8,128)(2,1)}, bf16[1024,128]{1,0:T(8,128)(2,1)}, u32[]{:S(2)}, u32[]{:S(2)}) %collective-permute-start.20) | collective-permute-done | bytes 262176 | tf_op jit(solution)/shard_map/ppermute | solution.py:51
  455.6 5.7 fusion.46
  464.0 27.7 %hidden.3 = (bf16[2,2048,512]{2,1,0:T(8,128)(2,1)}, bf16[2,2048,512]{2,1,0:T(8,128)(2,1)}, bf16[2,2048,512]{2,1,0:T(8,128)(2,1)}) custom-call(s32[1]{0:T(128)} %bitcast.37.half_ref, bf16[2048,2048]{1,0:T(8,128)(2,1)} %hold.37.rows_ref.near_rows, bf16[2,3,2048,1024]{3,2,1,0:T(8,128)(2,1)} %bitcast.269, bf16[2,3,2048,1024]{3,2,1,0:T(8,128)(2,1)} %bitcast.270, ...), custom_call_target="tpu_custom_call" | custom-call | tf_op jit(solution)/shard_map/hidden/pallas_call | solution.py:759
  491.7 8.0 collective-permute-done.14.refs_2_
  499.7 25.0 %grad.4 = bf16[2048,1024]{1,0:T(8,128)(2,1)} custom-call(s32[1]{0:T(128)} %bitcast.37.half_ref, bf16[2048,2048]{1,0:T(8,128)(2,1)} %bitcast.282, bf16[2,2048,1024]{2,1,0:T(8,128)(2,1)} %get-tuple-element.27.refs_1_.own_grads.refs_0_, bf16[2048,2048]{1,0:T(8,128)(2,1)} %all-gather.24.cloned.1.call-done.rows_ref.near_rows, ...), custom_call_target="tpu_custom_call" | custom-call | tf_op jit(solution)/shard_map/grad/pallas_call | solution.py:853
  534.1 5.7 convolution_convert_fusion.1
  540.9 18.0 %all_to_all.30 = bf16[8,4,128,128]{3,2,1,0:T(8,128)(2,1)S(1)} all-to-all(bf16[8,4,128,128]{3,2,1,0:T(8,128)(2,1)S(1)} %bitcast.305), channel_id=1, replica_groups=mesh['ctx'=4,'exp'=8] {'exp'}, dimensions={0} | all-to-all | bytes 2097152 | tf_op jit(solution)/shard_map/all_to_all | solution.py:957
  559.9 25.3 %grad.3.refs_1_ = bf16[2048,1024]{1,0:T(8,128)(2,1)} custom-call(s32[1]{0:T(128)} %bitcast.37.half_ref, bf16[2048,2048]{1,0:T(8,128)(2,1)} %hold.35.rows_ref.own_rows, bf16[2,2048,1024]{2,1,0:T(8,128)(2,1)} %get-tuple-element.29.refs_0_.own_grads, bf16[2048,2048]{1,0:T(8,128)(2,1)} %hold.37.rows_ref.near_rows, ...), custom_call_target="tpu_custom_call" | custom-call | tf_op jit(solution)/shard_map/grad/pallas_call | solution.py:853
  592.1 8.6 all_to_all.31
  604.6 8.9 collective-permute-done.17.refs_0_
  614.2 9.9 collective-permute-done.16.refs_0_
  628.3 36.0 %attend_back.1 = (bf16[4,3,1024,128]{3,2,1,0:T(8,128)(2,1)}, f32[4,4,512]{2,1,0:T(4,128)S(1)}) custom-call(s32[1]{0:T(128)} %bitcast.1.place_ref, bf16[4,2,1024,128]{3,2,1,0:T(8,128)(2,1)} %hold.33.qk_ref, bf16[4,1024,128]{2,1,0:T(8,128)(2,1)S(1)} %pad_maximum_fusion.3.v_ref, bf16[4,1024,128]{2,1,0:T(8,128)(2,1)S(1)} %pad_maximum_fusion.5.do_ref, ...), custom_call_target="tpu_custom_call" | custom-call | flops 171798691840 | tf_op jit(solution)/shard_map/attend_back/pallas_call | solution.py:285
  664.9 10.7 collective-permute-done.22.refs_1_.refs_0_
  697.6 24.9 %grad.5.refs_2_ = bf16[2048,1024]{1,0:T(8,128)(2,1)} custom-call(s32[1]{0:T(128)} %bitcast.37.half_ref, bf16[2048,2048]{1,0:T(8,128)(2,1)} %hold.35.rows_ref.own_rows, bf16[2,2048,1024]{2,1,0:T(8,128)(2,1)} %get-tuple-element.28.refs_1_.own_grads, bf16[2048,2048]{1,0:T(8,128)(2,1)} %hold.37.rows_ref.near_rows, ...), custom_call_target="tpu_custom_call" | custom-call | tf_op jit(solution)/shard_map/grad/pallas_call | solution.py:853
  722.8 29.8 %back.4.refs_1_.refs_0_ = bf16[2048,2048]{1,0:T(8,128)(2,1)} custom-call(bf16[2,2048,1024]{2,1,0:T(8,128)(2,1)} %get-tuple-element.27.refs_1_.own_grads.refs_0_, bf16[2,3,2048,1024]{3,2,1,0:T(8,128)(2,1)} %bitcast.271, bf16[2048,1024]{1,0:T(8,128)(2,1)} %grad.5.refs_2_), custom_call_target="tpu_custom_call" | custom-call | flops 137438953472 | tf_op jit(solution)/shard_map/back/pallas_call | solution.py:816
  754.1 8.3 collective-permute-done.30.refs_0_
  766.6 7.7 norm_back.1
  775.2 8.5 collective-permute-done.32
  784.8 6.1 collective-permute-done.33
  798.0 6.9 fusion.5
  804.9 14.7 %collective-permute-done.34.refs_1_.refs_0_ = bf16[512,1024]{1,0:T(8,128)(2,1)S(1)} collective-permute-done((bf16[512,1024]{1,0:T(8,128)(2,1)S(1)}, bf16[512,1024]{1,0:T(8,128)(2,1)S(1)}, u32[]{:S(2)}, u32[]{:S(2)}) %collective-permute-start.34) | collective-permute-done | bytes 1048608 | tf_op jit(solution)/shard_map/ppermute | solution.py:51
  819.6 14.3 %reduce-scatter.9.cloned.1.call-done.refs_2_.refs_0_ = bf16[1024,1024]{1,0:T(8,128)(2,1)} async-done(((bf16[2048,1024]{1,0:T(8,128)(2,1)}), bf16[1024,1024]{1,0:T(8,128)(2,1)}) %reduce-scatter.9.cloned.1.call-update) | async-done | bytes 2097168 | tf_op jit(solution)/shard_map/reduce_scatter | solution.py:879
  834.0 10.3 convolution_convert_fusion
  847.4 12.4 %back.5 = bf16[2048,2048]{1,0:T(8,128)(2,1)} custom-call(bf16[1,2048,768]{2,1,0:T(8,128)(2,1)} %bitcast.288, bf16[1,1,2048,768]{3,2,1,0:T(8,128)(2,1)} %bitcast.283, bf16[2048,1024]{1,0:T(8,128)(2,1)} %pad_maximum_fusion.refs_2_.refs_1_), custom_call_target="tpu_custom_call" | custom-call | tf_op jit(solution)/shard_map/back/pallas_call | solution.py:816
  889.0 28.2 %collective-permute-done.39.refs_1_.refs_0_ = bf16[512,1024]{1,0:T(8,128)(2,1)S(1)} collective-permute-done((bf16[512,1024]{1,0:T(8,128)(2,1)}, bf16[512,1024]{1,0:T(8,128)(2,1)S(1)}, u32[]{:S(2)}, u32[]{:S(2)}) %collective-permute-start.39) | collective-permute-done | bytes 1048608 | tf_op jit(solution)/shard_map/ppermute | solution.py:51
  918.2 11.1 %collective-permute-done.40.refs_0_ = bf16[256,2048]{1,0:T(8,128)(2,1)S(1)} collective-permute-done((bf16[256,2048]{1,0:T(8,128)(2,1)}, bf16[256,2048]{1,0:T(8,128)(2,1)S(1)}, u32[]{:S(2)}, u32[]{:S(2)}) %collective-permute-start.40) | collective-permute-done | bytes 1048608 | tf_op jit(solution)/shard_map/ppermute | solution.py:51
  936.4 7.8 all_to_all.32
  944.3 42.1 %collective-permute-start.44 = (f32[256]{0:T(256)S(1)}, f32[256]{0:T(256)S(1)}, u32[]{:S(2)}, u32[]{:S(2)}) collective-permute-start(f32[256]{0:T(256)S(1)} %reduce_sum.159), channel_id=1, source_target_pairs={{0,8},{8,0},{16,24},{24,16},{1,9},{9,1},{17,25},{25,17},{2,10},{10... | collective-permute-start | bytes 3080 | tf_op jit(solution)/shard_map/ppermute | solution.py:51
  1039.6 18.0 %collective-permute-done.43.refs_0_ = bf16[256,2048]{1,0:T(8,128)(2,1)} collective-permute-done((bf16[256,2048]{1,0:T(8,128)(2,1)}, bf16[256,2048]{1,0:T(8,128)(2,1)}, u32[]{:S(2)}, u32[]{:S(2)}) %collective-permute-start.43) | collective-permute-done | bytes 1048608 | tf_op jit(solution)/shard_map/ppermute | solution.py:51
  1057.6 19.0 %collective-permute-done.42.refs_0_ = bf16[256,2048]{1,0:T(8,128)(2,1)} collective-permute-done((bf16[256,2048]{1,0:T(8,128)(2,1)}, bf16[256,2048]{1,0:T(8,128)(2,1)}, u32[]{:S(2)}, u32[]{:S(2)}) %collective-permute-start.42) | collective-permute-done | bytes 1048608 | tf_op jit(solution)/shard_map/ppermute | solution.py:51
  1078.5 6.2 multiply_add_fusion
  (430 shorter events, 268.9 us)
Async XLA Ops:
  7.2 61.8 %all-gather.14.cloned.1.call-start = ((), (), s32[]{:S(2)}) async-start(), calls=%async_computation.9 | async-start | bytes 9437184 | tf_op jit(solution)/shard_map/all_gather | solution.py:920
  11.5 124.3 %all-gather.16.cloned.1.call-start = ((), (), s32[]{:S(2)}) async-start(), calls=%async_computation.10 | async-start | bytes 9437184 | tf_op jit(solution)/shard_map/all_gather | solution.py:920
  12.3 220.8 %all-gather.20.cloned.1.call-start = ((), (), s32[]{:S(2)}) async-start(), calls=%async_computation.16 | async-start | bytes 9437184 | tf_op jit(solution)/shard_map/all_gather | solution.py:920
  13.0 231.6 %all-gather.24.cloned.1.call-start = ((), (), s32[]{:S(2)}) async-start(), calls=%async_computation.18 | async-start | bytes 9437184 | tf_op jit(solution)/shard_map/all_gather | solution.py:920
  13.1 29.7 %collective-permute-start.10 = (bf16[256,2048]{1,0:T(8,128)(2,1)S(1)}, bf16[256,2048]{1,0:T(8,128)(2,1)S(1)}, u32[]{:S(2)}, u32[]{:S(2)}) collective-permute-start(bf16[256,2048]{1,0:T(8,128)(2,1)S(1)} %bitcast.291), channel_id=1, source_target_pairs={{0,24},{8,16},{16,8},{24,0},{1,25},{9,17},{17,9},{25,1},{2,26},{10... | collective-permute-start | bytes 3145736 | tf_op jit(solution)/shard_map/ppermute | solution.py:51
  43.8 256.4 %all-gather.22.cloned.1.call-start = ((), (), s32[]{:S(2)}) async-start(), calls=%async_computation.17 | async-start | bytes 9437184 | tf_op jit(solution)/shard_map/all_gather | solution.py:920
  53.7 9.6 collective-permute-start
  88.3 34.4 %collective-permute-start.9 = (bf16[1024,128]{1,0:T(8,128)(2,1)}, bf16[1024,128]{1,0:T(8,128)(2,1)S(1)}, u32[]{:S(2)}, u32[]{:S(2)}) collective-permute-start(bf16[1024,128]{1,0:T(8,128)(2,1)} %get-tuple-element.172), channel_id=1, source_target_pairs={{0,24},{8,16},{16,8},{24,0},{1,25},{9,17},{17,9},{25,1},{2,26},{10... | collective-permute-start | bytes 786440 | tf_op jit(solution)/shard_map/ppermute | solution.py:51
  102.6 68.3 %collective-permute-start.6 = (bf16[2,1024,128]{2,1,0:T(8,128)(2,1)}, bf16[2,1024,128]{2,1,0:T(8,128)(2,1)S(1)}, u32[]{:S(2)}, u32[]{:S(2)}) collective-permute-start(bf16[2,1024,128]{2,1,0:T(8,128)(2,1)} %get-tuple-element.152), channel_id=1, source_target_pairs={{0,24},{8,16},{16,8},{24,0},{1,25},{9,17},{17,9},{25,1},{2,26},{10... | collective-permute-start | bytes 1572872 | tf_op jit(solution)/shard_map/ppermute | solution.py:51
  105.5 65.4 %collective-permute-start.5 = (bf16[2,1024,128]{2,1,0:T(8,128)(2,1)S(1)}, bf16[2,1024,128]{2,1,0:T(8,128)(2,1)}, u32[]{:S(2)}, u32[]{:S(2)}) collective-permute-start(bf16[2,1024,128]{2,1,0:T(8,128)(2,1)S(1)} %get-tuple-element.153), channel_id=1, source_target_pairs={{0,16},{8,24},{16,0},{24,8},{1,17},{9,25},{17,1},{25,9},{2,18},{10... | collective-permute-start | bytes 1572872 | tf_op jit(solution)/shard_map/ppermute | solution.py:51
  120.4 50.4 %collective-permute-start.4 = (bf16[2,1024,128]{2,1,0:T(8,128)(2,1)S(1)}, bf16[2,1024,128]{2,1,0:T(8,128)(2,1)}, u32[]{:S(2)}, u32[]{:S(2)}) collective-permute-start(bf16[2,1024,128]{2,1,0:T(8,128)(2,1)S(1)} %get-tuple-element.154), channel_id=1, source_target_pairs={{0,8},{8,0},{16,24},{24,16},{1,9},{9,1},{17,25},{25,17},{2,10},{10... | collective-permute-start | bytes 1572872 | tf_op jit(solution)/shard_map/ppermute | solution.py:51
  120.4 48.4 %collective-permute-start.8 = (bf16[1024,128]{1,0:T(8,128)(2,1)S(1)}, bf16[1024,128]{1,0:T(8,128)(2,1)S(1)}, u32[]{:S(2)}, u32[]{:S(2)}) collective-permute-start(bf16[1024,128]{1,0:T(8,128)(2,1)S(1)} %copy-done.51), channel_id=1, source_target_pairs={{0,16},{8,24},{16,0},{24,8},{1,17},{9,25},{17,1},{25,9},{2,18},{10... | collective-permute-start | bytes 786440 | tf_op jit(solution)/shard_map/ppermute | solution.py:51
  122.7 46.1 %collective-permute-start.7 = (bf16[1024,128]{1,0:T(8,128)(2,1)S(1)}, bf16[1024,128]{1,0:T(8,128)(2,1)}, u32[]{:S(2)}, u32[]{:S(2)}) collective-permute-start(bf16[1024,128]{1,0:T(8,128)(2,1)S(1)} %copy-done.50), channel_id=1, source_target_pairs={{0,8},{8,0},{16,24},{24,16},{1,9},{9,1},{17,25},{25,17},{2,10},{10... | collective-permute-start | bytes 786440 | tf_op jit(solution)/shard_map/ppermute | solution.py:51
  241.4 213.6 %all-gather.26.cloned.1.call-start = ((), (), s32[]{:S(2)}) async-start(), calls=%async_computation.19 | async-start | bytes 9437184 | tf_op jit(solution)/shard_map/all_gather | solution.py:920
  241.4 26.7 %collective-permute-start.11 = (bf16[256,2048]{1,0:T(8,128)(2,1)}, bf16[256,2048]{1,0:T(8,128)(2,1)}, u32[]{:S(2)}, u32[]{:S(2)}) collective-permute-start(bf16[256,2048]{1,0:T(8,128)(2,1)} %multiply_convert_fusion), channel_id=1, source_target_pairs={{0,24},{8,16},{16,8},{24,0},{1,25},{9,17},{17,9},{25,1},{2,26},{10... | collective-permute-start | bytes 3145736 | tf_op jit(solution)/shard_map/ppermute | solution.py:51
  411.7 31.5 %collective-permute-start.12 = (bf16[4,256,2048]{2,1,0:T(8,128)(2,1)}, bf16[4,256,2048]{2,1,0:T(8,128)(2,1)}, u32[]{:S(2)}, u32[]{:S(2)}) collective-permute-start(bf16[4,256,2048]{2,1,0:T(8,128)(2,1)} %dynamic-slice_bitcast_fusion.2), channel_id=1, source_target_pairs={{0,1},{1,0},{2,3},{3,2},{4,5},{5,4},{6,7},{7,6},{8,9},{9,8},{10,11... | collective-permute-start | bytes 12582920 | tf_op jit(solution)/shard_map/ppermute | solution.py:51
  414.0 12.3 %collective-permute-start.21 = (bf16[1024,128]{1,0:T(8,128)(2,1)}, bf16[1024,128]{1,0:T(8,128)(2,1)}, u32[]{:S(2)}, u32[]{:S(2)}) collective-permute-start(bf16[1024,128]{1,0:T(8,128)(2,1)} %get-tuple-element.160), channel_id=1, source_target_pairs={{0,24},{8,16},{16,8},{24,0},{1,25},{9,17},{17,9},{25,1},{2,26},{10... | collective-permute-start | bytes 786440 | tf_op jit(solution)/shard_map/ppermute | solution.py:51
  417.4 23.2 %collective-permute-start.20 = (bf16[1024,128]{1,0:T(8,128)(2,1)}, bf16[1024,128]{1,0:T(8,128)(2,1)}, u32[]{:S(2)}, u32[]{:S(2)}) collective-permute-start(bf16[1024,128]{1,0:T(8,128)(2,1)} %get-tuple-element.161), channel_id=1, source_target_pairs={{0,16},{8,24},{16,0},{24,8},{1,17},{9,25},{17,1},{25,9},{2,18},{10... | collective-permute-start | bytes 786440 | tf_op jit(solution)/shard_map/ppermute | solution.py:51
  417.4 23.2 %collective-permute-start.19 = (bf16[1024,128]{1,0:T(8,128)(2,1)}, bf16[1024,128]{1,0:T(8,128)(2,1)}, u32[]{:S(2)}, u32[]{:S(2)}) collective-permute-start(bf16[1024,128]{1,0:T(8,128)(2,1)} %get-tuple-element.162), channel_id=1, source_target_pairs={{0,8},{8,0},{16,24},{24,16},{1,9},{9,1},{17,25},{25,17},{2,10},{10... | collective-permute-start | bytes 786440 | tf_op jit(solution)/shard_map/ppermute | solution.py:51
  422.6 32.4 %all-to-all-start.1 = ((f32[8,2,256]{2,1,0:T(2,128)}), f32[8,2,256]{2,1,0:T(2,128)S(1)}, u32[]{:S(2)}, u32[]{:S(2)}) async-start(f32[8,2,256]{2,1,0:T(2,128)} %bitcast.45), calls=%async_computation.1 | async-start | bytes 32768 | tf_op jit(solution)/shard_map/all_to_all | solution.py:957
  425.9 200.0 %reduce-scatter.5.cloned.1.call-start = ((), (), s32[]{:S(2)}) async-start(), calls=%async_computation.11 | async-start | bytes 6291456 | tf_op jit(solution)/shard_map/reduce_scatter | solution.py:879
  451.5 40.2 %collective-permute-start.15 = (bf16[256,2048]{1,0:T(8,128)(2,1)}, bf16[256,2048]{1,0:T(8,128)(2,1)}, u32[]{:S(2)}, u32[]{:S(2)}) collective-permute-start(bf16[256,2048]{1,0:T(8,128)(2,1)} %get-tuple-element.137), channel_id=1, source_target_pairs={{0,6},{1,7},{2,4},{3,5},{4,2},{5,3},{6,0},{7,1},{8,14},{9,15},{10,... | collective-permute-start | bytes 3145736 | tf_op jit(solution)/shard_map/ppermute | solution.py:51
  453.2 46.5 %collective-permute-start.14 = (bf16[256,2048]{1,0:T(8,128)(2,1)}, bf16[256,2048]{1,0:T(8,128)(2,1)}, u32[]{:S(2)}, u32[]{:S(2)}) collective-permute-start(bf16[256,2048]{1,0:T(8,128)(2,1)} %get-tuple-element.138), channel_id=1, source_target_pairs={{0,4},{1,5},{2,6},{3,7},{4,0},{5,1},{6,2},{7,3},{8,12},{9,13},{10,... | collective-permute-start | bytes 3145736 | tf_op jit(solution)/shard_map/ppermute | solution.py:51
  454.4 45.3 %collective-permute-start.13 = (bf16[256,2048]{1,0:T(8,128)(2,1)}, bf16[256,2048]{1,0:T(8,128)(2,1)}, u32[]{:S(2)}, u32[]{:S(2)}) collective-permute-start(bf16[256,2048]{1,0:T(8,128)(2,1)} %get-tuple-element.136), channel_id=1, source_target_pairs={{0,2},{1,3},{2,0},{3,1},{4,6},{5,7},{6,4},{7,5},{8,10},{9,11},{10,... | collective-permute-start | bytes 3145736 | tf_op jit(solution)/shard_map/ppermute | solution.py:51
  524.7 266.8 %reduce-scatter.7.cloned.1.call-start = ((), (), s32[]{:S(2)}) async-start(), calls=%async_computation.12 | async-start | bytes 6291456 | tf_op jit(solution)/shard_map/reduce_scatter | solution.py:879
  585.2 211.6 %all-gather.28.cloned.1.call-start = ((), (), s32[]{:S(2)}) async-start(), calls=%async_computation.20 | async-start | bytes 9437184 | tf_op jit(solution)/shard_map/all_gather | solution.py:920
  587.4 16.5 %collective-permute-start.18 = (bf16[1024,128]{1,0:T(8,128)(2,1)}, bf16[1024,128]{1,0:T(8,128)(2,1)S(1)}, u32[]{:S(2)}, u32[]{:S(2)}) collective-permute-start(bf16[1024,128]{1,0:T(8,128)(2,1)} %get-tuple-element.164), channel_id=1, source_target_pairs={{0,24},{8,16},{16,8},{24,0},{1,25},{9,17},{17,9},{25,1},{2,26},{10... | collective-permute-start | bytes 786440 | tf_op jit(solution)/shard_map/ppermute | solution.py:51
  589.8 23.7 %collective-permute-start.17 = (bf16[1024,128]{1,0:T(8,128)(2,1)}, bf16[1024,128]{1,0:T(8,128)(2,1)S(1)}, u32[]{:S(2)}, u32[]{:S(2)}) collective-permute-start(bf16[1024,128]{1,0:T(8,128)(2,1)} %get-tuple-element.165), channel_id=1, source_target_pairs={{0,16},{8,24},{16,0},{24,8},{1,17},{9,25},{17,1},{25,9},{2,18},{10... | collective-permute-start | bytes 786440 | tf_op jit(solution)/shard_map/ppermute | solution.py:51
  589.8 34.3 %collective-permute-start.16 = (bf16[1024,128]{1,0:T(8,128)(2,1)}, bf16[1024,128]{1,0:T(8,128)(2,1)S(1)}, u32[]{:S(2)}, u32[]{:S(2)}) collective-permute-start(bf16[1024,128]{1,0:T(8,128)(2,1)} %get-tuple-element.166), channel_id=1, source_target_pairs={{0,8},{8,0},{16,24},{24,16},{1,9},{9,1},{17,25},{25,17},{2,10},{10... | collective-permute-start | bytes 786440 | tf_op jit(solution)/shard_map/ppermute | solution.py:51
  602.2 231.8 %reduce-scatter.9.cloned.1.call-start = ((), (), s32[]{:S(2)}) async-start(), calls=%async_computation.13 | async-start | bytes 6291456 | tf_op jit(solution)/shard_map/reduce_scatter | solution.py:879
  628.3 47.3 %collective-permute-start.22 = (bf16[512,1024]{1,0:T(8,128)(2,1)}, bf16[512,1024]{1,0:T(8,128)(2,1)}, u32[]{:S(2)}, u32[]{:S(2)}) collective-permute-start(bf16[512,1024]{1,0:T(8,128)(2,1)} %slice.158), channel_id=1, source_target_pairs={{0,24},{8,16},{16,8},{24,0},{1,25},{9,17},{17,9},{25,1},{2,26},{10... | collective-permute-start | bytes 3145736 | tf_op jit(solution)/shard_map/ppermute | solution.py:51
  689.0 8.0 collective-permute-start.28
  692.6 61.5 %collective-permute-start.31 = (bf16[3,1024,128]{2,1,0:T(8,128)(2,1)}, bf16[3,1024,128]{2,1,0:T(8,128)(2,1)}, u32[]{:S(2)}, u32[]{:S(2)}) collective-permute-start(bf16[3,1024,128]{2,1,0:T(8,128)(2,1)} %get-tuple-element.146), channel_id=1, source_target_pairs={{0,24},{8,16},{16,8},{24,0},{1,25},{9,17},{17,9},{25,1},{2,26},{10... | collective-permute-start | bytes 2359304 | tf_op jit(solution)/shard_map/ppermute | solution.py:51
  694.1 68.2 %collective-permute-start.30 = (bf16[3,1024,128]{2,1,0:T(8,128)(2,1)}, bf16[3,1024,128]{2,1,0:T(8,128)(2,1)}, u32[]{:S(2)}, u32[]{:S(2)}) collective-permute-start(bf16[3,1024,128]{2,1,0:T(8,128)(2,1)} %get-tuple-element.147), channel_id=1, source_target_pairs={{0,16},{8,24},{16,0},{24,8},{1,17},{9,25},{17,1},{25,9},{2,18},{10... | collective-permute-start | bytes 2359304 | tf_op jit(solution)/shard_map/ppermute | solution.py:51
  695.1 67.3 %collective-permute-start.29 = (bf16[3,1024,128]{2,1,0:T(8,128)(2,1)}, bf16[3,1024,128]{2,1,0:T(8,128)(2,1)}, u32[]{:S(2)}, u32[]{:S(2)}) collective-permute-start(bf16[3,1024,128]{2,1,0:T(8,128)(2,1)} %get-tuple-element.148), channel_id=1, source_target_pairs={{0,8},{8,0},{16,24},{24,16},{1,9},{9,1},{17,25},{25,17},{2,10},{10... | collective-permute-start | bytes 2359304 | tf_op jit(solution)/shard_map/ppermute | solution.py:51
  722.6 271.2 %reduce-scatter.11.cloned.1.call-start = ((), (), s32[]{:S(2)}) async-start(), calls=%async_computation.14 | async-start | bytes 5242880 | tf_op jit(solution)/shard_map/reduce_scatter | solution.py:1083
  775.1 8.5 collective-permute-start.32
  793.0 26.7 %collective-permute-start.34 = (bf16[512,1024]{1,0:T(8,128)(2,1)S(1)}, bf16[512,1024]{1,0:T(8,128)(2,1)S(1)}, u32[]{:S(2)}, u32[]{:S(2)}) collective-permute-start(bf16[512,1024]{1,0:T(8,128)(2,1)S(1)} %slice.165), channel_id=1, source_target_pairs={{0,24},{8,16},{16,8},{24,0},{1,25},{9,17},{17,9},{25,1},{2,26},{10... | collective-permute-start | bytes 3145736 | tf_op jit(solution)/shard_map/ppermute | solution.py:51
  846.9 237.9 %all-gather.18.cloned.1.call-start = ((), (), s32[]{:S(2)}) async-start(), calls=%async_computation.15 | async-start | bytes 5242880 | tf_op jit(solution)/shard_map/all_gather | solution.py:1098
  866.9 50.3 %collective-permute-start.39 = (bf16[512,1024]{1,0:T(8,128)(2,1)}, bf16[512,1024]{1,0:T(8,128)(2,1)S(1)}, u32[]{:S(2)}, u32[]{:S(2)}) collective-permute-start(bf16[512,1024]{1,0:T(8,128)(2,1)} %slice.166), channel_id=1, source_target_pairs={{0,24},{8,16},{16,8},{24,0},{1,25},{9,17},{17,9},{25,1},{2,26},{10... | collective-permute-start | bytes 3145736 | tf_op jit(solution)/shard_map/ppermute | solution.py:51
  880.6 36.6 %collective-permute-start.41 = (bf16[256,2048]{1,0:T(8,128)(2,1)}, bf16[256,2048]{1,0:T(8,128)(2,1)}, u32[]{:S(2)}, u32[]{:S(2)}) collective-permute-start(bf16[256,2048]{1,0:T(8,128)(2,1)} %get-tuple-element.134), channel_id=1, source_target_pairs={{0,6},{1,7},{2,4},{3,5},{4,2},{5,3},{6,0},{7,1},{8,14},{9,15},{10,... | collective-permute-start | bytes 3145736 | tf_op jit(solution)/shard_map/ppermute | solution.py:51
  883.0 46.3 %collective-permute-start.40 = (bf16[256,2048]{1,0:T(8,128)(2,1)}, bf16[256,2048]{1,0:T(8,128)(2,1)S(1)}, u32[]{:S(2)}, u32[]{:S(2)}) collective-permute-start(bf16[256,2048]{1,0:T(8,128)(2,1)} %get-tuple-element.135), channel_id=1, source_target_pairs={{0,4},{1,5},{2,6},{3,7},{4,0},{5,1},{6,2},{7,3},{8,12},{9,13},{10,... | collective-permute-start | bytes 3145736 | tf_op jit(solution)/shard_map/ppermute | solution.py:51
  883.6 46.8 %collective-permute-start.38 = (bf16[256,2048]{1,0:T(8,128)(2,1)}, bf16[256,2048]{1,0:T(8,128)(2,1)S(1)}, u32[]{:S(2)}, u32[]{:S(2)}) collective-permute-start(bf16[256,2048]{1,0:T(8,128)(2,1)} %get-tuple-element.133), channel_id=1, source_target_pairs={{0,2},{1,3},{2,0},{3,1},{4,6},{5,7},{6,4},{7,5},{8,10},{9,11},{10,... | collective-permute-start | bytes 3145736 | tf_op jit(solution)/shard_map/ppermute | solution.py:51
  889.0 134.1 %collective-permute-start.36 = (bf16[4,256,2048]{2,1,0:T(8,128)(2,1)}, bf16[4,256,2048]{2,1,0:T(8,128)(2,1)}, u32[]{:S(2)}, u32[]{:S(2)}) collective-permute-start(bf16[4,256,2048]{2,1,0:T(8,128)(2,1)} %dynamic-slice_bitcast_fusion), channel_id=1, source_target_pairs={{0,1},{1,0},{2,3},{3,2},{4,5},{5,4},{6,7},{7,6},{8,9},{9,8},{10,11... | collective-permute-start | bytes 12582920 | tf_op jit(solution)/shard_map/ppermute | solution.py:51
  944.3 43.7 %collective-permute-start.44 = (f32[256]{0:T(256)S(1)}, f32[256]{0:T(256)S(1)}, u32[]{:S(2)}, u32[]{:S(2)}) collective-permute-start(f32[256]{0:T(256)S(1)} %reduce_sum.159), channel_id=1, source_target_pairs={{0,8},{8,0},{16,24},{24,16},{1,9},{9,1},{17,25},{25,17},{2,10},{10... | collective-permute-start | bytes 3080 | tf_op jit(solution)/shard_map/ppermute | solution.py:51
  1030.3 27.3 %collective-permute-start.43 = (bf16[256,2048]{1,0:T(8,128)(2,1)}, bf16[256,2048]{1,0:T(8,128)(2,1)}, u32[]{:S(2)}, u32[]{:S(2)}) collective-permute-start(bf16[256,2048]{1,0:T(8,128)(2,1)} %get-tuple-element.131), channel_id=1, source_target_pairs={{0,6},{1,7},{2,4},{3,5},{4,2},{5,3},{6,0},{7,1},{8,14},{9,15},{10,... | collective-permute-start | bytes 3145736 | tf_op jit(solution)/shard_map/ppermute | solution.py:51
  1031.0 45.7 %collective-permute-start.42 = (bf16[256,2048]{1,0:T(8,128)(2,1)}, bf16[256,2048]{1,0:T(8,128)(2,1)}, u32[]{:S(2)}, u32[]{:S(2)}) collective-permute-start(bf16[256,2048]{1,0:T(8,128)(2,1)} %get-tuple-element.132), channel_id=1, source_target_pairs={{0,4},{1,5},{2,6},{3,7},{4,0},{5,1},{6,2},{7,3},{8,12},{9,13},{10,... | collective-permute-start | bytes 3145736 | tf_op jit(solution)/shard_map/ppermute | solution.py:51
  1032.5 44.2 %collective-permute-start.37 = (bf16[256,2048]{1,0:T(8,128)(2,1)}, bf16[256,2048]{1,0:T(8,128)(2,1)}, u32[]{:S(2)}, u32[]{:S(2)}) collective-permute-start(bf16[256,2048]{1,0:T(8,128)(2,1)} %get-tuple-element.130), channel_id=1, source_target_pairs={{0,2},{1,3},{2,0},{3,1},{4,6},{5,7},{6,4},{7,5},{8,10},{9,11},{10,... | collective-permute-start | bytes 3145736 | tf_op jit(solution)/shard_map/ppermute | solution.py:51
  (90 other events, 1242.2 us)
Sparse Core Ops, SparseCore 0:
  11.6 57.3 all-gather.13
  70.9 54.7 all-gather.15
  127.6 54.3 all-gather.19
  184.3 60.2 all-gather.23
  246.9 53.2 all-gather.21
  301.9 54.3 all-gather.25
  524.9 53.4 reduce-scatter.4
  585.4 90.5 reduce-scatter.6
  677.9 54.6 all-gather.27
  734.7 99.2 reduce-scatter.8
  847.0 114.5 reduce-scatter.10
  994.0 79.4 all-gather.17

commit v4 on v3

--- a/solution.py
+++ b/solution.py
@@ -1093,9 +1093,11 @@
     grad_normed = reduce_total(normed_parts, normed_own, up_swapped[0])
     attend_part = jnp.sum(grad_normed * local_unit, axis=0)
     attend_sum = jnp.sum(exchange(attend_part.reshape(exp_count, -1)), axis=0)
-    attend_grad = butterfly_sum(attend_sum, "ctx")
-    proj_sum = hold(proj_sum, attend_grad)
-    proj_grad = lax.all_gather(proj_sum, "ctx", axis=0, tiled=True)
+    attend_high = attend_sum.astype(BF16)
+    attend_low = (attend_sum - attend_high.astype(F32)).astype(BF16)
+    ends = jnp.concatenate([attend_high, attend_low])[None]
+    ends = jnp.pad(ends, ((0, 15), (0, proj_sum.shape[1] - ends.shape[1])))
+    proj_all = lax.all_gather(jnp.concatenate([proj_sum, ends]), "ctx", axis=0, tiled=False)
     lunit_grad = grad_normed * attend_gain
     input_grad = grad_hidden + local_factor * (
         lunit_grad - local_unit * jnp.mean(lunit_grad * local_unit, axis=-1, keepdims=True)
@@ -1108,7 +1110,11 @@
     mixture = reduce_finish(*reduce_start(produced), grad_normed)
     block_output = (hidden + mixture).astype(BF16).reshape(block_input.shape)
 
-    proj_grad = hold(proj_grad, input_grad, block_output, expert_grad).astype(F32)
+    proj_all = hold(proj_all, input_grad, block_output, expert_grad)
+    shard_rows = proj_sum.shape[0]
+    proj_grad = proj_all[:, :shard_rows].reshape(model_width, -1).astype(F32)
+    ends = proj_all[:, shard_rows, : 2 * attend_sum.shape[0]].astype(F32)
+    attend_grad = jnp.sum(ends.reshape(ctx_count, 2, -1), axis=(0, 1))
     grads_of = [proj_grad[:, i * local_width : (i + 1) * local_width] for i in range(4)]
     return (
         block_output,

time: 1100 us -> 1110 us (level); the launches traced: 1100 us -> 1090 us
  starting transfers between devices: 135 us -> 87.3 us
  waiting for transfers between devices: 250 us -> 278 us
    ppermute x46 -> x44, starting transfers between devices: 130 us -> 82.4 us  [flip(): lax.ppermute(values, axis, [(i, i ^ mask) for i in range(lax.axis_size(ax...]
    reduce_scatter x1, waiting for transfers between devices: 0.01 us -> 19 us  [body(): lax.psum_scatter(proj_part, 'ctx', scatter_dimension=0, tiled=True)]
    ppermute x46 -> x44, waiting for transfers between devices: 196 us -> 190 us  [flip(): lax.ppermute(values, axis, [(i, i ^ mask) for i in range(lax.axis_size(ax...]
    unnamed x165 -> x157, local copies, waits for them, and re-layouts: 53.8 us -> 52.8 us
  transfers between devices with their start and end apart: 59 -> 57, of which waited for: 27 -> 28; matrix products, arithmetic and copies ran while one was open for 19% -> 20% of each run, Pallas kernels for 31% -> 31%
where the time goes in v4:
time: 1110 us; the launch traced here: 1090 us
  Pallas kernels  363 us (33%)
  waiting for transfers between devices  278 us (25%)
  local copies, waits for them, and re-layouts  129 us (12%)
  other arithmetic  89.3 us (8%)
  starting transfers between devices  87.3 us (8%)
  blocking collectives  72.9 us (7%)
  matrix products  56.9 us (5%)
  between operations  15.5 us (1%)
    ppermute x44, waiting for transfers between devices, flip(): lax.ppermute(values, axis, [(i, i ^ mask) for i in range(lax.axis_size(ax...  190 us
    pallas_call x3, Pallas kernels, back_call(): pl.pallas_call(functools.partial(back_kernel, count=len(parts), chunk=mat...  89.2 us
    ppermute x44, starting transfers between devices, flip(): lax.ppermute(values, axis, [(i, i ^ mask) for i in range(lax.axis_size(ax...  82.4 us
    pallas_call x2, Pallas kernels, hidden_call(): pl.pallas_call(functools.partial(hidden_kernel, chunk=math.gcd(tile, 256)...  79.7 us
    pallas_call x3, Pallas kernels, grad_call(): pl.pallas_call(grad_kernel, grid_spec=pltpu.PrefetchScalarGridSpec(num_sc...  75.1 us
    unnamed x157, local copies, waits for them, and re-layouts  52.8 us
    all_gather x7, waiting for transfers between devices, gather(): return lax.all_gather(values, 'exp', axis=0, tiled=False)  43.1 us
    pallas_call x2, Pallas kernels, down_call(): pl.pallas_call(down_kernel, grid_spec=pltpu.PrefetchScalarGridSpec(num_sc...  40.5 us
  transfers between devices with their start and end apart: 57, of which 28 were waited for; matrix products, arithmetic and copies ran while one was open for 20% of the time, Pallas kernels for 31%

profile of v4, /device:TPU:0, one launch (start us, length us, event | category | flops | bytes accessed | tf_op | source)
XLA Modules:
  0.0 1092.6 jit_solution(14667194776665252727)
XLA Ops:
  18.2 24.6 %copy.212 = bf16[2048,2,3,1024]{3,0,2,1:T(8,128)(2,1)} copy(bf16[2048,2,3,1024]{3,1,2,0:T(2,128)(2,1)} %param.23) | data formatting | bytes 50331648 | tf_op args[10]
  44.5 9.3 all_gather.47
  69.0 10.0 fusion.3.proj_ref
  92.2 6.9 rotate.1
  105.4 15.0 %collective-permute-start.5 = (bf16[2,1024,128]{2,1,0:T(8,128)(2,1)S(1)}, bf16[2,1024,128]{2,1,0:T(8,128)(2,1)}, u32[]{:S(2)}, u32[]{:S(2)}) collective-permute-start(bf16[2,1024,128]{2,1,0:T(8,128)(2,1)S(1)} %get-tuple-element.156), channel_id=1, source_target_pairs={{0,16},{8,24},{16,0},{24,8},{1,17},{9,25},{17,1},{25,9},{2,18},{10... | collective-permute-start | bytes 1572872 | tf_op jit(solution)/shard_map/ppermute | solution.py:51
  122.7 11.3 %collective-permute-start.7 = (bf16[1024,128]{1,0:T(8,128)(2,1)S(1)}, bf16[1024,128]{1,0:T(8,128)(2,1)S(1)}, u32[]{:S(2)}, u32[]{:S(2)}) collective-permute-start(bf16[1024,128]{1,0:T(8,128)(2,1)S(1)} %get-tuple-element.177), channel_id=1, source_target_pairs={{0,8},{8,0},{16,24},{24,16},{1,9},{9,1},{17,25},{25,17},{2,10},{10... | collective-permute-start | bytes 786440 | tf_op jit(solution)/shard_map/ppermute | solution.py:51
  134.0 24.7 %down.2.refs_1_.down_ref = f32[2,2048,1024]{2,1,0:T(8,128)} custom-call(s32[1]{0:T(128)} %constant.259.clone.1.half_ref, bf16[2048,2048]{1,0:T(8,128)(2,1)} %bitcast.284, bf16[2,3,2048,1024]{3,2,1,0:T(8,128)(2,1)} %bitcast.266), custom_call_target="tpu_custom_call" | custom-call | tf_op jit(solution)/shard_map/down/pallas_call | solution.py:692
  158.7 9.2 collective-permute-done.8
  172.7 27.8 %attend.1 = (bf16[4,1024,128]{2,1,0:T(8,128)(2,1)S(1)}, f32[128,4096]{1,0:T(8,128)}, f32[8,1,512]{2,1,0:T(1,128)S(1)}) custom-call(s32[1]{0:T(128)} %bitcast.1.place_ref, bf16[4,2,1024,128]{3,2,1,0:T(8,128)(2,1)} %hold.32.qk_ref, bf16[4,1024,128]{2,1,0:T(8,128)(2,1)S(1)} %pad_maximum_fusion.3.v_ref), custom_call_target="tpu_custom_call" | custom-call | tf_op jit(solution)/shard_map/attend/pallas_call | solution.py:265
  200.7 29.3 %all_to_all.29 = bf16[32,128,128]{2,1,0:T(8,128)(2,1)S(1)} all-to-all(bf16[32,128,128]{2,1,0:T(8,128)(2,1)S(1)} %bitcast.306), channel_id=1, replica_groups=mesh['ctx'=4,'exp'=8] {'ctx','exp'}, dimensions={0} | all-to-all | bytes 2097152 | tf_op jit(solution)/shard_map/all_to_all | solution.py:456
  232.7 6.9 multiply_reduce_fusion.4
  246.7 15.8 %down.3.refs_1_.down_ref = f32[2,2048,512]{2,1,0:T(8,128)} custom-call(s32[1]{0:T(128)} %bitcast.37.half_ref, bf16[2048,2048]{1,0:T(8,128)(2,1)} %all-gather.23.cloned.1.call-done.rows_ref.near_rows, bf16[2,3,2048,1024]{3,2,1,0:T(8,128)(2,1)} %bitcast.267), custom_call_target="tpu_custom_call" | custom-call | tf_op jit(solution)/shard_map/down/pallas_call | solution.py:692
  268.1 34.6 %all-gather.21.cloned.1.call-done.refs_0_ = bf16[2048,2048]{1,0:T(8,128)(2,1)} async-done(((bf16[256,2048]{1,0:T(8,128)(2,1)}), bf16[2048,2048]{1,0:T(8,128)(2,1)}) %all-gather.21.cloned.1.call-update) | async-done | bytes 8388624 | tf_op jit(solution)/shard_map/all_gather | solution.py:920
  302.7 5.7 fusion.47
  310.4 52.1 %hidden.2 = (bf16[2,2048,1024]{2,1,0:T(8,128)(2,1)}, bf16[2,2048,1024]{2,1,0:T(8,128)(2,1)}, bf16[2,2048,1024]{2,1,0:T(8,128)(2,1)}, f32[2,2,2048,128]{3,2,1,0:T(8,128)}) custom-call(s32[1]{0:T(128)} %constant.259.clone.1.half_ref, bf16[2048,2048]{1,0:T(8,128)(2,1)} %hold.34.rows_ref.own_rows, bf16[2,3,2048,1024]{3,2,1,0:T(8,128)(2,1)} %bitcast.268, ...), custom_call_target="tpu_custom_call" | custom-call | tf_op jit(solution)/shard_map/hidden/pallas_call | solution.py:759
  362.5 46.9 %back.3 = bf16[2048,2048]{1,0:T(8,128)(2,1)} custom-call(bf16[2,2048,1024]{2,1,0:T(8,128)(2,1)} %get-tuple-element.29.refs_0_.own_grads, bf16[2,2048,1024]{2,1,0:T(8,128)(2,1)} %get-tuple-element.28.refs_1_.own_grads, bf16[2,3,2048,1024]{3,2,1,0:T(8,128)(2,1)} %bitcast.270, bf16[2,3,2048,1024]{3,2,1,0:T(8,128)(2,1)} %bitcast.271), custom_call_target="tpu_custom_call" | custom-call | tf_op jit(solution)/shard_map/back/pallas_call | solution.py:816
  428.8 14.3 %collective-permute-done.20 = bf16[1024,128]{1,0:T(8,128)(2,1)} collective-permute-done((bf16[1024,128]{1,0:T(8,128)(2,1)}, bf16[1024,128]{1,0:T(8,128)(2,1)}, u32[]{:S(2)}, u32[]{:S(2)}) %collective-permute-start.20) | collective-permute-done | bytes 262176 | tf_op jit(solution)/shard_map/ppermute | solution.py:51
  458.0 5.7 fusion.49
  466.5 27.6 %hidden.3 = (bf16[2,2048,512]{2,1,0:T(8,128)(2,1)}, bf16[2,2048,512]{2,1,0:T(8,128)(2,1)}, bf16[2,2048,512]{2,1,0:T(8,128)(2,1)}) custom-call(s32[1]{0:T(128)} %bitcast.37.half_ref, bf16[2048,2048]{1,0:T(8,128)(2,1)} %hold.36.rows_ref.near_rows, bf16[2,3,2048,1024]{3,2,1,0:T(8,128)(2,1)} %bitcast.272, bf16[2,3,2048,1024]{3,2,1,0:T(8,128)(2,1)} %bitcast.273, ...), custom_call_target="tpu_custom_call" | custom-call | tf_op jit(solution)/shard_map/hidden/pallas_call | solution.py:759
  494.1 8.0 collective-permute-done.14.refs_2_
  502.1 25.0 %grad.4 = bf16[2048,1024]{1,0:T(8,128)(2,1)} custom-call(s32[1]{0:T(128)} %bitcast.37.half_ref, bf16[2048,2048]{1,0:T(8,128)(2,1)} %bitcast.285, bf16[2,2048,1024]{2,1,0:T(8,128)(2,1)} %get-tuple-element.27.refs_1_.own_grads.refs_0_, bf16[2048,2048]{1,0:T(8,128)(2,1)} %all-gather.23.cloned.1.call-done.rows_ref.near_rows, ...), custom_call_target="tpu_custom_call" | custom-call | tf_op jit(solution)/shard_map/grad/pallas_call | solution.py:853
  536.5 5.7 convolution_convert_fusion.1
  543.3 18.0 %all_to_all.30 = bf16[8,4,128,128]{3,2,1,0:T(8,128)(2,1)S(1)} all-to-all(bf16[8,4,128,128]{3,2,1,0:T(8,128)(2,1)S(1)} %bitcast.309), channel_id=1, replica_groups=mesh['ctx'=4,'exp'=8] {'exp'}, dimensions={0} | all-to-all | bytes 2097152 | tf_op jit(solution)/shard_map/all_to_all | solution.py:957
  562.4 25.3 %grad.3.refs_1_ = bf16[2048,1024]{1,0:T(8,128)(2,1)} custom-call(s32[1]{0:T(128)} %bitcast.37.half_ref, bf16[2048,2048]{1,0:T(8,128)(2,1)} %hold.34.rows_ref.own_rows, bf16[2,2048,1024]{2,1,0:T(8,128)(2,1)} %get-tuple-element.29.refs_0_.own_grads, bf16[2048,2048]{1,0:T(8,128)(2,1)} %hold.36.rows_ref.near_rows, ...), custom_call_target="tpu_custom_call" | custom-call | tf_op jit(solution)/shard_map/grad/pallas_call | solution.py:853
  594.6 8.6 all_to_all.31
  607.0 9.0 collective-permute-done.17.refs_0_
  616.6 9.9 collective-permute-done.16.refs_0_
  630.7 36.0 %attend_back.1 = (bf16[4,3,1024,128]{3,2,1,0:T(8,128)(2,1)}, f32[4,4,512]{2,1,0:T(4,128)S(1)}) custom-call(s32[1]{0:T(128)} %bitcast.1.place_ref, bf16[4,2,1024,128]{3,2,1,0:T(8,128)(2,1)} %hold.32.qk_ref, bf16[4,1024,128]{2,1,0:T(8,128)(2,1)S(1)} %pad_maximum_fusion.3.v_ref, bf16[4,1024,128]{2,1,0:T(8,128)(2,1)S(1)} %pad_maximum_fusion.5.do_ref, ...), custom_call_target="tpu_custom_call" | custom-call | flops 171798691840 | tf_op jit(solution)/shard_map/attend_back/pallas_call | solution.py:285
  667.3 10.7 collective-permute-done.22.refs_1_.refs_0_
  700.1 24.9 %grad.5.refs_2_ = bf16[2048,1024]{1,0:T(8,128)(2,1)} custom-call(s32[1]{0:T(128)} %bitcast.37.half_ref, bf16[2048,2048]{1,0:T(8,128)(2,1)} %hold.34.rows_ref.own_rows, bf16[2,2048,1024]{2,1,0:T(8,128)(2,1)} %get-tuple-element.28.refs_1_.own_grads, bf16[2048,2048]{1,0:T(8,128)(2,1)} %hold.36.rows_ref.near_rows, ...), custom_call_target="tpu_custom_call" | custom-call | tf_op jit(solution)/shard_map/grad/pallas_call | solution.py:853
  725.5 29.9 %back.4.refs_1_.refs_0_ = bf16[2048,2048]{1,0:T(8,128)(2,1)} custom-call(bf16[2,2048,1024]{2,1,0:T(8,128)(2,1)} %get-tuple-element.27.refs_1_.own_grads.refs_0_, bf16[2,3,2048,1024]{3,2,1,0:T(8,128)(2,1)} %bitcast.274, bf16[2048,1024]{1,0:T(8,128)(2,1)} %grad.5.refs_2_), custom_call_target="tpu_custom_call" | custom-call | flops 137438953472 | tf_op jit(solution)/shard_map/back/pallas_call | solution.py:816
  756.8 8.0 collective-permute-done.30.refs_0_
  769.0 7.7 norm_back.1
  777.6 8.4 collective-permute-done.32
  787.3 6.1 collective-permute-done.33
  800.5 6.9 fusion.5
  807.4 14.7 %collective-permute-done.34.refs_1_.refs_0_ = bf16[512,1024]{1,0:T(8,128)(2,1)S(1)} collective-permute-done((bf16[512,1024]{1,0:T(8,128)(2,1)S(1)}, bf16[512,1024]{1,0:T(8,128)(2,1)S(1)}, u32[]{:S(2)}, u32[]{:S(2)}) %collective-permute-start.34) | collective-permute-done | bytes 1048608 | tf_op jit(solution)/shard_map/ppermute | solution.py:51
  822.1 14.3 %reduce-scatter.9.cloned.1.call-done.refs_2_.refs_0_ = bf16[1024,1024]{1,0:T(8,128)(2,1)} async-done(((bf16[2048,1024]{1,0:T(8,128)(2,1)}), bf16[1024,1024]{1,0:T(8,128)(2,1)}) %reduce-scatter.9.cloned.1.call-update) | async-done | bytes 2097168 | tf_op jit(solution)/shard_map/reduce_scatter | solution.py:879
  836.4 10.3 convolution_convert_fusion
  849.6 12.4 %back.5 = bf16[2048,2048]{1,0:T(8,128)(2,1)} custom-call(bf16[1,2048,768]{2,1,0:T(8,128)(2,1)} %bitcast.292, bf16[1,1,2048,768]{3,2,1,0:T(8,128)(2,1)} %bitcast.286, bf16[2048,1024]{1,0:T(8,128)(2,1)} %pad_maximum_fusion.refs_2_.refs_1_), custom_call_target="tpu_custom_call" | custom-call | tf_op jit(solution)/shard_map/back/pallas_call | solution.py:816
  891.2 28.2 %collective-permute-done.39.refs_1_.refs_0_ = bf16[512,1024]{1,0:T(8,128)(2,1)S(1)} collective-permute-done((bf16[512,1024]{1,0:T(8,128)(2,1)}, bf16[512,1024]{1,0:T(8,128)(2,1)S(1)}, u32[]{:S(2)}, u32[]{:S(2)}) %collective-permute-start.39) | collective-permute-done | bytes 1048608 | tf_op jit(solution)/shard_map/ppermute | solution.py:51
  921.3 10.3 collective-permute-done.40.refs_0_
  937.1 7.6 all_to_all.32
  944.8 19.0 %reduce-scatter.11.cloned.1.call-done = bf16[512,1024]{1,0:T(8,128)(2,1)} async-done(((bf16[2048,1024]{1,0:T(8,128)(2,1)}), bf16[512,1024]{1,0:T(8,128)(2,1)}) %reduce-scatter.11.cloned.1.call-update) | async-done | bytes 1048592 | tf_op jit(solution)/shard_map/reduce_scatter | solution.py:1083
  1016.6 16.3 %collective-permute-done.43.refs_0_ = bf16[256,2048]{1,0:T(8,128)(2,1)} collective-permute-done((bf16[256,2048]{1,0:T(8,128)(2,1)}, bf16[256,2048]{1,0:T(8,128)(2,1)}, u32[]{:S(2)}, u32[]{:S(2)}) %collective-permute-start.43) | collective-permute-done | bytes 1048608 | tf_op jit(solution)/shard_map/ppermute | solution.py:51
  1032.9 20.1 %collective-permute-done.42.refs_0_ = bf16[256,2048]{1,0:T(8,128)(2,1)} collective-permute-done((bf16[256,2048]{1,0:T(8,128)(2,1)}, bf16[256,2048]{1,0:T(8,128)(2,1)}, u32[]{:S(2)}, u32[]{:S(2)}) %collective-permute-start.42) | collective-permute-done | bytes 1048608 | tf_op jit(solution)/shard_map/ppermute | solution.py:51
  1054.7 6.4 multiply_add_fusion
  1061.1 10.4 all-gather.29.cloned.1.call-done
  (422 shorter events, 281.0 us)
Async XLA Ops:
  7.2 61.8 %all-gather.15.cloned.1.call-start = ((), (), s32[]{:S(2)}) async-start(), calls=%async_computation.9 | async-start | bytes 9437184 | tf_op jit(solution)/shard_map/all_gather | solution.py:920
  11.5 122.5 %all-gather.17.cloned.1.call-start = ((), (), s32[]{:S(2)}) async-start(), calls=%async_computation.10 | async-start | bytes 9437184 | tf_op jit(solution)/shard_map/all_gather | solution.py:920
  12.3 220.4 %all-gather.19.cloned.1.call-start = ((), (), s32[]{:S(2)}) async-start(), calls=%async_computation.15 | async-start | bytes 9437184 | tf_op jit(solution)/shard_map/all_gather | solution.py:920
  13.0 233.6 %all-gather.23.cloned.1.call-start = ((), (), s32[]{:S(2)}) async-start(), calls=%async_computation.17 | async-start | bytes 9437184 | tf_op jit(solution)/shard_map/all_gather | solution.py:920
  13.1 29.7 %collective-permute-start.10 = (bf16[256,2048]{1,0:T(8,128)(2,1)S(1)}, bf16[256,2048]{1,0:T(8,128)(2,1)S(1)}, u32[]{:S(2)}, u32[]{:S(2)}) collective-permute-start(bf16[256,2048]{1,0:T(8,128)(2,1)S(1)} %bitcast.295), channel_id=1, source_target_pairs={{0,24},{8,16},{16,8},{24,0},{1,25},{9,17},{17,9},{25,1},{2,26},{10... | collective-permute-start | bytes 3145736 | tf_op jit(solution)/shard_map/ppermute | solution.py:51
  43.8 258.9 %all-gather.21.cloned.1.call-start = ((), (), s32[]{:S(2)}) async-start(), calls=%async_computation.16 | async-start | bytes 9437184 | tf_op jit(solution)/shard_map/all_gather | solution.py:920
  53.8 9.6 collective-permute-start
  87.4 35.3 %collective-permute-start.9 = (bf16[1024,128]{1,0:T(8,128)(2,1)S(1)}, bf16[1024,128]{1,0:T(8,128)(2,1)S(1)}, u32[]{:S(2)}, u32[]{:S(2)}) collective-permute-start(bf16[1024,128]{1,0:T(8,128)(2,1)S(1)} %get-tuple-element.175), channel_id=1, source_target_pairs={{0,24},{8,16},{16,8},{24,0},{1,25},{9,17},{17,9},{25,1},{2,26},{10... | collective-permute-start | bytes 786440 | tf_op jit(solution)/shard_map/ppermute | solution.py:51
  102.3 67.6 %collective-permute-start.6 = (bf16[2,1024,128]{2,1,0:T(8,128)(2,1)}, bf16[2,1024,128]{2,1,0:T(8,128)(2,1)S(1)}, u32[]{:S(2)}, u32[]{:S(2)}) collective-permute-start(bf16[2,1024,128]{2,1,0:T(8,128)(2,1)} %get-tuple-element.155), channel_id=1, source_target_pairs={{0,24},{8,16},{16,8},{24,0},{1,25},{9,17},{17,9},{25,1},{2,26},{10... | collective-permute-start | bytes 1572872 | tf_op jit(solution)/shard_map/ppermute | solution.py:51
  105.4 64.5 %collective-permute-start.5 = (bf16[2,1024,128]{2,1,0:T(8,128)(2,1)S(1)}, bf16[2,1024,128]{2,1,0:T(8,128)(2,1)}, u32[]{:S(2)}, u32[]{:S(2)}) collective-permute-start(bf16[2,1024,128]{2,1,0:T(8,128)(2,1)S(1)} %get-tuple-element.156), channel_id=1, source_target_pairs={{0,16},{8,24},{16,0},{24,8},{1,17},{9,25},{17,1},{25,9},{2,18},{10... | collective-permute-start | bytes 1572872 | tf_op jit(solution)/shard_map/ppermute | solution.py:51
  120.4 49.5 %collective-permute-start.4 = (bf16[2,1024,128]{2,1,0:T(8,128)(2,1)S(1)}, bf16[2,1024,128]{2,1,0:T(8,128)(2,1)}, u32[]{:S(2)}, u32[]{:S(2)}) collective-permute-start(bf16[2,1024,128]{2,1,0:T(8,128)(2,1)S(1)} %get-tuple-element.157), channel_id=1, source_target_pairs={{0,8},{8,0},{16,24},{24,16},{1,9},{9,1},{17,25},{25,17},{2,10},{10... | collective-permute-start | bytes 1572872 | tf_op jit(solution)/shard_map/ppermute | solution.py:51
  120.4 47.5 %collective-permute-start.8 = (bf16[1024,128]{1,0:T(8,128)(2,1)S(1)}, bf16[1024,128]{1,0:T(8,128)(2,1)}, u32[]{:S(2)}, u32[]{:S(2)}) collective-permute-start(bf16[1024,128]{1,0:T(8,128)(2,1)S(1)} %get-tuple-element.176), channel_id=1, source_target_pairs={{0,16},{8,24},{16,0},{24,8},{1,17},{9,25},{17,1},{25,9},{2,18},{10... | collective-permute-start | bytes 786440 | tf_op jit(solution)/shard_map/ppermute | solution.py:51
  122.7 45.2 %collective-permute-start.7 = (bf16[1024,128]{1,0:T(8,128)(2,1)S(1)}, bf16[1024,128]{1,0:T(8,128)(2,1)S(1)}, u32[]{:S(2)}, u32[]{:S(2)}) collective-permute-start(bf16[1024,128]{1,0:T(8,128)(2,1)S(1)} %get-tuple-element.177), channel_id=1, source_target_pairs={{0,8},{8,0},{16,24},{24,16},{1,9},{9,1},{17,25},{25,17},{2,10},{10... | collective-permute-start | bytes 786440 | tf_op jit(solution)/shard_map/ppermute | solution.py:51
  241.1 216.3 %all-gather.25.cloned.1.call-start = ((), (), s32[]{:S(2)}) async-start(), calls=%async_computation.18 | async-start | bytes 9437184 | tf_op jit(solution)/shard_map/all_gather | solution.py:920
  241.1 26.7 %collective-permute-start.11 = (bf16[256,2048]{1,0:T(8,128)(2,1)}, bf16[256,2048]{1,0:T(8,128)(2,1)}, u32[]{:S(2)}, u32[]{:S(2)}) collective-permute-start(bf16[256,2048]{1,0:T(8,128)(2,1)} %multiply_convert_fusion), channel_id=1, source_target_pairs={{0,24},{8,16},{16,8},{24,0},{1,25},{9,17},{17,9},{25,1},{2,26},{10... | collective-permute-start | bytes 3145736 | tf_op jit(solution)/shard_map/ppermute | solution.py:51
  414.1 31.4 %collective-permute-start.12 = (bf16[4,256,2048]{2,1,0:T(8,128)(2,1)}, bf16[4,256,2048]{2,1,0:T(8,128)(2,1)}, u32[]{:S(2)}, u32[]{:S(2)}) collective-permute-start(bf16[4,256,2048]{2,1,0:T(8,128)(2,1)} %dynamic-slice_bitcast_fusion.2), channel_id=1, source_target_pairs={{0,1},{1,0},{2,3},{3,2},{4,5},{5,4},{6,7},{7,6},{8,9},{9,8},{10,11... | collective-permute-start | bytes 12582920 | tf_op jit(solution)/shard_map/ppermute | solution.py:51
  416.5 12.3 %collective-permute-start.21 = (bf16[1024,128]{1,0:T(8,128)(2,1)}, bf16[1024,128]{1,0:T(8,128)(2,1)}, u32[]{:S(2)}, u32[]{:S(2)}) collective-permute-start(bf16[1024,128]{1,0:T(8,128)(2,1)} %get-tuple-element.163), channel_id=1, source_target_pairs={{0,24},{8,16},{16,8},{24,0},{1,25},{9,17},{17,9},{25,1},{2,26},{10... | collective-permute-start | bytes 786440 | tf_op jit(solution)/shard_map/ppermute | solution.py:51
  419.9 23.2 %collective-permute-start.20 = (bf16[1024,128]{1,0:T(8,128)(2,1)}, bf16[1024,128]{1,0:T(8,128)(2,1)}, u32[]{:S(2)}, u32[]{:S(2)}) collective-permute-start(bf16[1024,128]{1,0:T(8,128)(2,1)} %get-tuple-element.164), channel_id=1, source_target_pairs={{0,16},{8,24},{16,0},{24,8},{1,17},{9,25},{17,1},{25,9},{2,18},{10... | collective-permute-start | bytes 786440 | tf_op jit(solution)/shard_map/ppermute | solution.py:51
  419.9 23.2 %collective-permute-start.19 = (bf16[1024,128]{1,0:T(8,128)(2,1)}, bf16[1024,128]{1,0:T(8,128)(2,1)}, u32[]{:S(2)}, u32[]{:S(2)}) collective-permute-start(bf16[1024,128]{1,0:T(8,128)(2,1)} %get-tuple-element.165), channel_id=1, source_target_pairs={{0,8},{8,0},{16,24},{24,16},{1,9},{9,1},{17,25},{25,17},{2,10},{10... | collective-permute-start | bytes 786440 | tf_op jit(solution)/shard_map/ppermute | solution.py:51
  425.0 32.4 %all-to-all-start.1 = ((f32[8,2,256]{2,1,0:T(2,128)}), f32[8,2,256]{2,1,0:T(2,128)S(1)}, u32[]{:S(2)}, u32[]{:S(2)}) async-start(f32[8,2,256]{2,1,0:T(2,128)} %bitcast.45), calls=%async_computation.1 | async-start | bytes 32768 | tf_op jit(solution)/shard_map/all_to_all | solution.py:957
  428.4 199.9 %reduce-scatter.5.cloned.1.call-start = ((), (), s32[]{:S(2)}) async-start(), calls=%async_computation.11 | async-start | bytes 6291456 | tf_op jit(solution)/shard_map/reduce_scatter | solution.py:879
  453.9 40.2 %collective-permute-start.15 = (bf16[256,2048]{1,0:T(8,128)(2,1)}, bf16[256,2048]{1,0:T(8,128)(2,1)}, u32[]{:S(2)}, u32[]{:S(2)}) collective-permute-start(bf16[256,2048]{1,0:T(8,128)(2,1)} %get-tuple-element.140), channel_id=1, source_target_pairs={{0,6},{1,7},{2,4},{3,5},{4,2},{5,3},{6,0},{7,1},{8,14},{9,15},{10,... | collective-permute-start | bytes 3145736 | tf_op jit(solution)/shard_map/ppermute | solution.py:51
  455.6 46.5 %collective-permute-start.14 = (bf16[256,2048]{1,0:T(8,128)(2,1)}, bf16[256,2048]{1,0:T(8,128)(2,1)}, u32[]{:S(2)}, u32[]{:S(2)}) collective-permute-start(bf16[256,2048]{1,0:T(8,128)(2,1)} %get-tuple-element.141), channel_id=1, source_target_pairs={{0,4},{1,5},{2,6},{3,7},{4,0},{5,1},{6,2},{7,3},{8,12},{9,13},{10,... | collective-permute-start | bytes 3145736 | tf_op jit(solution)/shard_map/ppermute | solution.py:51
  456.9 45.3 %collective-permute-start.13 = (bf16[256,2048]{1,0:T(8,128)(2,1)}, bf16[256,2048]{1,0:T(8,128)(2,1)}, u32[]{:S(2)}, u32[]{:S(2)}) collective-permute-start(bf16[256,2048]{1,0:T(8,128)(2,1)} %get-tuple-element.139), channel_id=1, source_target_pairs={{0,2},{1,3},{2,0},{3,1},{4,6},{5,7},{6,4},{7,5},{8,10},{9,11},{10,... | collective-permute-start | bytes 3145736 | tf_op jit(solution)/shard_map/ppermute | solution.py:51
  527.1 266.9 %reduce-scatter.7.cloned.1.call-start = ((), (), s32[]{:S(2)}) async-start(), calls=%async_computation.12 | async-start | bytes 6291456 | tf_op jit(solution)/shard_map/reduce_scatter | solution.py:879
  587.7 211.6 %all-gather.27.cloned.1.call-start = ((), (), s32[]{:S(2)}) async-start(), calls=%async_computation.19 | async-start | bytes 9437184 | tf_op jit(solution)/shard_map/all_gather | solution.py:920
  589.8 16.5 %collective-permute-start.18 = (bf16[1024,128]{1,0:T(8,128)(2,1)}, bf16[1024,128]{1,0:T(8,128)(2,1)S(1)}, u32[]{:S(2)}, u32[]{:S(2)}) collective-permute-start(bf16[1024,128]{1,0:T(8,128)(2,1)} %get-tuple-element.167), channel_id=1, source_target_pairs={{0,24},{8,16},{16,8},{24,0},{1,25},{9,17},{17,9},{25,1},{2,26},{10... | collective-permute-start | bytes 786440 | tf_op jit(solution)/shard_map/ppermute | solution.py:51
  592.2 23.7 %collective-permute-start.17 = (bf16[1024,128]{1,0:T(8,128)(2,1)}, bf16[1024,128]{1,0:T(8,128)(2,1)S(1)}, u32[]{:S(2)}, u32[]{:S(2)}) collective-permute-start(bf16[1024,128]{1,0:T(8,128)(2,1)} %get-tuple-element.168), channel_id=1, source_target_pairs={{0,16},{8,24},{16,0},{24,8},{1,17},{9,25},{17,1},{25,9},{2,18},{10... | collective-permute-start | bytes 786440 | tf_op jit(solution)/shard_map/ppermute | solution.py:51
  592.2 34.3 %collective-permute-start.16 = (bf16[1024,128]{1,0:T(8,128)(2,1)}, bf16[1024,128]{1,0:T(8,128)(2,1)S(1)}, u32[]{:S(2)}, u32[]{:S(2)}) collective-permute-start(bf16[1024,128]{1,0:T(8,128)(2,1)} %get-tuple-element.169), channel_id=1, source_target_pairs={{0,8},{8,0},{16,24},{24,16},{1,9},{9,1},{17,25},{25,17},{2,10},{10... | collective-permute-start | bytes 786440 | tf_op jit(solution)/shard_map/ppermute | solution.py:51
  604.6 231.8 %reduce-scatter.9.cloned.1.call-start = ((), (), s32[]{:S(2)}) async-start(), calls=%async_computation.13 | async-start | bytes 6291456 | tf_op jit(solution)/shard_map/reduce_scatter | solution.py:879
  630.7 47.3 %collective-permute-start.22 = (bf16[512,1024]{1,0:T(8,128)(2,1)}, bf16[512,1024]{1,0:T(8,128)(2,1)}, u32[]{:S(2)}, u32[]{:S(2)}) collective-permute-start(bf16[512,1024]{1,0:T(8,128)(2,1)} %slice.166), channel_id=1, source_target_pairs={{0,24},{8,16},{16,8},{24,0},{1,25},{9,17},{17,9},{25,1},{2,26},{10... | collective-permute-start | bytes 3145736 | tf_op jit(solution)/shard_map/ppermute | solution.py:51
  691.4 8.0 collective-permute-start.28
  695.1 61.7 %collective-permute-start.31 = (bf16[3,1024,128]{2,1,0:T(8,128)(2,1)}, bf16[3,1024,128]{2,1,0:T(8,128)(2,1)}, u32[]{:S(2)}, u32[]{:S(2)}) collective-permute-start(bf16[3,1024,128]{2,1,0:T(8,128)(2,1)} %get-tuple-element.149), channel_id=1, source_target_pairs={{0,24},{8,16},{16,8},{24,0},{1,25},{9,17},{17,9},{25,1},{2,26},{10... | collective-permute-start | bytes 2359304 | tf_op jit(solution)/shard_map/ppermute | solution.py:51
  696.6 68.2 %collective-permute-start.30 = (bf16[3,1024,128]{2,1,0:T(8,128)(2,1)}, bf16[3,1024,128]{2,1,0:T(8,128)(2,1)}, u32[]{:S(2)}, u32[]{:S(2)}) collective-permute-start(bf16[3,1024,128]{2,1,0:T(8,128)(2,1)} %get-tuple-element.150), channel_id=1, source_target_pairs={{0,16},{8,24},{16,0},{24,8},{1,17},{9,25},{17,1},{25,9},{2,18},{10... | collective-permute-start | bytes 2359304 | tf_op jit(solution)/shard_map/ppermute | solution.py:51
  697.5 67.3 %collective-permute-start.29 = (bf16[3,1024,128]{2,1,0:T(8,128)(2,1)}, bf16[3,1024,128]{2,1,0:T(8,128)(2,1)}, u32[]{:S(2)}, u32[]{:S(2)}) collective-permute-start(bf16[3,1024,128]{2,1,0:T(8,128)(2,1)} %get-tuple-element.151), channel_id=1, source_target_pairs={{0,8},{8,0},{16,24},{24,16},{1,9},{9,1},{17,25},{25,17},{2,10},{10... | collective-permute-start | bytes 2359304 | tf_op jit(solution)/shard_map/ppermute | solution.py:51
  725.0 238.9 %reduce-scatter.11.cloned.1.call-start = ((), (), s32[]{:S(2)}) async-start(), calls=%async_computation.14 | async-start | bytes 5242880 | tf_op jit(solution)/shard_map/reduce_scatter | solution.py:1083
  777.6 8.5 collective-permute-start.32
  795.4 26.7 %collective-permute-start.34 = (bf16[512,1024]{1,0:T(8,128)(2,1)S(1)}, bf16[512,1024]{1,0:T(8,128)(2,1)S(1)}, u32[]{:S(2)}, u32[]{:S(2)}) collective-permute-start(bf16[512,1024]{1,0:T(8,128)(2,1)S(1)} %slice.173), channel_id=1, source_target_pairs={{0,24},{8,16},{16,8},{24,0},{1,25},{9,17},{17,9},{25,1},{2,26},{10... | collective-permute-start | bytes 3145736 | tf_op jit(solution)/shard_map/ppermute | solution.py:51
  849.3 222.2 %all-gather.29.cloned.1.call-start = ((), (), s32[]{:S(2)}) async-start(), calls=%async_computation.20 | async-start | bytes 5406720 | tf_op jit(solution)/shard_map/all_gather | solution.py:1100
  866.8 7.5 collective-permute-start.35
  869.1 50.3 %collective-permute-start.39 = (bf16[512,1024]{1,0:T(8,128)(2,1)}, bf16[512,1024]{1,0:T(8,128)(2,1)S(1)}, u32[]{:S(2)}, u32[]{:S(2)}) collective-permute-start(bf16[512,1024]{1,0:T(8,128)(2,1)} %slice.174), channel_id=1, source_target_pairs={{0,24},{8,16},{16,8},{24,0},{1,25},{9,17},{17,9},{25,1},{2,26},{10... | collective-permute-start | bytes 3145736 | tf_op jit(solution)/shard_map/ppermute | solution.py:51
  882.8 36.6 %collective-permute-start.41 = (bf16[256,2048]{1,0:T(8,128)(2,1)}, bf16[256,2048]{1,0:T(8,128)(2,1)S(1)}, u32[]{:S(2)}, u32[]{:S(2)}) collective-permute-start(bf16[256,2048]{1,0:T(8,128)(2,1)} %get-tuple-element.137), channel_id=1, source_target_pairs={{0,6},{1,7},{2,4},{3,5},{4,2},{5,3},{6,0},{7,1},{8,14},{9,15},{10,... | collective-permute-start | bytes 3145736 | tf_op jit(solution)/shard_map/ppermute | solution.py:51
  885.2 46.5 %collective-permute-start.40 = (bf16[256,2048]{1,0:T(8,128)(2,1)}, bf16[256,2048]{1,0:T(8,128)(2,1)}, u32[]{:S(2)}, u32[]{:S(2)}) collective-permute-start(bf16[256,2048]{1,0:T(8,128)(2,1)} %get-tuple-element.138), channel_id=1, source_target_pairs={{0,4},{1,5},{2,6},{3,7},{4,0},{5,1},{6,2},{7,3},{8,12},{9,13},{10,... | collective-permute-start | bytes 3145736 | tf_op jit(solution)/shard_map/ppermute | solution.py:51
  885.7 45.9 %collective-permute-start.38 = (bf16[256,2048]{1,0:T(8,128)(2,1)}, bf16[256,2048]{1,0:T(8,128)(2,1)S(1)}, u32[]{:S(2)}, u32[]{:S(2)}) collective-permute-start(bf16[256,2048]{1,0:T(8,128)(2,1)} %get-tuple-element.136), channel_id=1, source_target_pairs={{0,2},{1,3},{2,0},{3,1},{4,6},{5,7},{6,4},{7,5},{8,10},{9,11},{10,... | collective-permute-start | bytes 3145736 | tf_op jit(solution)/shard_map/ppermute | solution.py:51
  891.2 107.0 %collective-permute-start.36 = (bf16[4,256,2048]{2,1,0:T(8,128)(2,1)}, bf16[4,256,2048]{2,1,0:T(8,128)(2,1)}, u32[]{:S(2)}, u32[]{:S(2)}) collective-permute-start(bf16[4,256,2048]{2,1,0:T(8,128)(2,1)} %dynamic-slice_bitcast_fusion), channel_id=1, source_target_pairs={{0,1},{1,0},{2,3},{3,2},{4,5},{5,4},{6,7},{7,6},{8,9},{9,8},{10,11... | collective-permute-start | bytes 12582920 | tf_op jit(solution)/shard_map/ppermute | solution.py:51
  1005.6 27.4 %collective-permute-start.43 = (bf16[256,2048]{1,0:T(8,128)(2,1)}, bf16[256,2048]{1,0:T(8,128)(2,1)}, u32[]{:S(2)}, u32[]{:S(2)}) collective-permute-start(bf16[256,2048]{1,0:T(8,128)(2,1)} %get-tuple-element.134), channel_id=1, source_target_pairs={{0,6},{1,7},{2,4},{3,5},{4,2},{5,3},{6,0},{7,1},{8,14},{9,15},{10,... | collective-permute-start | bytes 3145736 | tf_op jit(solution)/shard_map/ppermute | solution.py:51
  1008.0 45.0 %collective-permute-start.42 = (bf16[256,2048]{1,0:T(8,128)(2,1)}, bf16[256,2048]{1,0:T(8,128)(2,1)}, u32[]{:S(2)}, u32[]{:S(2)}) collective-permute-start(bf16[256,2048]{1,0:T(8,128)(2,1)} %get-tuple-element.135), channel_id=1, source_target_pairs={{0,4},{1,5},{2,6},{3,7},{4,0},{5,1},{6,2},{7,3},{8,12},{9,13},{10,... | collective-permute-start | bytes 3145736 | tf_op jit(solution)/shard_map/ppermute | solution.py:51
  1008.6 44.6 %collective-permute-start.37 = (bf16[256,2048]{1,0:T(8,128)(2,1)}, bf16[256,2048]{1,0:T(8,128)(2,1)}, u32[]{:S(2)}, u32[]{:S(2)}) collective-permute-start(bf16[256,2048]{1,0:T(8,128)(2,1)} %get-tuple-element.133), channel_id=1, source_target_pairs={{0,2},{1,3},{2,0},{3,1},{4,6},{5,7},{6,4},{7,5},{8,10},{9,11},{10,... | collective-permute-start | bytes 3145736 | tf_op jit(solution)/shard_map/ppermute | solution.py:51
  (84 other events, 1164.0 us)
Sparse Core Ops, SparseCore 0:
  11.6 57.3 all-gather.14
  70.9 54.7 all-gather.16
  127.6 54.4 all-gather.18
  184.4 62.2 all-gather.22
  249.0 53.6 all-gather.20
  304.4 54.3 all-gather.24
  527.3 53.5 reduce-scatter.4
  587.8 90.4 reduce-scatter.6
  680.2 54.7 all-gather.26
  737.1 99.2 reduce-scatter.8
  849.5 114.3 reduce-scatter.10
  966.3 105.1 all-gather.28
